TPU v7x, 32 devices: a whole 2x2x4 slice. The times are simulated.
32 devices in a mesh: row: 4 (over y, core), col: 8 (over z, x).
Axes of the slice: x: 2, y: 2, z: 4, core: 2. Of those that a mesh axis runs over, the one named last changes fastest.
Arguments:
- positions: float32 [4, 4096, 4096], P(None, 'row', 'col'), may hold values from -2 to 2, as said below
Outputs:
- rotated: float32 [4, 4096, 4096], P(None, 'row', 'col')
Inputs may be any that keep to these rules, and one draw needn't show every extreme that they name: `positions`: each of the 4 matrices is symmetric.
All inputs are finite; a program needn't handle non-finite values.
Results may differ from a plain program's by a relative error of at most 0.00026.
Values sent between devices are 32-bit elements; how exact they have to be, the bound alone decides.
No kernel may reach another device: no remote copies, remote signals or barrier semaphores. Data moves between devices by JAX's collectives and lax.ppermute only.
A program may use at most 256 MiB of HBM per device.

v0:
```python
import jax
import jax.numpy as jnp
from jax import lax
from jax.sharding import PartitionSpec as P

TERMS = 4


STEP_SIZE = 0.4
HIGHEST = lax.Precision.HIGHEST


def partner_2(value, axis, bit):
    mask = 2**bit
    pairs = [(source, source ^ mask) for source in range(lax.axis_size(axis))]
    return lax.ppermute(value, axis, pairs)


def spread(value, axis, source):
    kept = jnp.where(lax.axis_index(axis) == source, value, 0).astype(value.dtype)
    return lax.psum(kept, axis)


def regroup(tile_set):
    half_rows = tile_set.shape[1] // 2
    is_upper = lax.axis_index("row") >= lax.axis_size("row") // 2
    outgoing = jnp.where(is_upper, tile_set[:, :half_rows], tile_set[:, half_rows:])
    arrived = partner_2(outgoing, "row", lax.axis_size("row").bit_length() - 2)
    upper_result = jnp.concatenate((arrived, tile_set[:, half_rows:]), axis=1)
    lower_result = jnp.concatenate((tile_set[:, :half_rows], arrived), axis=1)
    return jnp.where(is_upper, upper_result, lower_result)


def taylor_columns(generator, start_columns):
    current = start_columns
    summed = start_columns
    for power in range(1, TERMS + 1):
        current = (
            jnp.dot(generator, current, precision=HIGHEST, preferred_element_type=jnp.float32)
            / power
        )
        summed = summed + current
    return summed


def times_weights(tile_set, weights):
    return jnp.einsum("kai,ib->kab", tile_set, weights, precision=HIGHEST)


def jacobi_round(tile_set, late):
    block_width = tile_set.shape[2]
    pair_rows = tile_set.shape[1]
    row_count = lax.axis_size("row")
    col_count = lax.axis_size("col")
    row_id = lax.axis_index("row")
    col_id = lax.axis_index("col")
    if late:
        stride = col_count // 2
        column_bit = col_count.bit_length() - 2
        first_block = 2 * row_id - jnp.where(row_id >= row_count // 2, stride - 1, 0)
        column_root = col_id % stride // 2 + col_id % 2 * (row_count // 2)
        col_first = col_id < stride
    else:
        stride = 1
        column_bit = 0
        first_block = 2 * row_id
        column_root = col_id // 2
        col_first = col_id % 2 == 0
    second_block = first_block + stride
    on_diagonal = jnp.logical_or(col_id == first_block, col_id == second_block)
    offset = jnp.where(col_first, 0, block_width)
    other_offset = block_width - offset
    own_rows = lax.dynamic_slice_in_dim(tile_set, offset, block_width, 1)
    own_centres = jnp.diagonal(own_rows, axis1=1, axis2=2)
    other_centres = partner_2(own_centres, "col", column_bit)
    pair_centres = jnp.where(
        col_first,
        jnp.concatenate((own_centres, other_centres), axis=1),
        jnp.concatenate((other_centres, own_centres), axis=1),
    )
    half_generator = jnp.sum(
        tile_set * (own_centres[:, None, :] - pair_centres[:, :, None]), axis=0
    )
    other_generator = partner_2(half_generator, "col", column_bit)
    generator = STEP_SIZE * jnp.where(
        col_first,
        jnp.concatenate((half_generator, other_generator), axis=1),
        jnp.concatenate((other_generator, half_generator), axis=1),
    )
    identity = jnp.eye(pair_rows, dtype=jnp.float32)
    start_columns = lax.dynamic_slice_in_dim(identity, offset, block_width, 1)
    own_rotation = lax.cond(
        on_diagonal,
        lambda: taylor_columns(generator, start_columns),
        lambda: jnp.zeros_like(start_columns),
    )
    left_columns = spread(own_rotation, "col", first_block)
    right_columns = spread(own_rotation, "col", second_block)
    full_rotation = jnp.concatenate((left_columns, right_columns), axis=1)
    column_rotation = spread(own_rotation, "row", column_root)
    own_weights = lax.dynamic_slice_in_dim(column_rotation, offset, block_width, 0)
    other_weights = lax.dynamic_slice_in_dim(column_rotation, other_offset, block_width, 0)
    partner = partner_2(tile_set, "col", column_bit)
    right_side = times_weights(tile_set, own_weights) + times_weights(partner, other_weights)
    return jnp.einsum("ia,kib->kab", full_rotation, right_side, precision=HIGHEST)


def local(positions):
    tile_set = jacobi_round(positions, False)
    tile_set = regroup(tile_set)
    tile_set = jacobi_round(tile_set, True)
    return regroup(tile_set)


def solution(mesh):
    placed = (P(None, "row", "col"),)
    return jax.shard_map(
        local, mesh=mesh, in_specs=placed, out_specs=P(None, "row", "col"), check_vma=False
    )
```

profile of v0, /device:TPU:0, one launch (start us, length us, event | category | flops | bytes accessed | tf_op | source)
XLA Modules:
  0.0 1560.0 jit_solution(16962951519205486000)
XLA Ops:
  6.5 2.9 collective-permute-start.2
  9.5 4.7 constant_dynamic-slice_fusion.1
  14.2 60.3 %copy.59 = f32[4,512,512]{0,2,1:T(8,128)} copy(f32[4,512,512]{2,1,0:T(8,128)} %constant_dynamic-slice_fusion.1) | data formatting | bytes 8388608
  74.4 5.5 gather_fusion
  80.1 0.1 copy.17
  80.2 115.6 %collective-permute-done = f32[4,512]{0,1:T(8,128)S(1)} collective-permute-done((f32[4,512]{0,1:T(8,128)S(1)}, f32[4,512]{0,1:T(8,128)S(1)}, u32[]{:S(2)}, u32[]{:S(2)}) %collective-permute-start) | collective-permute-done | bytes 8224 | tf_op jit(solution)/shard_map/ppermute | solution.py:16
  195.8 0.1 copy.19
  195.9 4.2 multiply_reduce_fusion.1
  200.1 1.8 collective-permute-start.1
  201.9 0.5 fusion.35
  202.4 44.7 %collective-permute-done.1 = f32[1024,512]{1,0:T(8,128)} collective-permute-done((f32[1024,512]{1,0:T(8,128)S(1)}, f32[1024,512]{1,0:T(8,128)}, u32[]{:S(2)}, u32[]{:S(2)}) %collective-permute-start.1) | collective-permute-done | bytes 2097184 | tf_op jit(solution)/shard_map/ppermute | solution.py:16
  247.1 6.7 pad_maximum_fusion.1
  253.8 2.7 broadcast.62
  256.5 1.0 copy-done.2
  257.5 36.5 %conditional.2 = (f32[1024,512]{0,1:T(8,128)S(1)}) conditional(s32[]{:T(128)} %convert_element_type.19, () %tuple.21, (f32[1024,1024]{1,0:T(8,128)S(1)}, s32[]{:T(128)}, pred[]{:T(512)}, f32[1024,1024]{1,0:T(8,128)}, f32[1024,1024]{1,0:T(8,128)S(1)}, /*index=5*/f32[1024,1024]{1,0:T(8,128)}) %tuple.55), branch_computations={%region_1.2_spmd, %region_2.3_spmd} | conditional | flops 25776619520 | bytes 62914576 | solution.py:92
  257.7 5.0 select_multiply_fusion
  262.6 7.0 fusion.4
  269.6 6.9 fusion.62
  276.6 6.7 fusion.2
  283.3 8.5 multiply_add_fusion
  291.7 1.9 copy.56
  294.0 2.9 broadcast_select_fusion.7
  297.0 0.7 all-reduce.13.cloned.1.call-update
  297.8 50.0 %all-reduce.7.cloned.1.call-done = f32[1024,512]{0,1:T(8,128)} async-done(((f32[1024,512]{0,1:T(8,128)}), f32[1024,512]{0,1:T(8,128)}) %all-reduce.7.cloned.1.call-update) | async-done | bytes 2097168 | tf_op jit(solution)/shard_map/psum | solution.py:21
  347.7 17.7 %fusion.48 = f32[512,4,1024]{2,0,1:T(8,128)} fusion(f32[4,1024,512]{2,1,0:T(8,128)} %param.5, f32[1024,512]{0,1:T(8,128)} %all-reduce.7.cloned.1.call-done, s32[]{:T(128)} %select_n.159), kind=kOutput, calls=%fused_computation.59 | convolution fusion | flops 12884901888 | bytes 17826304 | tf_op jit(solution)/shard_map/kai,ib->kab/dot_general | solution.py:47
  365.4 17.4 %fusion.46 = f32[512,4,1024]{2,0,1:T(8,128)} fusion(f32[4,1024,512]{2,1,0:T(8,128)} %collective-permute-done.2, f32[1024,512]{0,1:T(8,128)S(1)} %copy-done.4, s32[]{:T(128)S(6)} %select_n.163), kind=kOutput, calls=%fused_computation.57 | convolution fusion | flops 12884901888 | bytes 17825796 | tf_op jit(solution)/shard_map/kai,ib->kab/dot_general | solution.py:47
  382.8 125.9 %all-reduce.13.cloned.1.call-done = (f32[1024,512]{0,1:T(8,128)}, f32[1024,512]{0,1:T(8,128)}) async-done(((f32[1024,512]{0,1:T(8,128)}, f32[1024,512]{0,1:T(8,128)}), (f32[1024,512]{0,1:T(8,128)}, f32[1024,512]{0,1:T(8,128)})) %all-reduce.13.cloned.1.call-update) | async-done | bytes 4194320 | tf_op jit(solution)/shard_map/psum | solution.py:21
  508.7 33.6 %fusion.39 = f32[4,1024,512]{1,2,0:T(8,128)} fusion(f32[1024,512]{0,1:T(8,128)} %get-tuple-element.91, f32[1024,512]{0,1:T(8,128)} %get-tuple-element.92, f32[512,4,1024]{2,0,1:T(8,128)} %fusion.48, f32[512,4,1024]{2,0,1:T(8,128)} %fusion.46), kind=kOutput, calls=%fused_computation.50 | convolution fusion | flops 25772949504 | bytes 29360128 | tf_op jit(solution)/shard_map/ia,kib->kab/dot_general | solution.py:105
  542.3 7.5 fusion.61
  549.9 1.5 collective-permute-start.3
  551.4 91.0 %collective-permute-done.3 = f32[4,512,512]{1,2,0:T(8,128)S(1)} collective-permute-done((f32[4,512,512]{1,2,0:T(8,128)}, f32[4,512,512]{1,2,0:T(8,128)S(1)}, u32[]{:S(2)}, u32[]{:S(2)}) %collective-permute-start.3) | collective-permute-done | bytes 4194336 | tf_op jit(solution)/shard_map/ppermute | solution.py:16
  642.4 4.3 maximum_select_fusion
  646.7 1.4 collective-permute-start.6
  648.2 4.6 constant_dynamic-slice_fusion
  652.8 60.7 %copy.26 = f32[4,512,512]{0,2,1:T(8,128)} copy(f32[4,512,512]{1,2,0:T(8,128)} %constant_dynamic-slice_fusion) | data formatting | bytes 8388608 | tf_op jit(solution)/shard_map/dynamic_slice | solution.py:73
  713.4 5.5 gather_fusion.1
  719.0 1.5 collective-permute-start.4
  720.5 0.1 copy.27
  720.6 298.3 %collective-permute-done.4 = f32[4,512]{0,1:T(8,128)S(1)} collective-permute-done((f32[4,512]{0,1:T(8,128)S(1)}, f32[4,512]{0,1:T(8,128)S(1)}, u32[]{:S(2)}, u32[]{:S(2)}) %collective-permute-start.4) | collective-permute-done | bytes 8224 | tf_op jit(solution)/shard_map/ppermute | solution.py:16
  1018.9 0.1 copy.29
  1019.0 4.1 multiply_reduce_fusion
  1023.3 92.4 %collective-permute-done.5 = f32[1024,512]{0,1:T(8,128)} collective-permute-done((f32[1024,512]{0,1:T(8,128)S(1)}, f32[1024,512]{0,1:T(8,128)}, u32[]{:S(2)}, u32[]{:S(2)}) %collective-permute-start.5) | collective-permute-done | bytes 2097184 | tf_op jit(solution)/shard_map/ppermute | solution.py:16
  1115.7 6.7 pad_maximum_fusion.3
  1122.3 47.3 %conditional.3 = (f32[1024,512]{0,1:T(8,128)S(1)}) conditional(s32[]{:T(128)} %convert_element_type.21, () %tuple.23, (f32[1024,1024]{1,0:T(8,128)}, s32[]{:T(128)}, pred[]{:T(512)}, f32[1024,1024]{0,1:T(8,128)}, f32[1024,1024]{0,1:T(8,128)}, /*index=5*/f32[1024,1024]{1,0:T(8,128)}) %tuple.54), branch_computations={%region_7.8_spmd, %region_8.9_spmd} | conditional | flops 25776619520 | bytes 96469032 | solution.py:92
  1122.4 5.4 copy.32
  1127.7 5.7 copy.33
  1133.5 5.1 select_multiply_fusion.1
  1138.6 6.7 fusion.17
  1145.3 6.9 fusion.63
  1152.2 6.7 fusion.15
  1158.9 8.6 multiply_add_fusion.1
  1167.5 1.9 copy.58
  1169.6 2.8 broadcast_select_fusion.4
  1172.4 0.5 all-reduce.11.cloned.1.call-update
  1173.0 50.6 %all-reduce.9.cloned.1.call-done = f32[1024,512]{0,1:T(8,128)} async-done(((f32[1024,512]{0,1:T(8,128)}), f32[1024,512]{0,1:T(8,128)}) %all-reduce.9.cloned.1.call-update) | async-done | bytes 2097168 | tf_op jit(solution)/shard_map/psum | solution.py:21
  1223.6 30.1 %fusion.44 = f32[4,1024,512]{2,1,0:T(8,128)} fusion(f32[4,1024,512]{1,2,0:T(8,128)} %maximum_select_fusion, f32[1024,512]{0,1:T(8,128)} %all-reduce.9.cloned.1.call-done, s32[]{:T(128)} %select_n.174), kind=kOutput, calls=%fused_computation.55 | convolution fusion | flops 12884901888 | bytes 17826304 | tf_op jit(solution)/shard_map/kai,ib->kab/dot_general | solution.py:47
  1253.7 30.3 %fusion.42 = f32[4,1024,512]{2,1,0:T(8,128)} fusion(f32[4,1024,512]{1,2,0:T(8,128)} %collective-permute-done.6, f32[1024,512]{0,1:T(8,128)S(1)} %copy-done.3, s32[]{:T(128)S(6)} %select_n.178), kind=kOutput, calls=%fused_computation.53 | convolution fusion | flops 12884901888 | bytes 17825796 | tf_op jit(solution)/shard_map/kai,ib->kab/dot_general | solution.py:47
  1284.0 100.0 %all-reduce.11.cloned.1.call-done = (f32[1024,512]{0,1:T(8,128)}, f32[1024,512]{0,1:T(8,128)}) async-done(((f32[1024,512]{0,1:T(8,128)}, f32[1024,512]{0,1:T(8,128)}), (f32[1024,512]{0,1:T(8,128)}, f32[1024,512]{0,1:T(8,128)})) %all-reduce.11.cloned.1.call-update) | async-done | bytes 4194320 | tf_op jit(solution)/shard_map/psum | solution.py:21
  1383.9 58.1 %fusion.36 = f32[4,1024,512]{1,2,0:T(8,128)} fusion(f32[1024,512]{0,1:T(8,128)} %get-tuple-element.89, f32[1024,512]{0,1:T(8,128)} %get-tuple-element.90, f32[4,1024,512]{2,1,0:T(8,128)} %fusion.44, f32[4,1024,512]{2,1,0:T(8,128)} %fusion.42), kind=kOutput, calls=%fused_computation.49 | convolution fusion | flops 25772949504 | bytes 29360128 | tf_op jit(solution)/shard_map/ia,kib->kab/dot_general | solution.py:105
  1442.0 5.9 fusion.60
  1447.9 1.7 collective-permute-start.7
  1449.6 90.8 %collective-permute-done.7 = f32[4,512,512]{1,2,0:T(8,128)S(1)} collective-permute-done((f32[4,512,512]{1,2,0:T(8,128)S(1)}, f32[4,512,512]{1,2,0:T(8,128)S(1)}, u32[]{:S(2)}, u32[]{:S(2)}) %collective-permute-start.7) | collective-permute-done | bytes 4194336 | tf_op jit(solution)/shard_map/ppermute | solution.py:16
  1540.4 4.2 maximum_select_fusion.1
  1544.6 8.7 copy.43
  (22 shorter events, 0.3 us)
Async XLA Ops:
  6.5 341.2 %all-reduce.7.cloned.1.call-start = ((), (), s32[]{:S(2)}) async-start(), calls=%async_computation | async-start | bytes 4194304 | tf_op jit(solution)/shard_map/psum | solution.py:21
  6.5 358.9 %collective-permute-start.2 = (f32[4,1024,512]{2,1,0:T(8,128)}, f32[4,1024,512]{2,1,0:T(8,128)}, u32[]{:S(2)}, u32[]{:S(2)}) collective-permute-start(f32[4,1024,512]{2,1,0:T(8,128)} %param.5), channel_id=1, source_target_pairs={{0,1},{1,0},{2,3},{3,2},{4,5},{5,4},{6,7},{7,6},{8,9},{9,8},{10,11... | collective-permute-start | bytes 25165832 | tf_op jit(solution)/shard_map/ppermute | solution.py:16
  80.0 115.8 %collective-permute-start = (f32[4,512]{0,1:T(8,128)S(1)}, f32[4,512]{0,1:T(8,128)S(1)}, u32[]{:S(2)}, u32[]{:S(2)}) collective-permute-start(f32[4,512]{0,1:T(8,128)S(1)} %bitcast.52), channel_id=1, source_target_pairs={{0,1},{1,0},{2,3},{3,2},{4,5},{5,4},{6,7},{7,6},{8,9},{9,8},{10,11... | collective-permute-start | bytes 24584 | tf_op jit(solution)/shard_map/ppermute | solution.py:16
  200.1 47.0 %collective-permute-start.1 = (f32[1024,512]{1,0:T(8,128)S(1)}, f32[1024,512]{1,0:T(8,128)}, u32[]{:S(2)}, u32[]{:S(2)}) collective-permute-start(f32[1024,512]{1,0:T(8,128)S(1)} %multiply_reduce_fusion.1), channel_id=1, source_target_pairs={{0,1},{1,0},{2,3},{3,2},{4,5},{5,4},{6,7},{7,6},{8,9},{9,8},{10,11... | collective-permute-start | bytes 6291464 | tf_op jit(solution)/shard_map/ppermute | solution.py:16
  202.4 55.1 %copy-start = (f32[1024,1024]{1,0:T(8,128)}, f32[1024,1024]{1,0:T(8,128)S(1)}, u32[]{:S(2)}) copy-start(f32[1024,1024]{1,0:T(8,128)S(1)} %fusion.35) | copy-start | bytes 12582916
  253.8 3.7 copy-start.2
  297.0 211.7 %all-reduce.13.cloned.1.call-start = ((), (), s32[]{:S(2)}) async-start(), calls=%async_computation.3 | async-start | bytes 8388608 | tf_op jit(solution)/shard_map/psum | solution.py:21
  297.7 925.9 %all-reduce.9.cloned.1.call-start = ((), (), s32[]{:S(2)}) async-start(), calls=%async_computation.1 | async-start | bytes 4194304 | tf_op jit(solution)/shard_map/psum | solution.py:21
  347.7 17.7 %copy-start.4 = (f32[1024,512]{0,1:T(8,128)S(1)}, f32[1024,512]{0,1:T(8,128)}, u32[]{:S(2)}) copy-start(f32[1024,512]{0,1:T(8,128)} %all-reduce.7.cloned.1.call-done) | copy-start | bytes 6291460
  549.9 92.5 %collective-permute-start.3 = (f32[4,512,512]{1,2,0:T(8,128)}, f32[4,512,512]{1,2,0:T(8,128)S(1)}, u32[]{:S(2)}, u32[]{:S(2)}) collective-permute-start(f32[4,512,512]{1,2,0:T(8,128)} %get-tuple-element.97), channel_id=1, source_target_pairs={{0,16},{8,24},{16,0},{24,8},{1,17},{9,25},{17,1},{25,9},{2,18},{10... | collective-permute-start | bytes 12582920 | tf_op jit(solution)/shard_map/ppermute | solution.py:16
  646.7 607.0 %collective-permute-start.6 = (f32[4,1024,512]{1,2,0:T(8,128)}, f32[4,1024,512]{1,2,0:T(8,128)}, u32[]{:S(2)}, u32[]{:S(2)}) collective-permute-start(f32[4,1024,512]{1,2,0:T(8,128)} %maximum_select_fusion), channel_id=1, source_target_pairs={{0,4},{1,5},{2,6},{3,7},{4,0},{5,1},{6,2},{7,3},{8,12},{9,13},{10,... | collective-permute-start | bytes 25165832 | tf_op jit(solution)/shard_map/ppermute | solution.py:16
  719.0 299.9 %collective-permute-start.4 = (f32[4,512]{0,1:T(8,128)S(1)}, f32[4,512]{0,1:T(8,128)S(1)}, u32[]{:S(2)}, u32[]{:S(2)}) collective-permute-start(f32[4,512]{0,1:T(8,128)S(1)} %bitcast.50), channel_id=1, source_target_pairs={{0,4},{1,5},{2,6},{3,7},{4,0},{5,1},{6,2},{7,3},{8,12},{9,13},{10,... | collective-permute-start | bytes 24584 | tf_op jit(solution)/shard_map/ppermute | solution.py:16
  1023.1 92.5 %collective-permute-start.5 = (f32[1024,512]{0,1:T(8,128)S(1)}, f32[1024,512]{0,1:T(8,128)}, u32[]{:S(2)}, u32[]{:S(2)}) collective-permute-start(f32[1024,512]{0,1:T(8,128)S(1)} %multiply_reduce_fusion), channel_id=1, source_target_pairs={{0,4},{1,5},{2,6},{3,7},{4,0},{5,1},{6,2},{7,3},{8,12},{9,13},{10,... | collective-permute-start | bytes 6291464 | tf_op jit(solution)/shard_map/ppermute | solution.py:16
  1133.4 5.1 copy-start.1
  1172.4 211.5 %all-reduce.11.cloned.1.call-start = ((), (), s32[]{:S(2)}) async-start(), calls=%async_computation.2 | async-start | bytes 8388608 | tf_op jit(solution)/shard_map/psum | solution.py:21
  1223.6 30.1 %copy-start.3 = (f32[1024,512]{0,1:T(8,128)S(1)}, f32[1024,512]{0,1:T(8,128)}, u32[]{:S(2)}) copy-start(f32[1024,512]{0,1:T(8,128)} %all-reduce.9.cloned.1.call-done) | copy-start | bytes 6291460
  1447.9 92.5 %collective-permute-start.7 = (f32[4,512,512]{1,2,0:T(8,128)S(1)}, f32[4,512,512]{1,2,0:T(8,128)S(1)}, u32[]{:S(2)}, u32[]{:S(2)}) collective-permute-start(f32[4,512,512]{1,2,0:T(8,128)S(1)} %get-tuple-element.94), channel_id=1, source_target_pairs={{0,16},{8,24},{16,0},{24,8},{1,17},{9,25},{17,1},{25,9},{2,18},{10... | collective-permute-start | bytes 12582920 | tf_op jit(solution)/shard_map/ppermute | solution.py:16
Sparse Core Ops, SparseCore 0:
  297.1 50.6 all-reduce.6
  351.9 156.7 all-reduce.12
  1172.5 51.0 all-reduce.8
  1227.2 156.7 all-reduce.10
where the time goes:
time: 1570 us; the launch traced here: 1560 us
  waiting for transfers between devices  1060 us (68%)
  matrix products  245 us (16%)
  local copies, waits for them, and re-layouts  169 us (11%)
  other arithmetic  60 us (4%)
    ppermute x8, waiting for transfers between devices, partner_2(): return lax.ppermute(value, axis, pairs)  733 us
    psum x4, waiting for transfers between devices, spread(): return lax.psum(kept, axis)  326 us
    dot_general x4, matrix products, times_weights(): return jnp.einsum('kai,ib->kab', tile_set, weights, precision=HIGHEST)  95.4 us
    dot_general x2, matrix products, jacobi_round(): jnp.einsum('ia,kib->kab', full_rotation, right_side, precision=HIGHEST)  91.7 us
    dynamic_slice x3, local copies, waits for them, and re-layouts, jacobi_round(): own_rows = lax.dynamic_slice_in_dim(tile_set, offset, block_width, 1)  69.9 us
    unnamed x9, local copies, waits for them, and re-layouts  61.3 us
    dot_general x8, matrix products, taylor_columns(): jnp.dot(generator, current, precision=HIGHEST, preferred_element_type=jnp...  57.9 us
  transfers between devices with their start and end apart: 12, of which 10 were waited for; matrix products, arithmetic and copies ran while one was open for 22% of the time, Pallas kernels for 0%

commit v1 on v0

v1 whole, which is shorter than its diff:
```python
import functools

import jax
import jax.numpy as jnp
from jax import lax
from jax.experimental import pallas as pl
from jax.experimental.pallas import tpu as pltpu
from jax.sharding import PartitionSpec as P

STEP_SIZE = 0.4
EARLY = 2


def after(value, *earlier):
    return lax.optimization_barrier((value, *earlier))[0]


class Grid:
    def __init__(self, rows, cols):
        self.rows, self.cols = rows, cols
        self.groups = rows // 2
        row_id, col_id = lax.axis_index("row"), lax.axis_index("col")
        self.row_high, self.row_group = row_id // self.groups, row_id % self.groups
        self.col_high = col_id // (cols // 2)
        self.col_group = col_id % (cols // 2) // 2
        self.parity = col_id % 2

    def split(self, row, col):
        half = self.cols // 2
        return row // self.groups, row % self.groups, col // half, col % half // 2, col % 2

    def send(self, value, row_flip, col_flip, chosen=None):
        pairs = []
        for row in range(self.rows):
            for col in range(self.cols):
                if chosen is None or chosen(*self.split(row, col)):
                    target = (row ^ row_flip) * self.cols + (col ^ col_flip)
                    pairs.append((row * self.cols + col, target))
        return lax.ppermute(value, ("row", "col"), pairs)

    def swap_parity(self, value, chosen=None):
        return self.send(value, 0, 1, chosen)

    def swap_col_high(self, value, chosen=None):
        return self.send(value, 0, self.cols // 2, chosen)

    def swap_row_high(self, value, chosen=None):
        return self.send(value, self.rows // 2, 0, chosen)

    def spread_col_group(self, value):
        bit = 1
        while bit < self.groups:
            def holds(rh, rg, ch, cg, e, bit=bit):
                return (rg ^ cg) < bit

            arrived = self.send(value, 0, 2 * bit, holds)
            value = jnp.where((self.row_group ^ self.col_group) & bit != 0, arrived, value)
            bit *= 2
        return value

    def spread_row_group(self, value):
        bit = 1
        while bit < self.groups:
            def holds(rh, rg, ch, cg, e, bit=bit):
                return (rg ^ cg) < bit

            arrived = self.send(value, bit, 0, holds)
            value = jnp.where((self.row_group ^ self.col_group) & bit != 0, arrived, value)
            bit *= 2
        return value


def on_group(rh, rg, ch, cg, e):
    return rg == cg


def off_group(rh, rg, ch, cg, e):
    return rg != cg


def on_pair(rh, rg, ch, cg, e):
    return rg == cg and rh == ch


def triangle_masks(width):
    row = lax.broadcasted_iota(jnp.int32, (width, width), 0)
    col = lax.broadcasted_iota(jnp.int32, (width, width), 1)
    return row, col


def diagonal(blocks):
    row, col = triangle_masks(blocks.shape[-1])
    return jnp.sum(jnp.where((row == col)[None], blocks, 0.0), axis=1)


def halves(value):
    high = value.astype(jnp.bfloat16)
    return high, (value - high.astype(jnp.float32)).astype(jnp.bfloat16)


def three_pass(left_high, left_low, right_high, right_low):
    def dot(a, b):
        return jnp.dot(a, b, preferred_element_type=jnp.float32)

    small = dot(left_high, right_low) + dot(left_low, right_high)
    return dot(left_high, right_high) + small


def rotation_kernel(
    flags_ref, first_ref, second_ref, columns_ref, high_ref, low_ref,
    gen, square_ref, gen_high, gen_low, in_high, in_low,
):
    width = first_ref.shape[0]
    size = 2 * width
    step = min(width, 256)
    first, second = first_ref[...], second_ref[...]
    first_t, second_t = first.T, second.T
    row, col = triangle_masks(width)
    gen[:width, :width] = jnp.where(row < col, first, jnp.where(row > col, -first_t, 0.0))
    gen[width:, width:] = jnp.where(row < col, second, jnp.where(row > col, -second_t, 0.0))
    gen[width:, :width] = jnp.where(row >= col, first, -second_t)
    gen[:width, width:] = jnp.where(row <= col, -first_t, second)
    gen_high[...], gen_low[...] = halves(gen[...])

    def on_eye(index):
        row = lax.broadcasted_iota(jnp.int32, (step, size), 0) + index * step
        return row == lax.broadcasted_iota(jnp.int32, (step, size), 1)

    def square(index, carry):
        rows = pl.ds(pl.multiple_of(index * step, step), step)
        product = three_pass(gen_high[rows, :], gen_low[rows, :], gen_high[...], gen_low[...])
        square_ref[rows, :] = product
        value = gen[rows, :] * (1 / 6) + product * (1 / 24)
        in_high[rows, :], in_low[rows, :] = halves(value + jnp.where(on_eye(index), 0.5, 0.0))
        return carry

    lax.fori_loop(0, size // step, square, 0)
    swap_rows, swap_cols, chosen = flags_ref[0], flags_ref[1], flags_ref[2]

    def outer(index, carry):
        rows = pl.ds(pl.multiple_of(index * step, step), step)
        high, low = halves(square_ref[rows, :])
        product = three_pass(high, low, in_high[...], in_low[...])
        value = product + gen[rows, :] + jnp.where(on_eye(index), 1.0, 0.0)
        columns_ref[rows, :] = jnp.where(chosen == 0, value[:, :width], value[:, width:])
        turned = value.T
        per_half = width // step
        place = (index // per_half + swap_cols) % 2 * per_half + index % per_half
        cols = pl.ds(pl.multiple_of(place * step, step), step)
        for part in range(2):
            start = pl.multiple_of((part + swap_rows) % 2 * width, width)
            high, low = halves(turned[part * width : (part + 1) * width])
            high_ref[pl.ds(start, width), cols] = high
            low_ref[pl.ds(start, width), cols] = low
        return carry

    lax.fori_loop(0, size // step, outer, 0)


NO_COST = pl.CostEstimate(flops=0, bytes_accessed=0, transcendentals=0)


def rotation_of(first, second, swap_rows, swap_cols, chosen):
    width = first.shape[0]
    size = 2 * width
    whole = pl.BlockSpec(memory_space=pltpu.VMEM)
    flags = jnp.stack([jnp.asarray(flag, jnp.int32) for flag in (swap_rows, swap_cols, chosen)])
    return pl.pallas_call(
        rotation_kernel,
        out_shape=(
            jax.ShapeDtypeStruct((size, width), jnp.float32),
            jax.ShapeDtypeStruct((size, size), jnp.bfloat16),
            jax.ShapeDtypeStruct((size, size), jnp.bfloat16),
        ),
        in_specs=[pl.BlockSpec(memory_space=pltpu.SMEM), whole, whole],
        out_specs=(whole, whole, whole),
        scratch_shapes=[pltpu.VMEM((size, size), jnp.float32)] * 2
        + [pltpu.VMEM((size, size), jnp.bfloat16)] * 4,
        compiler_params=pltpu.CompilerParams(vmem_limit_bytes=48 * 2**20),
        cost_estimate=NO_COST,
    )(flags, first, second)


def rotate_kernel(spans, per_half, *refs):
    step = pl.program_id(0)
    at = sum(count for side in spans for _, _, count in side)
    weights, turn_high, turn_low = refs[at : at + 2], refs[at + 2], refs[at + 3]
    outs = refs[at + 4 : -6]
    weight_high, weight_low = refs[-6:-4], refs[-4:-2]
    mid_high, mid_low = refs[-2:]
    block = turn_high.shape[0]
    first_part = 2 * per_half

    @pl.when(step == 0)
    def _():
        for side in range(2):
            weight_high[side][...], weight_low[side][...] = halves(weights[side][...])

    for now in range(first_part):

        @pl.when(step == now)
        def _(now=now):
            total, at = None, 0
            for side in range(2):
                for first, steps, count in spans[side]:
                    if first <= now < first + steps:
                        value = refs[at][...]
                        for ref in refs[at + 1 : at + count]:
                            value = value + ref[...]
                        high, low = halves(value)
                        part = three_pass(high, low, weight_high[side][...], weight_low[side][...])
                        total = part if total is None else total + part
                    at += count
            rows = pl.ds(now * block, block)
            mid_high[rows, :], mid_low[rows, :] = halves(total)

    @pl.when(step >= first_part)
    def _():
        product = three_pass(turn_high[...], turn_low[...], mid_high[...], mid_low[...])
        for half, out in enumerate(outs):

            @pl.when((step - first_part) // per_half == half)
            def _(out=out):
                out[...] = product


def block_rows(width):
    return min(width, 256)


def rotate(near, far, near_weights, far_weights, turn):
    width = near_weights.shape[0]
    size = 2 * width
    block = block_rows(width)
    per_half = width // block
    first_part = 2 * per_half
    turn_high, turn_low = turn
    out_halves = turn_high.shape[0] // width
    arrays, specs, spans = [], [], []
    for side in (near, far):
        span, first = [], 0
        for piece in side:
            steps = piece[0].shape[0] // block
            span.append((first, steps, len(piece)))

            def place(step, first=first, steps=steps):
                return jnp.clip(step - first, 0, steps - 1), 0

            for array in piece:
                arrays.append(array)
                specs.append(pl.BlockSpec((block, width), place))
            first += steps
        spans.append(tuple(span))
    fixed = pl.BlockSpec((width, width), lambda step: (0, 0))
    turning = pl.BlockSpec(
        (block, size),
        lambda step: (jnp.clip(step - first_part, 0, out_halves * per_half - 1), 0),
    )
    outs = [
        pl.BlockSpec(
            (block, width),
            lambda step, half=half: (
                jnp.clip(step - first_part - half * per_half, 0, per_half - 1),
                0,
            ),
        )
        for half in range(out_halves)
    ]
    return pl.pallas_call(
        functools.partial(rotate_kernel, tuple(spans), per_half),
        grid=(first_part + out_halves * per_half,),
        out_shape=[jax.ShapeDtypeStruct((width, width), jnp.float32)] * out_halves,
        in_specs=[*specs, fixed, fixed, turning, turning],
        out_specs=outs,
        scratch_shapes=[pltpu.VMEM((width, width), jnp.bfloat16)] * 4
        + [pltpu.VMEM((size, width), jnp.bfloat16)] * 2,
        compiler_params=pltpu.CompilerParams(vmem_limit_bytes=40 * 2**20),
        cost_estimate=NO_COST,
    )(*arrays, near_weights, far_weights, turn_high, turn_low)


def rows_of(value, which, width):
    return lax.dynamic_slice_in_dim(value, which * width, width, value.ndim - 2)


def first_generator(grid, tiles, own_centres, other_centres):
    width = tiles.shape[2]
    is_first = grid.parity == 0
    centres = jnp.where(
        is_first,
        jnp.concatenate((own_centres, other_centres), axis=1),
        jnp.concatenate((other_centres, own_centres), axis=1),
    )
    generator = STEP_SIZE * jnp.sum(
        tiles * (own_centres[:, None, :] - centres[:, :, None]), axis=0
    )
    row, col = triangle_masks(width)
    top, bottom = generator[:width], generator[width:]
    return jnp.where(
        is_first, jnp.where(row < col, top, bottom), jnp.where(row < col, bottom, top)
    )


def second_generator(grid, blocks, own_centres, row_centres, col_centres):
    same = grid.row_high == grid.col_high
    row_centres = jnp.where(same, own_centres, row_centres)
    col_centres = jnp.where(same, own_centres, col_centres)
    return STEP_SIZE * jnp.sum(
        blocks * (col_centres[:, None, :] - row_centres[:, :, None]), axis=0
    )


def cut(array, block):
    return [array[row : row + block] for row in range(0, array.shape[0], block)]


def take(queue, count):
    taken = queue[:count]
    del queue[:count]
    return taken


def local(positions):
    grid = Grid(lax.axis_size("row"), lax.axis_size("col"))
    count, height, width = positions.shape
    block = block_rows(width)
    pieces_of = height // block
    early, late = list(range(EARLY)), list(range(EARLY, count))
    is_first = grid.parity == 0
    is_low = grid.row_high == 0
    is_left = grid.col_high == 0
    same = grid.row_high == grid.col_high
    groups = grid.groups > 1
    gate = lax.optimization_barrier

    raw_queue = [(k, piece) for k in early for piece in range(pieces_of)]
    far = {k: [] for k in early}

    def send_raw(tiles, number):
        for k, piece in take(raw_queue, number):
            rows = tiles[k, piece * block : (piece + 1) * block]
            far[k].append(grid.swap_col_high(rows))

    def weights_of(columns, which):
        return rows_of(columns, which, width), rows_of(columns, 1 - which, width)

    tiles = positions
    own_centres = diagonal(rows_of(tiles, grid.parity, width))
    other_centres = grid.swap_parity(own_centres, on_pair)
    send_raw(tiles, 1)
    packed = first_generator(grid, tiles, own_centres, other_centres)
    tiles, packed, far = gate((tiles, packed, far))

    urgent = [grid.swap_parity(tiles[0], on_group)]
    packed = jnp.where(same, packed, grid.swap_col_high(packed, on_pair))
    tiles, packed, urgent = gate((tiles, packed, urgent))

    packed = grid.spread_col_group(packed)
    urgent.append(grid.swap_parity(tiles[1], on_group))
    send_raw(tiles, 1)
    tiles, packed, urgent, far = gate((tiles, packed, urgent, far))

    other = grid.swap_parity(packed)
    send_raw(tiles, 1)
    tiles, packed, other, far = gate((tiles, packed, other, far))

    urgent.append(grid.swap_parity(tiles[2], on_group))
    send_raw(tiles, 1)
    columns, *turn = rotation_of(
        jnp.where(is_first, packed, other),
        jnp.where(is_first, other, packed),
        grid.row_high,
        0,
        grid.parity,
    )
    tiles, columns, turn, urgent, far = gate((tiles, columns, turn, urgent, far))

    arrived = grid.swap_row_high(columns, on_group)
    urgent += [grid.swap_parity(tiles[k], on_group) for k in range(3, count)]
    send_raw(tiles, 1)
    columns = jnp.stack((jnp.where(same, columns, arrived), jnp.where(same, arrived, columns)))
    tiles, columns, turn, urgent, far = gate((tiles, columns, turn, urgent, far))

    columns = grid.spread_row_group(columns)
    near_weights = weights_of(columns[0], grid.parity)
    far_weights = weights_of(columns[1], grid.parity)
    partner = [[urgent[k]] for k in range(count)]
    if groups:
        for k in late:
            partner[k].append(grid.swap_parity(tiles[k], off_group))
    send_raw(tiles, 2)
    block_turn = [rows_of(part, grid.parity ^ grid.row_high, width) for part in turn]
    blocks = jnp.stack(
        [
            rotate([[tiles[k]]], [[urgent[k]]], *near_weights, block_turn)[0]
            for k in range(count)
        ]
    )
    state = (tiles, near_weights, far_weights, partner, far, blocks, turn)
    tiles, near_weights, far_weights, partner, far, blocks, turn = gate(state)

    near, sent = {}, {}

    def first_round(k):
        near[k], sent[k] = rotate([[tiles[k]]], [partner[k]], *near_weights, turn)

    own_centres = diagonal(blocks)
    row_centres = grid.swap_col_high(own_centres, on_pair)
    col_centres = grid.swap_row_high(own_centres, on_pair)
    if groups:
        partner[early[0]].append(grid.swap_parity(tiles[early[0]], off_group))
    send_raw(tiles, len(raw_queue))
    first_round(late[0])
    own = second_generator(grid, blocks, own_centres, row_centres, col_centres)
    tiles, partner, far, own, near, sent = gate((tiles, partner, far, own, near, sent))

    late_near = cut(near[late[0]], block)
    late_far = {k: [] for k in late}
    other = grid.swap_row_high(own, on_group)
    if groups:
        for k in early[1:]:
            partner[k].append(grid.swap_parity(tiles[k], off_group))
    late_far[late[0]].append(grid.swap_col_high(late_near[0]))
    first_round(late[1])
    top, bottom = jnp.where(is_low, own, other), jnp.where(is_low, other, own)
    row, col = triangle_masks(width)
    packed = jnp.where(
        is_left, jnp.where(row < col, top, bottom), jnp.where(row < col, bottom, top)
    )
    state = (tiles, partner, near, sent, packed, late_far, late_near)
    tiles, partner, near, sent, packed, late_far, late_near = gate(state)

    arrived = grid.swap_parity(packed, lambda rh, rg, ch, cg, e: rg == cg and e == rh)
    late_far[late[0]] += [grid.swap_col_high(part) for part in late_near[1:]]
    moved = {late[0]: grid.swap_row_high(sent[late[0]])}
    first_round(early[0])
    packed = jnp.where(grid.parity == grid.row_high, packed, arrived)
    state = (tiles, partner, near, sent, packed, late_far, moved, far)
    tiles, partner, near, sent, packed, late_far, moved, far = gate(state)

    raw_pieces = [(k, piece) for k in early for piece in range(pieces_of)]
    far_partner = {k: [] for k in early}

    def send_far(number):
        for k, piece in take(raw_pieces, number):
            far_partner[k].append(grid.swap_parity(far[k][piece]))

    other = grid.swap_col_high(packed, on_group)
    moved[late[1]] = grid.swap_row_high(sent[late[1]])
    first_round(early[1])
    send_far(2)
    both = jnp.stack((jnp.where(is_left, packed, other), jnp.where(is_left, other, packed)))
    state = (near, sent, both, late_far, moved, far, far_partner)
    near, sent, both, late_far, moved, far, far_partner = gate(state)

    both = grid.spread_col_group(both)
    moved[early[0]] = grid.swap_row_high(sent[early[0]])
    late_near = cut(moved[late[0]], block)
    late_far[late[0]].append(grid.swap_col_high(late_near[0]))
    send_far(2)
    state = (sent, both, late_far, late_near, moved, far, far_partner)
    sent, both, late_far, late_near, moved, far, far_partner = gate(state)

    moved[early[1]] = grid.swap_row_high(sent[early[1]])
    late_far[late[0]] += [grid.swap_col_high(part) for part in late_near[1:]]
    send_far(2)
    columns, *second_turn = rotation_of(
        both[0], both[1], grid.row_high, grid.row_high, grid.col_high
    )
    state = (near, columns, second_turn, late_far, moved, far, far_partner)
    near, columns, second_turn, late_far, moved, far, far_partner = gate(state)

    def far_round(k):
        pieces = [[part] for part in far[k]]
        others = [[part] for part in far_partner[k]]
        return rotate(pieces, others, *far_weights, turn)

    arrived = grid.swap_row_high(columns, lambda rh, rg, ch, cg, e: rg == cg and rh == e)
    late_near = cut(near[late[1]], block)
    late_far[late[1]].append(grid.swap_col_high(late_near[0]))
    send_far(len(raw_pieces))
    far_near, far_sent = {}, {}
    far_near[early[0]], far_sent[early[0]] = far_round(early[0])
    columns = jnp.where(grid.row_high == grid.parity, columns, arrived)
    state = (columns, late_far, late_near, moved, far_near, far_sent, far_partner)
    columns, late_far, late_near, moved, far_near, far_sent, far_partner = gate(state)

    columns = grid.spread_row_group(columns)
    late_far[late[1]] += [grid.swap_col_high(part) for part in late_near[1:]]
    far_moved = {early[0]: grid.swap_row_high(far_sent[early[0]])}
    far_near[early[1]], far_sent[early[1]] = far_round(early[1])
    weights = weights_of(columns, grid.col_high)
    state = (weights, late_far, moved, far_near, far_sent, far_moved)
    weights, late_far, moved, far_near, far_sent, far_moved = gate(state)

    late_far[late[1]] += [grid.swap_col_high(part) for part in cut(moved[late[1]], block)]
    far_moved[early[1]] = grid.swap_row_high(far_sent[early[1]])
    outputs = [None] * count
    for k in [late[0], *early, late[1]]:
        mine = [[near[k]], [moved[k]]]
        if k in early:
            theirs = [[far_near[k]], [far_moved[k]]]
        else:
            theirs = [[part] for part in late_far[k]]
        kept, leaving = rotate(mine, theirs, *weights, second_turn)
        arrived = grid.swap_row_high(leaving)
        outputs[k] = [jnp.where(is_low, kept, arrived), jnp.where(is_low, arrived, kept)]
    return jnp.stack([part for pair in outputs for part in pair]).reshape(positions.shape)


def solution(mesh):
    spec = P(None, "row", "col")
    return jax.shard_map(local, mesh=mesh, in_specs=(spec,), out_specs=spec, check_vma=False)
```

time: 1570 us -> 656 us (0.42)
  the two profiles are of different devices: /device:TPU:0 before, /device:TPU:9 now
where the time goes in v1:
time: 656 us; the launch traced here: 645 us
  waiting for transfers between devices  266 us (41%)
  Pallas kernels  164 us (25%)
  starting transfers between devices  102 us (16%)
  local copies, waits for them, and re-layouts  75 us (11%)
  other arithmetic  35.3 us (5%)
    ppermute x56, waiting for transfers between devices, send(): return lax.ppermute(value, ('row', 'col'), pairs)  266 us
    pallas_call x14, Pallas kernels, rotate(): pl.pallas_call(functools.partial(rotate_kernel, tuple(spans), per_half),...  126 us
    ppermute x56, starting transfers between devices, send(): return lax.ppermute(value, ('row', 'col'), pairs)  102 us
    pallas_call x2, Pallas kernels, rotation_of(): pl.pallas_call(rotation_kernel, out_shape=(jax.ShapeDtypeStruct((size, wi...  38.6 us
    unnamed x164, local copies, waits for them, and re-layouts  34.1 us
  transfers between devices with their start and end apart: 56, of which 24 were waited for; matrix products, arithmetic and copies ran while one was open for 8% of the time, Pallas kernels for 26%

profile of v1, /device:TPU:9, one launch (start us, length us, event | category | flops | bytes accessed | tf_op | source)
XLA Modules:
  0.0 644.9 jit_solution(14123441119847830092)
XLA Ops:
  2.9 3.1 collective-permute-start
  7.3 4.1 multiply_reduce_fusion
  12.9 16.9 %collective-permute-done.1.refs_0_ = f32[256,512]{1,0:T(8,128)S(1)} collective-permute-done((f32[256,512]{1,0:T(8,128)S(1)}, f32[256,512]{1,0:T(8,128)S(1)}, u32[]{:S(2)}, u32[]{:S(2)}) %collective-permute-start.1) | collective-permute-done | bytes 524320 | tf_op jit(solution)/shard_map/ppermute | solution.py:39
  30.6 3.1 slice_bitcast_fusion.13
  33.6 3.1 collective-permute-start.3
  36.7 6.0 collective-permute-start.2
  42.7 31.8 %collective-permute-done.2 = f32[512,512]{1,0:T(8,128)} collective-permute-done((f32[512,512]{1,0:T(8,128)}, f32[512,512]{1,0:T(8,128)}, u32[]{:S(2)}, u32[]{:S(2)}) %collective-permute-start.2) | collective-permute-done | bytes 1048608 | tf_op jit(solution)/shard_map/ppermute | solution.py:39
  76.0 3.8 slice_bitcast_fusion.12
  84.4 2.9 collective-permute-start.6
  87.3 7.6 %collective-permute-done.4 = f32[512,512]{1,0:T(8,128)S(1)} collective-permute-done((f32[512,512]{1,0:T(8,128)S(1)}, f32[512,512]{1,0:T(8,128)S(1)}, u32[]{:S(2)}, u32[]{:S(2)}) %collective-permute-start.4) | collective-permute-done | bytes 1048608 | tf_op jit(solution)/shard_map/ppermute | solution.py:39
  95.2 14.4 %collective-permute-done.6.refs_1_ = f32[256,512]{1,0:T(8,128)S(1)} collective-permute-done((f32[256,512]{1,0:T(8,128)S(1)}, f32[256,512]{1,0:T(8,128)S(1)}, u32[]{:S(2)}, u32[]{:S(2)}) %collective-permute-start.6) | collective-permute-done | bytes 524320 | tf_op jit(solution)/shard_map/ppermute | solution.py:39
  109.6 8.5 %collective-permute-done.5.refs_1_ = f32[1024,512]{1,0:T(8,128)} collective-permute-done((f32[1024,512]{1,0:T(8,128)}, f32[1024,512]{1,0:T(8,128)}, u32[]{:S(2)}, u32[]{:S(2)}) %collective-permute-start.5) | collective-permute-done | bytes 2097184 | tf_op jit(solution)/shard_map/ppermute | solution.py:39
  119.4 2.9 collective-permute-start.8
  122.3 21.8 %collective-permute-done.8.refs_2_ = f32[256,512]{1,0:T(8,128)} collective-permute-done((f32[256,512]{1,0:T(8,128)S(1)}, f32[256,512]{1,0:T(8,128)}, u32[]{:S(2)}, u32[]{:S(2)}) %collective-permute-start.8) | collective-permute-done | bytes 524320 | tf_op jit(solution)/shard_map/ppermute | solution.py:39
  144.1 3.2 slice_bitcast_fusion.11
  150.5 3.0 collective-permute-start.10
  153.8 19.0 %shard_map.17 = (f32[1024,512]{1,0:T(8,128)S(1)}, bf16[1024,1024]{1,0:T(8,128)(2,1)}, bf16[1024,1024]{1,0:T(8,128)(2,1)}) custom-call(s32[3]{0:T(128)S(1)} %pad_add_fusion.flags_ref, f32[512,512]{1,0:T(8,128)S(1)} %get-tuple-element.514.first_ref, f32[512,512]{1,0:T(8,128)S(1)} %get-tuple-element.513.second_ref), custom_call_target="tpu_custom_call" | custom-call | tf_op jit(solution)/shard_map/pallas_call | solution.py:168
  180.3 3.0 collective-permute-start.13
  183.2 18.3 %collective-permute-done.11 = f32[1024,512]{1,0:T(8,128)S(1)} collective-permute-done((f32[1024,512]{1,0:T(8,128)S(1)}, f32[1024,512]{1,0:T(8,128)S(1)}, u32[]{:S(2)}, u32[]{:S(2)}) %collective-permute-start.11) | collective-permute-done | bytes 2097184 | tf_op jit(solution)/shard_map/ppermute | solution.py:39
  204.6 6.7 %collective-permute-done.13.refs_0_ = f32[256,512]{1,0:T(8,128)S(1)} collective-permute-done((f32[256,512]{1,0:T(8,128)S(1)}, f32[256,512]{1,0:T(8,128)S(1)}, u32[]{:S(2)}, u32[]{:S(2)}) %collective-permute-start.13) | collective-permute-done | bytes 524320 | tf_op jit(solution)/shard_map/ppermute | solution.py:39
  211.3 16.4 %collective-permute-done.12.refs_1_ = f32[1024,512]{1,0:T(8,128)S(1)} collective-permute-done((f32[1024,512]{1,0:T(8,128)S(1)}, f32[1024,512]{1,0:T(8,128)S(1)}, u32[]{:S(2)}, u32[]{:S(2)}) %collective-permute-start.12) | collective-permute-done | bytes 2097184 | tf_op jit(solution)/shard_map/ppermute | solution.py:39
  229.1 3.3 collective-permute-start.14
  232.4 3.6 slice_bitcast_fusion.7
  241.5 3.0 collective-permute-start.17
  246.0 3.2 broadcast_select_fusion
  251.6 7.6 %shard_map.20 = f32[512,512]{1,0:T(8,128)S(1)} custom-call(f32[1024,512]{1,0:T(8,128)} %get-tuple-element.496.refs_0_, f32[1024,512]{1,0:T(8,128)S(1)} %copy-done.18, f32[512,512]{1,0:T(8,128)S(1)} %get-tuple-element.307.refs_2_.refs_3_, f32[512,512]{1,0:T(8,128)S(1)} %get-tuple-element.308.refs_3_.refs_4_, ...), custom_call_target="tpu_custom_call" | custom-call | tf_op jit(solution)/shard_map/pallas_call | solution.py:269
  259.3 7.4 %shard_map.21 = f32[512,512]{1,0:T(8,128)S(1)} custom-call(f32[1024,512]{1,0:T(8,128)} %get-tuple-element.495.refs_0_, f32[1024,512]{1,0:T(8,128)S(1)} %copy-done.15, f32[512,512]{1,0:T(8,128)S(1)} %get-tuple-element.307.refs_2_.refs_3_, f32[512,512]{1,0:T(8,128)S(1)} %get-tuple-element.308.refs_3_.refs_4_, ...), custom_call_target="tpu_custom_call" | custom-call | tf_op jit(solution)/shard_map/pallas_call | solution.py:269
  266.7 6.2 shard_map.18
  272.9 7.5 %shard_map.19 = f32[512,512]{1,0:T(8,128)S(1)} custom-call(f32[1024,512]{1,0:T(8,128)S(1)} %copy-done.20, f32[1024,512]{1,0:T(8,128)} %collective-permute-done.5.refs_1_, f32[512,512]{1,0:T(8,128)S(1)} %get-tuple-element.307.refs_2_.refs_3_, f32[512,512]{1,0:T(8,128)S(1)} %get-tuple-element.308.refs_3_.refs_4_, ...), custom_call_target="tpu_custom_call" | custom-call | tf_op jit(solution)/shard_map/pallas_call | solution.py:269
  280.9 5.9 slice_bitcast_fusion.4
  288.2 3.4 collective-permute-start.21
  293.8 10.5 %shard_map.22 = (f32[512,512]{1,0:T(8,128)S(1)}, f32[512,512]{1,0:T(8,128)}) custom-call(f32[1024,512]{1,0:T(8,128)S(1)} %get-tuple-element.491.refs_0_, f32[1024,512]{1,0:T(8,128)S(1)} %copy-done.18, f32[1024,512]{1,0:T(8,128)} %collective-permute-done.15.refs_2_, f32[512,512]{1,0:T(8,128)S(1)} %get-tuple-element.307.refs_2_.refs_3_, ...), custom_call_target="tpu_custom_call" | custom-call | tf_op jit(solution)/shard_map/pallas_call | solution.py:269
  304.4 3.1 multiply_reduce_fusion.1
  314.3 3.1 collective-permute-start.24
  318.5 2.9 collective-permute-start.25
  325.8 10.0 %shard_map.23 = (f32[512,512]{1,0:T(8,128)S(1)}, f32[512,512]{1,0:T(8,128)S(1)}) custom-call(f32[1024,512]{1,0:T(8,128)S(1)} %copy-done.19, f32[1024,512]{1,0:T(8,128)S(1)} %copy-done.16, f32[1024,512]{1,0:T(8,128)} %collective-permute-done.16.refs_2_, f32[512,512]{1,0:T(8,128)S(1)} %get-tuple-element.307.refs_2_.refs_3_, f32[512,512]{1,0:T(8,128)S(1)} %copy-done.4, ...), custom_call_target="tpu_custom_call" | custom-call | tf_op jit(solution)/shard_map/pallas_call | solution.py:269
  337.8 2.9 select_select_fusion
  342.2 3.7 collective-permute-start.26
  345.9 3.0 collective-permute-start.27
  352.3 9.4 %shard_map.24 = (f32[512,512]{1,0:T(8,128)S(1)}, f32[512,512]{1,0:T(8,128)S(1)}) custom-call(f32[1024,512]{1,0:T(8,128)S(1)} %slice_bitcast_fusion.1.refs_0_, f32[1024,512]{1,0:T(8,128)S(1)} %copy-done.13, f32[1024,512]{1,0:T(8,128)S(1)} %copy-done.30, f32[512,512]{1,0:T(8,128)S(1)} %get-tuple-element.307.refs_2_.refs_3_, f32[512,512]{1,0:T(8,128)S(1)} %copy-done.5, ...), custom_call_target="tpu_custom_call" | custom-call | tf_op jit(solution)/shard_map/pallas_call | solution.py:269
  363.6 7.3 %collective-permute-done.27.refs_3_ = f32[256,512]{1,0:T(8,128)S(1)} collective-permute-done((f32[256,512]{1,0:T(8,128)}, f32[256,512]{1,0:T(8,128)S(1)}, u32[]{:S(2)}, u32[]{:S(2)}) %collective-permute-start.27) | collective-permute-done | bytes 524320 | tf_op jit(solution)/shard_map/ppermute | solution.py:39
  371.7 4.9 collective-permute-start.29
  380.1 10.1 %shard_map.25 = (f32[512,512]{1,0:T(8,128)S(1)}, f32[512,512]{1,0:T(8,128)S(1)}) custom-call(f32[1024,512]{1,0:T(8,128)S(1)} %slice_bitcast_fusion.refs_0_, f32[1024,512]{1,0:T(8,128)} %collective-permute-done.5.refs_1_, f32[1024,512]{1,0:T(8,128)} %collective-permute-done.23.refs_2_, f32[512,512]{1,0:T(8,128)S(1)} %get-tuple-element.307.refs_2_.refs_3_, ...), custom_call_target="tpu_custom_call" | custom-call | tf_op jit(solution)/shard_map/pallas_call | solution.py:269
  390.3 9.2 %collective-permute-done.29 = f32[512,512]{1,0:T(8,128)S(1)} collective-permute-done((f32[512,512]{1,0:T(8,128)S(1)}, f32[512,512]{1,0:T(8,128)S(1)}, u32[]{:S(2)}, u32[]{:S(2)}) %collective-permute-start.29) | collective-permute-done | bytes 1048608 | tf_op jit(solution)/shard_map/ppermute | solution.py:39
  403.2 3.0 collective-permute-start.34
  407.7 28.0 %collective-permute-done.33 = f32[2,512,512]{2,1,0:T(8,128)S(1)} collective-permute-done((f32[2,512,512]{2,1,0:T(8,128)S(1)}, f32[2,512,512]{2,1,0:T(8,128)S(1)}, u32[]{:S(2)}, u32[]{:S(2)}) %collective-permute-start.33) | collective-permute-done | bytes 2097184 | tf_op jit(solution)/shard_map/ppermute | solution.py:39
  442.7 19.6 %shard_map.26 = (f32[1024,512]{1,0:T(8,128)}, bf16[1024,1024]{1,0:T(8,128)(2,1)}, bf16[1024,1024]{1,0:T(8,128)(2,1)}) custom-call(s32[3]{0:T(128)S(1)} %pad_add_fusion.1.flags_ref, f32[512,512]{1,0:T(8,128)S(1)} %get-tuple-element.506.first_ref, f32[512,512]{1,0:T(8,128)S(1)} %get-tuple-element.505.second_ref), custom_call_target="tpu_custom_call" | custom-call | tf_op jit(solution)/shard_map/pallas_call | solution.py:168
  463.5 4.5 collective-permute-start.42
  469.0 4.1 collective-permute-start.43
  484.8 10.2 %shard_map.27 = (f32[512,512]{1,0:T(8,128)S(1)}, f32[512,512]{1,0:T(8,128)}) custom-call(f32[256,512]{1,0:T(8,128)S(1)} %copy-done.43, f32[256,512]{1,0:T(8,128)S(1)} %copy-done.46, f32[256,512]{1,0:T(8,128)} %collective-permute-done.8.refs_2_, f32[256,512]{1,0:T(8,128)S(1)} %copy-done.52, f32[256,512]{1,0:T(8,128)S(1)} %copy-done.63, ...), custom_call_target="tpu_custom_call" | custom-call | tf_op jit(solution)/shard_map/pallas_call | solution.py:269
  495.0 3.8 broadcast_select_fusion.1
  498.8 3.7 collective-permute-start.46
  510.8 10.1 %shard_map.28 = (f32[512,512]{1,0:T(8,128)S(1)}, f32[512,512]{1,0:T(8,128)S(1)}) custom-call(f32[256,512]{1,0:T(8,128)S(1)} %copy-done.49, f32[256,512]{1,0:T(8,128)S(1)} %copy-done.55, f32[256,512]{1,0:T(8,128)} %collective-permute-done.18.refs_2_, f32[256,512]{1,0:T(8,128)} %collective-permute-done.20.refs_3_, f32[256,512]{1,0:T(8,128)S(1)} %copy-done.67, ...), custom_call_target="tpu_custom_call" | custom-call | tf_op jit(solution)/shard_map/pallas_call | solution.py:269
  523.3 2.9 collective-permute-done.48.refs_3_
  527.4 9.4 %shard_map.29 = (f32[512,512]{1,0:T(8,128)S(1)}, f32[512,512]{1,0:T(8,128)S(1)}) custom-call(f32[512,512]{1,0:T(8,128)S(1)} %copy-done.32, f32[512,512]{1,0:T(8,128)S(1)} %copy-done.36, f32[512,512]{1,0:T(8,128)S(1)} %copy-done.40, f32[512,512]{1,0:T(8,128)} %collective-permute-done.48.refs_3_, f32[512,512]{1,0:T(8,128)S(1)} %get-tuple-element.464.refs_4_.refs_6_, ...), custom_call_target="tpu_custom_call" | custom-call | tf_op jit(solution)/shard_map/pallas_call | solution.py:269
  539.8 11.5 %collective-permute-done.50.refs_3_ = f32[512,512]{1,0:T(8,128)S(1)} collective-permute-done((f32[512,512]{1,0:T(8,128)S(1)}, f32[512,512]{1,0:T(8,128)S(1)}, u32[]{:S(2)}, u32[]{:S(2)}) %collective-permute-start.50) | collective-permute-done | bytes 1048608 | tf_op jit(solution)/shard_map/ppermute | solution.py:39
  551.3 8.3 %shard_map.30 = (f32[512,512]{1,0:T(8,128)S(1)}, f32[512,512]{1,0:T(8,128)S(1)}) custom-call(f32[512,512]{1,0:T(8,128)S(1)} %copy-done.34, f32[512,512]{1,0:T(8,128)S(1)} %copy-done.38, f32[512,512]{1,0:T(8,128)S(1)} %get-tuple-element.472.refs_2_, f32[512,512]{1,0:T(8,128)S(1)} %collective-permute-done.50.refs_3_, ...), custom_call_target="tpu_custom_call" | custom-call | tf_op jit(solution)/shard_map/pallas_call | solution.py:269
  560.8 9.8 %shard_map.31 = (f32[512,512]{1,0:T(8,128)S(1)}, f32[512,512]{1,0:T(8,128)S(1)}) custom-call(f32[512,512]{1,0:T(8,128)S(1)} %copy-done.23, f32[512,512]{1,0:T(8,128)} %collective-permute-done.28.refs_1_, f32[256,512]{1,0:T(8,128)} %collective-permute-done.25.refs_2_, f32[256,512]{1,0:T(8,128)S(1)} %copy-done.57, f32[256,512]{1,0:T(8,128)S(1)} %copy-done.59, ...), custom_call_target="tpu_custom_call" | custom-call | tf_op jit(solution)/shard_map/pallas_call | solution.py:269
  571.1 5.8 collective-permute-done.54.refs_5_
  576.9 9.3 %shard_map.32 = (f32[512,512]{1,0:T(8,128)S(1)}, f32[512,512]{1,0:T(8,128)S(1)}) custom-call(f32[512,512]{1,0:T(8,128)S(1)} %copy-done.26, f32[512,512]{1,0:T(8,128)S(1)} %copy-done.28, f32[256,512]{1,0:T(8,128)} %collective-permute-done.43.refs_2_, f32[256,512]{1,0:T(8,128)S(1)} %collective-permute-done.47.refs_3_, ...), custom_call_target="tpu_custom_call" | custom-call | tf_op jit(solution)/shard_map/pallas_call | solution.py:269
  588.1 8.1 %collective-permute-done.51 = f32[512,512]{1,0:T(8,128)S(1)} collective-permute-done((f32[512,512]{1,0:T(8,128)S(1)}, f32[512,512]{1,0:T(8,128)S(1)}, u32[]{:S(2)}, u32[]{:S(2)}) %collective-permute-start.51) | collective-permute-done | bytes 1048608 | tf_op jit(solution)/shard_map/ppermute | solution.py:39
  596.7 22.0 %collective-permute-done.52 = f32[512,512]{1,0:T(8,128)S(1)} collective-permute-done((f32[512,512]{1,0:T(8,128)S(1)}, f32[512,512]{1,0:T(8,128)S(1)}, u32[]{:S(2)}, u32[]{:S(2)}) %collective-permute-start.52) | collective-permute-done | bytes 1048608 | tf_op jit(solution)/shard_map/ppermute | solution.py:39
  619.2 21.5 %collective-permute-done.55 = f32[512,512]{1,0:T(8,128)S(1)} collective-permute-done((f32[512,512]{1,0:T(8,128)S(1)}, f32[512,512]{1,0:T(8,128)S(1)}, u32[]{:S(2)}, u32[]{:S(2)}) %collective-permute-start.55) | collective-permute-done | bytes 1048608 | tf_op jit(solution)/shard_map/ppermute | solution.py:39
  641.1 3.4 copy-done.77
  (289 shorter events, 113.2 us)
Async XLA Ops:
  2.9 4.4 collective-permute-start
  7.1 22.7 %collective-permute-start.1 = (f32[256,512]{1,0:T(8,128)S(1)}, f32[256,512]{1,0:T(8,128)S(1)}, u32[]{:S(2)}, u32[]{:S(2)}) collective-permute-start(f32[256,512]{1,0:T(8,128)S(1)} %slice_bitcast_fusion.23), channel_id=1, source_target_pairs={{0,4},{1,5},{2,6},{3,7},{4,0},{5,1},{6,2},{7,3},{8,12},{9,13},{10,... | collective-permute-start | bytes 1572872 | tf_op jit(solution)/shard_map/ppermute | solution.py:39
  33.6 42.3 %collective-permute-start.3 = (f32[1024,512]{1,0:T(8,128)}, f32[1024,512]{1,0:T(8,128)S(1)}, u32[]{:S(2)}, u32[]{:S(2)}) collective-permute-start(f32[1024,512]{1,0:T(8,128)} %slice_bitcast_fusion.13), channel_id=1, source_target_pairs={{0,1},{1,0},{4,5},{5,4},{10,11},{11,10},{14,15},{15,14},{16,17},{1... | collective-permute-start | bytes 6291464 | tf_op jit(solution)/shard_map/ppermute | solution.py:39
  36.7 37.8 %collective-permute-start.2 = (f32[512,512]{1,0:T(8,128)}, f32[512,512]{1,0:T(8,128)}, u32[]{:S(2)}, u32[]{:S(2)}) collective-permute-start(f32[512,512]{1,0:T(8,128)} %select_select_fusion.1), channel_id=1, source_target_pairs={{0,4},{1,5},{10,14},{11,15},{20,16},{21,17},{30,26},{31,27}} | collective-permute-start | bytes 3145736 | tf_op jit(solution)/shard_map/ppermute | solution.py:39
  79.8 38.3 %collective-permute-start.5 = (f32[1024,512]{1,0:T(8,128)}, f32[1024,512]{1,0:T(8,128)}, u32[]{:S(2)}, u32[]{:S(2)}) collective-permute-start(f32[1024,512]{1,0:T(8,128)} %slice_bitcast_fusion.12), channel_id=1, source_target_pairs={{0,1},{1,0},{4,5},{5,4},{10,11},{11,10},{14,15},{15,14},{16,17},{1... | collective-permute-start | bytes 6291464 | tf_op jit(solution)/shard_map/ppermute | solution.py:39
  81.9 13.0 %collective-permute-start.4 = (f32[512,512]{1,0:T(8,128)S(1)}, f32[512,512]{1,0:T(8,128)S(1)}, u32[]{:S(2)}, u32[]{:S(2)}) collective-permute-start(f32[512,512]{1,0:T(8,128)S(1)} %broadcast_select_fusion.6), channel_id=1, source_target_pairs={{0,2},{1,3},{4,6},{5,7},{10,8},{11,9},{14,12},{15,13},{16,18},{17,... | collective-permute-start | bytes 3145736 | tf_op jit(solution)/shard_map/ppermute | solution.py:39
  84.4 25.2 %collective-permute-start.6 = (f32[256,512]{1,0:T(8,128)S(1)}, f32[256,512]{1,0:T(8,128)S(1)}, u32[]{:S(2)}, u32[]{:S(2)}) collective-permute-start(f32[256,512]{1,0:T(8,128)S(1)} %slice_bitcast_fusion.22), channel_id=1, source_target_pairs={{0,4},{1,5},{2,6},{3,7},{4,0},{5,1},{6,2},{7,3},{8,12},{9,13},{10,... | collective-permute-start | bytes 1572872 | tf_op jit(solution)/shard_map/ppermute | solution.py:39
  109.6 37.8 %copy-start.44 = (f32[256,512]{1,0:T(8,128)}, f32[256,512]{1,0:T(8,128)S(1)}, u32[]{:S(2)}) copy-start(f32[256,512]{1,0:T(8,128)S(1)} %collective-permute-done.6.refs_1_) | copy-start | bytes 1572868
  118.1 26.0 %collective-permute-start.7 = (f32[512,512]{1,0:T(8,128)S(1)}, f32[512,512]{1,0:T(8,128)S(1)}, u32[]{:S(2)}, u32[]{:S(2)}) collective-permute-start(f32[512,512]{1,0:T(8,128)S(1)} %broadcast_select_fusion.5), channel_id=1, source_target_pairs={{0,1},{1,0},{2,3},{3,2},{4,5},{5,4},{6,7},{7,6},{8,9},{9,8},{10,11... | collective-permute-start | bytes 3145736 | tf_op jit(solution)/shard_map/ppermute | solution.py:39
  119.4 24.7 %collective-permute-start.8 = (f32[256,512]{1,0:T(8,128)S(1)}, f32[256,512]{1,0:T(8,128)}, u32[]{:S(2)}, u32[]{:S(2)}) collective-permute-start(f32[256,512]{1,0:T(8,128)S(1)} %slice_bitcast_fusion.21), channel_id=1, source_target_pairs={{0,4},{1,5},{2,6},{3,7},{4,0},{5,1},{6,2},{7,3},{8,12},{9,13},{10,... | collective-permute-start | bytes 1572872 | tf_op jit(solution)/shard_map/ppermute | solution.py:39
  144.1 36.1 %slice-start = ((s8[8388608]{0:T(1024)(128)(4,1)}), s8[4194304]{0:T(1024)(128)(4,1)S(1)}, s32[]{:S(2)}) async-start(s8[8388608]{0:T(1024)(128)(4,1)} %bitcast.92), calls=%async_computation | async-start | bytes 8388608
  147.4 27.0 %collective-permute-start.9 = (f32[1024,512]{1,0:T(8,128)}, f32[1024,512]{1,0:T(8,128)S(1)}, u32[]{:S(2)}, u32[]{:S(2)}) collective-permute-start(f32[1024,512]{1,0:T(8,128)} %slice_bitcast_fusion.11), channel_id=1, source_target_pairs={{0,1},{1,0},{4,5},{5,4},{10,11},{11,10},{14,15},{15,14},{16,17},{1... | collective-permute-start | bytes 6291464 | tf_op jit(solution)/shard_map/ppermute | solution.py:39
  150.5 22.3 %collective-permute-start.10 = (f32[256,512]{1,0:T(8,128)S(1)}, f32[256,512]{1,0:T(8,128)S(1)}, u32[]{:S(2)}, u32[]{:S(2)}) collective-permute-start(f32[256,512]{1,0:T(8,128)S(1)} %slice_bitcast_fusion.20), channel_id=1, source_target_pairs={{0,4},{1,5},{2,6},{3,7},{4,0},{5,1},{6,2},{7,3},{8,12},{9,13},{10,... | collective-permute-start | bytes 1572872 | tf_op jit(solution)/shard_map/ppermute | solution.py:39
  174.3 27.2 %collective-permute-start.11 = (f32[1024,512]{1,0:T(8,128)S(1)}, f32[1024,512]{1,0:T(8,128)S(1)}, u32[]{:S(2)}, u32[]{:S(2)}) collective-permute-start(f32[1024,512]{1,0:T(8,128)S(1)} %get-tuple-element.269), channel_id=1, source_target_pairs={{0,16},{1,17},{4,20},{5,21},{10,26},{11,27},{14,30},{15,31},{16,0}... | collective-permute-start | bytes 6291464 | tf_op jit(solution)/shard_map/ppermute | solution.py:39
  178.0 49.7 %collective-permute-start.12 = (f32[1024,512]{1,0:T(8,128)S(1)}, f32[1024,512]{1,0:T(8,128)S(1)}, u32[]{:S(2)}, u32[]{:S(2)}) collective-permute-start(f32[1024,512]{1,0:T(8,128)S(1)} %slice_bitcast_fusion.10), channel_id=1, source_target_pairs={{0,1},{1,0},{4,5},{5,4},{10,11},{11,10},{14,15},{15,14},{16,17},{1... | collective-permute-start | bytes 6291464 | tf_op jit(solution)/shard_map/ppermute | solution.py:39
  180.3 31.1 %collective-permute-start.13 = (f32[256,512]{1,0:T(8,128)S(1)}, f32[256,512]{1,0:T(8,128)S(1)}, u32[]{:S(2)}, u32[]{:S(2)}) collective-permute-start(f32[256,512]{1,0:T(8,128)S(1)} %slice_bitcast_fusion.19), channel_id=1, source_target_pairs={{0,4},{1,5},{2,6},{3,7},{4,0},{5,1},{6,2},{7,3},{8,12},{9,13},{10,... | collective-permute-start | bytes 1572872 | tf_op jit(solution)/shard_map/ppermute | solution.py:39
  229.1 17.0 %collective-permute-start.14 = (f32[2,1024,512]{2,1,0:T(8,128)}, f32[2,1024,512]{2,1,0:T(8,128)}, u32[]{:S(2)}, u32[]{:S(2)}) collective-permute-start(f32[2,1024,512]{2,1,0:T(8,128)} %pad_maximum_fusion), channel_id=1, source_target_pairs={{0,8},{1,9},{4,12},{5,13},{10,2},{11,3},{14,6},{15,7},{16,24},{17,... | collective-permute-start | bytes 12582920 | tf_op jit(solution)/shard_map/ppermute | solution.py:39
  236.0 44.9 %collective-permute-start.15 = (f32[1024,512]{1,0:T(8,128)}, f32[1024,512]{1,0:T(8,128)}, u32[]{:S(2)}, u32[]{:S(2)}) collective-permute-start(f32[1024,512]{1,0:T(8,128)} %get-tuple-element.496.refs_0_), channel_id=1, source_target_pairs={{2,3},{3,2},{6,7},{7,6},{8,9},{9,8},{12,13},{13,12},{18,19},{19,18... | collective-permute-start | bytes 6291464 | tf_op jit(solution)/shard_map/ppermute | solution.py:39
  238.1 42.8 %collective-permute-start.16 = (f32[1024,512]{1,0:T(8,128)}, f32[1024,512]{1,0:T(8,128)}, u32[]{:S(2)}, u32[]{:S(2)}) collective-permute-start(f32[1024,512]{1,0:T(8,128)} %get-tuple-element.495.refs_0_), channel_id=1, source_target_pairs={{2,3},{3,2},{6,7},{7,6},{8,9},{9,8},{12,13},{13,12},{18,19},{19,18... | collective-permute-start | bytes 6291464 | tf_op jit(solution)/shard_map/ppermute | solution.py:39
  241.5 39.3 %collective-permute-start.17 = (f32[256,512]{1,0:T(8,128)S(1)}, f32[256,512]{1,0:T(8,128)S(1)}, u32[]{:S(2)}, u32[]{:S(2)}) collective-permute-start(f32[256,512]{1,0:T(8,128)S(1)} %get-tuple-element.498), channel_id=1, source_target_pairs={{0,4},{1,5},{2,6},{3,7},{4,0},{5,1},{6,2},{7,3},{8,12},{9,13},{10,... | collective-permute-start | bytes 1572872 | tf_op jit(solution)/shard_map/ppermute | solution.py:39
  244.5 36.3 %collective-permute-start.18 = (f32[256,512]{1,0:T(8,128)S(1)}, f32[256,512]{1,0:T(8,128)}, u32[]{:S(2)}, u32[]{:S(2)}) collective-permute-start(f32[256,512]{1,0:T(8,128)S(1)} %get-tuple-element.497), channel_id=1, source_target_pairs={{0,4},{1,5},{2,6},{3,7},{4,0},{5,1},{6,2},{7,3},{8,12},{9,13},{10,... | collective-permute-start | bytes 1572872 | tf_op jit(solution)/shard_map/ppermute | solution.py:39
  251.6 42.3 %copy-start.3 = (f32[512,512]{1,0:T(8,128)}, f32[512,512]{1,0:T(8,128)S(1)}, u32[]{:S(2)}) copy-start(f32[512,512]{1,0:T(8,128)S(1)} %get-tuple-element.308.refs_3_.refs_4_) | copy-start | bytes 3145732
  286.8 22.7 %collective-permute-start.19 = (f32[1024,512]{1,0:T(8,128)}, f32[1024,512]{1,0:T(8,128)S(1)}, u32[]{:S(2)}, u32[]{:S(2)}) collective-permute-start(f32[1024,512]{1,0:T(8,128)} %get-tuple-element.492), channel_id=1, source_target_pairs={{2,3},{3,2},{6,7},{7,6},{8,9},{9,8},{12,13},{13,12},{18,19},{19,18... | collective-permute-start | bytes 6291464 | tf_op jit(solution)/shard_map/ppermute | solution.py:39
  288.2 16.2 %collective-permute-start.21 = (f32[4,512]{1,0:T(4,128)S(1)}, f32[4,512]{1,0:T(4,128)S(1)}, u32[]{:S(2)}, u32[]{:S(2)}) collective-permute-start(f32[4,512]{1,0:T(4,128)S(1)} %select_reduce_fusion), channel_id=1, source_target_pairs={{0,16},{1,17},{10,26},{11,27},{20,4},{21,5},{30,14},{31,15}} | collective-permute-start | bytes 24584 | tf_op jit(solution)/shard_map/ppermute | solution.py:39
  291.5 12.8 %collective-permute-start.22 = (f32[4,512]{1,0:T(4,128)S(1)}, f32[4,512]{1,0:T(4,128)S(1)}, u32[]{:S(2)}, u32[]{:S(2)}) collective-permute-start(f32[4,512]{1,0:T(4,128)S(1)} %select_reduce_fusion), channel_id=1, source_target_pairs={{0,4},{1,5},{10,14},{11,15},{20,16},{21,17},{30,26},{31,27}} | collective-permute-start | bytes 24584 | tf_op jit(solution)/shard_map/ppermute | solution.py:39
  293.7 15.8 %collective-permute-start.20 = (f32[256,512]{1,0:T(8,128)S(1)}, f32[256,512]{1,0:T(8,128)}, u32[]{:S(2)}, u32[]{:S(2)}) collective-permute-start(f32[256,512]{1,0:T(8,128)S(1)} %slice_bitcast_fusion.16), channel_id=1, source_target_pairs={{0,4},{1,5},{2,6},{3,7},{4,0},{5,1},{6,2},{7,3},{8,12},{9,13},{10,... | collective-permute-start | bytes 1572872 | tf_op jit(solution)/shard_map/ppermute | solution.py:39
  312.3 29.9 %collective-permute-start.23 = (f32[1024,512]{1,0:T(8,128)}, f32[1024,512]{1,0:T(8,128)}, u32[]{:S(2)}, u32[]{:S(2)}) collective-permute-start(f32[1024,512]{1,0:T(8,128)} %get-tuple-element.490), channel_id=1, source_target_pairs={{2,3},{3,2},{6,7},{7,6},{8,9},{9,8},{12,13},{13,12},{18,19},{19,18... | collective-permute-start | bytes 6291464 | tf_op jit(solution)/shard_map/ppermute | solution.py:39
  314.3 23.5 %collective-permute-start.24 = (f32[512,512]{1,0:T(8,128)}, f32[512,512]{1,0:T(8,128)}, u32[]{:S(2)}, u32[]{:S(2)}) collective-permute-start(f32[512,512]{1,0:T(8,128)} %broadcast_multiply_fusion.1), channel_id=1, source_target_pairs={{0,16},{1,17},{4,20},{5,21},{10,26},{11,27},{14,30},{15,31},{16,0}... | collective-permute-start | bytes 3145736 | tf_op jit(solution)/shard_map/ppermute | solution.py:39
  318.5 23.7 %collective-permute-start.25 = (f32[256,512]{1,0:T(8,128)}, f32[256,512]{1,0:T(8,128)}, u32[]{:S(2)}, u32[]{:S(2)}) collective-permute-start(f32[256,512]{1,0:T(8,128)} %get-tuple-element.522), channel_id=1, source_target_pairs={{0,4},{1,5},{2,6},{3,7},{4,0},{5,1},{6,2},{7,3},{8,12},{9,13},{10,... | collective-permute-start | bytes 1572872 | tf_op jit(solution)/shard_map/ppermute | solution.py:39
  342.2 19.5 %collective-permute-start.26 = (f32[512,512]{1,0:T(8,128)}, f32[512,512]{1,0:T(8,128)}, u32[]{:S(2)}, u32[]{:S(2)}) collective-permute-start(f32[512,512]{1,0:T(8,128)} %select_select_fusion), channel_id=1, source_target_pairs={{0,1},{4,5},{10,11},{14,15},{17,16},{21,20},{27,26},{31,30}} | collective-permute-start | bytes 3145736 | tf_op jit(solution)/shard_map/ppermute | solution.py:39
  345.9 25.7 %collective-permute-start.28 = (f32[512,512]{1,0:T(8,128)}, f32[512,512]{1,0:T(8,128)}, u32[]{:S(2)}, u32[]{:S(2)}) collective-permute-start(f32[512,512]{1,0:T(8,128)} %get-tuple-element.333), channel_id=1, source_target_pairs={{0,16},{1,17},{2,18},{3,19},{4,20},{5,21},{6,22},{7,23},{8,24},{9,... | collective-permute-start | bytes 3145736 | tf_op jit(solution)/shard_map/ppermute | solution.py:39
  345.9 24.9 %collective-permute-start.27 = (f32[256,512]{1,0:T(8,128)}, f32[256,512]{1,0:T(8,128)S(1)}, u32[]{:S(2)}, u32[]{:S(2)}) collective-permute-start(f32[256,512]{1,0:T(8,128)} %get-tuple-element.337), channel_id=1, source_target_pairs={{0,4},{1,5},{2,6},{3,7},{4,0},{5,1},{6,2},{7,3},{8,12},{9,13},{10,... | collective-permute-start | bytes 1572872 | tf_op jit(solution)/shard_map/ppermute | solution.py:39
  371.7 27.9 %collective-permute-start.29 = (f32[512,512]{1,0:T(8,128)S(1)}, f32[512,512]{1,0:T(8,128)S(1)}, u32[]{:S(2)}, u32[]{:S(2)}) collective-permute-start(f32[512,512]{1,0:T(8,128)S(1)} %broadcast_select_fusion.4), channel_id=1, source_target_pairs={{0,4},{1,5},{4,0},{5,1},{10,14},{11,15},{14,10},{15,11},{16,20},{1... | collective-permute-start | bytes 3145736 | tf_op jit(solution)/shard_map/ppermute | solution.py:39
  376.6 23.5 %collective-permute-start.30 = (f32[512,512]{1,0:T(8,128)S(1)}, f32[512,512]{1,0:T(8,128)S(1)}, u32[]{:S(2)}, u32[]{:S(2)}) collective-permute-start(f32[512,512]{1,0:T(8,128)S(1)} %copy-done.75), channel_id=1, source_target_pairs={{0,16},{1,17},{2,18},{3,19},{4,20},{5,21},{6,22},{7,23},{8,24},{9,... | collective-permute-start | bytes 3145736 | tf_op jit(solution)/shard_map/ppermute | solution.py:39
  376.9 23.1 %collective-permute-start.31 = (f32[256,512]{1,0:T(8,128)S(1)}, f32[256,512]{1,0:T(8,128)S(1)}, u32[]{:S(2)}, u32[]{:S(2)}) collective-permute-start(f32[256,512]{1,0:T(8,128)S(1)} %copy-done.42), channel_id=1, source_target_pairs={{0,1},{1,0},{2,3},{3,2},{4,5},{5,4},{6,7},{7,6},{8,9},{9,8},{10,11... | collective-permute-start | bytes 1572872 | tf_op jit(solution)/shard_map/ppermute | solution.py:39
  377.5 22.5 %collective-permute-start.32 = (f32[256,512]{1,0:T(8,128)S(1)}, f32[256,512]{1,0:T(8,128)S(1)}, u32[]{:S(2)}, u32[]{:S(2)}) collective-permute-start(f32[256,512]{1,0:T(8,128)S(1)} %copy-done.45), channel_id=1, source_target_pairs={{0,1},{1,0},{2,3},{3,2},{4,5},{5,4},{6,7},{7,6},{8,9},{9,8},{10,11... | collective-permute-start | bytes 1572872 | tf_op jit(solution)/shard_map/ppermute | solution.py:39
  400.0 36.2 %copy-start.62 = (f32[256,512]{1,0:T(8,128)}, f32[256,512]{1,0:T(8,128)S(1)}, u32[]{:S(2)}) copy-start(f32[256,512]{1,0:T(8,128)S(1)} %collective-permute-done.31.refs_4_) | copy-start | bytes 1572868
  400.0 36.1 %copy-start.64 = (f32[256,512]{1,0:T(8,128)}, f32[256,512]{1,0:T(8,128)S(1)}, u32[]{:S(2)}) copy-start(f32[256,512]{1,0:T(8,128)S(1)} %collective-permute-done.32.refs_5_) | copy-start | bytes 1572868
  400.1 36.1 %copy-start.27 = (f32[512,512]{1,0:T(8,128)}, f32[512,512]{1,0:T(8,128)S(1)}, u32[]{:S(2)}) copy-start(f32[512,512]{1,0:T(8,128)S(1)} %collective-permute-done.30.refs_1_) | copy-start | bytes 3145732
  400.1 35.6 %collective-permute-start.33 = (f32[2,512,512]{2,1,0:T(8,128)S(1)}, f32[2,512,512]{2,1,0:T(8,128)S(1)}, u32[]{:S(2)}, u32[]{:S(2)}) collective-permute-start(f32[2,512,512]{2,1,0:T(8,128)S(1)} %pad_maximum_fusion.2), channel_id=1, source_target_pairs={{0,2},{1,3},{4,6},{5,7},{10,8},{11,9},{14,12},{15,13},{16,18},{17,... | collective-permute-start | bytes 6291464 | tf_op jit(solution)/shard_map/ppermute | solution.py:39
  401.6 39.0 %collective-permute-start.35 = (f32[512,512]{1,0:T(8,128)S(1)}, f32[512,512]{1,0:T(8,128)S(1)}, u32[]{:S(2)}, u32[]{:S(2)}) collective-permute-start(f32[512,512]{1,0:T(8,128)S(1)} %get-tuple-element.372), channel_id=1, source_target_pairs={{0,16},{1,17},{2,18},{3,19},{4,20},{5,21},{6,22},{7,23},{8,24},{9,... | collective-permute-start | bytes 3145736 | tf_op jit(solution)/shard_map/ppermute | solution.py:39
  403.2 37.7 %copy-start.48 = (f32[256,512]{1,0:T(8,128)S(1)}, f32[256,512]{1,0:T(8,128)}, u32[]{:S(2)}) copy-start(f32[256,512]{1,0:T(8,128)} %copy-done.47) | copy-start | bytes 1572868
  403.2 38.3 %copy-start.54 = (f32[256,512]{1,0:T(8,128)S(1)}, f32[256,512]{1,0:T(8,128)}, u32[]{:S(2)}) copy-start(f32[256,512]{1,0:T(8,128)} %copy-done.53) | copy-start | bytes 1572868
  403.2 35.7 %collective-permute-start.34 = (f32[256,512]{1,0:T(8,128)S(1)}, f32[256,512]{1,0:T(8,128)S(1)}, u32[]{:S(2)}, u32[]{:S(2)}) collective-permute-start(f32[256,512]{1,0:T(8,128)S(1)} %get-tuple-element.520), channel_id=1, source_target_pairs={{0,4},{1,5},{2,6},{3,7},{4,0},{5,1},{6,2},{7,3},{8,12},{9,13},{10,... | collective-permute-start | bytes 1572872 | tf_op jit(solution)/shard_map/ppermute | solution.py:39
  406.2 32.7 %collective-permute-start.36 = (f32[256,512]{1,0:T(8,128)}, f32[256,512]{1,0:T(8,128)S(1)}, u32[]{:S(2)}, u32[]{:S(2)}) collective-permute-start(f32[256,512]{1,0:T(8,128)} %collective-permute-done.8.refs_2_), channel_id=1, source_target_pairs={{0,1},{1,0},{2,3},{3,2},{4,5},{5,4},{6,7},{7,6},{8,9},{9,8},{10,11... | collective-permute-start | bytes 1572872 | tf_op jit(solution)/shard_map/ppermute | solution.py:39
  406.8 33.0 %collective-permute-start.37 = (f32[256,512]{1,0:T(8,128)S(1)}, f32[256,512]{1,0:T(8,128)S(1)}, u32[]{:S(2)}, u32[]{:S(2)}) collective-permute-start(f32[256,512]{1,0:T(8,128)S(1)} %copy-done.51), channel_id=1, source_target_pairs={{0,1},{1,0},{2,3},{3,2},{4,5},{5,4},{6,7},{7,6},{8,9},{9,8},{10,11... | collective-permute-start | bytes 1572872 | tf_op jit(solution)/shard_map/ppermute | solution.py:39
  440.6 22.9 %collective-permute-start.39 = (f32[512,512]{1,0:T(8,128)S(1)}, f32[512,512]{1,0:T(8,128)S(1)}, u32[]{:S(2)}, u32[]{:S(2)}) collective-permute-start(f32[512,512]{1,0:T(8,128)S(1)} %get-tuple-element.398), channel_id=1, source_target_pairs={{0,16},{1,17},{2,18},{3,19},{4,20},{5,21},{6,22},{7,23},{8,24},{9,... | collective-permute-start | bytes 3145736 | tf_op jit(solution)/shard_map/ppermute | solution.py:39
  440.9 21.7 %collective-permute-start.38 = (f32[256,512]{1,0:T(8,128)S(1)}, f32[256,512]{1,0:T(8,128)S(1)}, u32[]{:S(2)}, u32[]{:S(2)}) collective-permute-start(f32[256,512]{1,0:T(8,128)S(1)} %get-tuple-element.396), channel_id=1, source_target_pairs={{0,4},{1,5},{2,6},{3,7},{4,0},{5,1},{6,2},{7,3},{8,12},{9,13},{10,... | collective-permute-start | bytes 1572872 | tf_op jit(solution)/shard_map/ppermute | solution.py:39
  440.9 21.7 %collective-permute-start.40 = (f32[256,512]{1,0:T(8,128)S(1)}, f32[256,512]{1,0:T(8,128)S(1)}, u32[]{:S(2)}, u32[]{:S(2)}) collective-permute-start(f32[256,512]{1,0:T(8,128)S(1)} %copy-done.48), channel_id=1, source_target_pairs={{0,1},{1,0},{2,3},{3,2},{4,5},{5,4},{6,7},{7,6},{8,9},{9,8},{10,11... | collective-permute-start | bytes 1572872 | tf_op jit(solution)/shard_map/ppermute | solution.py:39
  441.5 21.1 %collective-permute-start.41 = (f32[256,512]{1,0:T(8,128)S(1)}, f32[256,512]{1,0:T(8,128)S(1)}, u32[]{:S(2)}, u32[]{:S(2)}) collective-permute-start(f32[256,512]{1,0:T(8,128)S(1)} %copy-done.54), channel_id=1, source_target_pairs={{0,1},{1,0},{2,3},{3,2},{4,5},{5,4},{6,7},{7,6},{8,9},{9,8},{10,11... | collective-permute-start | bytes 1572872 | tf_op jit(solution)/shard_map/ppermute | solution.py:39
  463.5 31.5 %collective-permute-start.42 = (f32[1024,512]{1,0:T(8,128)}, f32[1024,512]{1,0:T(8,128)}, u32[]{:S(2)}, u32[]{:S(2)}) collective-permute-start(f32[1024,512]{1,0:T(8,128)} %get-tuple-element.414), channel_id=1, source_target_pairs={{0,16},{4,20},{10,26},{14,30},{17,1},{21,5},{27,11},{31,15}} | collective-permute-start | bytes 6291464 | tf_op jit(solution)/shard_map/ppermute | solution.py:39
  469.0 29.7 %collective-permute-start.43 = (f32[256,512]{1,0:T(8,128)}, f32[256,512]{1,0:T(8,128)}, u32[]{:S(2)}, u32[]{:S(2)}) collective-permute-start(f32[256,512]{1,0:T(8,128)} %get-tuple-element.518), channel_id=1, source_target_pairs={{0,4},{1,5},{2,6},{3,7},{4,0},{5,1},{6,2},{7,3},{8,12},{9,13},{10,... | collective-permute-start | bytes 1572872 | tf_op jit(solution)/shard_map/ppermute | solution.py:39
  473.2 25.6 %collective-permute-start.44 = (f32[256,512]{1,0:T(8,128)}, f32[256,512]{1,0:T(8,128)}, u32[]{:S(2)}, u32[]{:S(2)}) collective-permute-start(f32[256,512]{1,0:T(8,128)} %collective-permute-done.18.refs_2_), channel_id=1, source_target_pairs={{0,1},{1,0},{2,3},{3,2},{4,5},{5,4},{6,7},{7,6},{8,9},{9,8},{10,11... | collective-permute-start | bytes 1572872 | tf_op jit(solution)/shard_map/ppermute | solution.py:39
  473.2 25.6 %collective-permute-start.45 = (f32[256,512]{1,0:T(8,128)}, f32[256,512]{1,0:T(8,128)}, u32[]{:S(2)}, u32[]{:S(2)}) collective-permute-start(f32[256,512]{1,0:T(8,128)} %collective-permute-done.20.refs_3_), channel_id=1, source_target_pairs={{0,1},{1,0},{2,3},{3,2},{4,5},{5,4},{6,7},{7,6},{8,9},{9,8},{10,11... | collective-permute-start | bytes 1572872 | tf_op jit(solution)/shard_map/ppermute | solution.py:39
  498.8 22.1 %collective-permute-start.46 = (f32[1024,512]{1,0:T(8,128)}, f32[1024,512]{1,0:T(8,128)}, u32[]{:S(2)}, u32[]{:S(2)}) collective-permute-start(f32[1024,512]{1,0:T(8,128)} %broadcast_select_fusion.1), channel_id=1, source_target_pairs={{0,8},{1,9},{4,12},{5,13},{10,2},{11,3},{14,6},{15,7},{16,24},{17,... | collective-permute-start | bytes 6291464 | tf_op jit(solution)/shard_map/ppermute | solution.py:39
  502.5 23.7 %collective-permute-start.48 = (f32[512,512]{1,0:T(8,128)}, f32[512,512]{1,0:T(8,128)}, u32[]{:S(2)}, u32[]{:S(2)}) collective-permute-start(f32[512,512]{1,0:T(8,128)} %get-tuple-element.459), channel_id=1, source_target_pairs={{0,16},{1,17},{2,18},{3,19},{4,20},{5,21},{6,22},{7,23},{8,24},{9,... | collective-permute-start | bytes 3145736 | tf_op jit(solution)/shard_map/ppermute | solution.py:39
  503.6 19.7 %collective-permute-start.47 = (f32[256,512]{1,0:T(8,128)}, f32[256,512]{1,0:T(8,128)S(1)}, u32[]{:S(2)}, u32[]{:S(2)}) collective-permute-start(f32[256,512]{1,0:T(8,128)} %get-tuple-element.446), channel_id=1, source_target_pairs={{0,4},{1,5},{2,6},{3,7},{4,0},{5,1},{6,2},{7,3},{8,12},{9,13},{10,... | collective-permute-start | bytes 1572872 | tf_op jit(solution)/shard_map/ppermute | solution.py:39
  526.3 25.1 %collective-permute-start.50 = (f32[512,512]{1,0:T(8,128)S(1)}, f32[512,512]{1,0:T(8,128)S(1)}, u32[]{:S(2)}, u32[]{:S(2)}) collective-permute-start(f32[512,512]{1,0:T(8,128)S(1)} %get-tuple-element.473), channel_id=1, source_target_pairs={{0,16},{1,17},{2,18},{3,19},{4,20},{5,21},{6,22},{7,23},{8,24},{9,... | collective-permute-start | bytes 3145736 | tf_op jit(solution)/shard_map/ppermute | solution.py:39
  536.9 50.9 %collective-permute-start.49 = (f32[512,512]{1,0:T(8,128)S(1)}, f32[512,512]{1,0:T(8,128)S(1)}, u32[]{:S(2)}, u32[]{:S(2)}) collective-permute-start(f32[512,512]{1,0:T(8,128)S(1)} %get-tuple-element.469), channel_id=1, source_target_pairs={{0,16},{1,17},{2,18},{3,19},{4,20},{5,21},{6,22},{7,23},{8,24},{9,... | collective-permute-start | bytes 3145736 | tf_op jit(solution)/shard_map/ppermute | solution.py:39
  537.3 33.8 %collective-permute-start.53 = (f32[256,512]{1,0:T(8,128)S(1)}, f32[256,512]{1,0:T(8,128)S(1)}, u32[]{:S(2)}, u32[]{:S(2)}) collective-permute-start(f32[256,512]{1,0:T(8,128)S(1)} %get-tuple-element.516), channel_id=1, source_target_pairs={{0,4},{1,5},{2,6},{3,7},{4,0},{5,1},{6,2},{7,3},{8,12},{9,13},{10,... | collective-permute-start | bytes 1572872 | tf_op jit(solution)/shard_map/ppermute | solution.py:39
  538.4 38.5 %collective-permute-start.54 = (f32[256,512]{1,0:T(8,128)S(1)}, f32[256,512]{1,0:T(8,128)S(1)}, u32[]{:S(2)}, u32[]{:S(2)}) collective-permute-start(f32[256,512]{1,0:T(8,128)S(1)} %get-tuple-element.515), channel_id=1, source_target_pairs={{0,4},{1,5},{2,6},{3,7},{4,0},{5,1},{6,2},{7,3},{8,12},{9,13},{10,... | collective-permute-start | bytes 1572872 | tf_op jit(solution)/shard_map/ppermute | solution.py:39
  559.6 36.6 %collective-permute-start.51 = (f32[512,512]{1,0:T(8,128)S(1)}, f32[512,512]{1,0:T(8,128)S(1)}, u32[]{:S(2)}, u32[]{:S(2)}) collective-permute-start(f32[512,512]{1,0:T(8,128)S(1)} %get-tuple-element.475), channel_id=1, source_target_pairs={{0,16},{1,17},{2,18},{3,19},{4,20},{5,21},{6,22},{7,23},{8,24},{9,... | collective-permute-start | bytes 3145736 | tf_op jit(solution)/shard_map/ppermute | solution.py:39
  570.7 48.1 %collective-permute-start.52 = (f32[512,512]{1,0:T(8,128)S(1)}, f32[512,512]{1,0:T(8,128)S(1)}, u32[]{:S(2)}, u32[]{:S(2)}) collective-permute-start(f32[512,512]{1,0:T(8,128)S(1)} %get-tuple-element.483), channel_id=1, source_target_pairs={{0,16},{1,17},{2,18},{3,19},{4,20},{5,21},{6,22},{7,23},{8,24},{9,... | collective-permute-start | bytes 3145736 | tf_op jit(solution)/shard_map/ppermute | solution.py:39
  586.3 54.4 %collective-permute-start.55 = (f32[512,512]{1,0:T(8,128)S(1)}, f32[512,512]{1,0:T(8,128)S(1)}, u32[]{:S(2)}, u32[]{:S(2)}) collective-permute-start(f32[512,512]{1,0:T(8,128)S(1)} %get-tuple-element.488), channel_id=1, source_target_pairs={{0,16},{1,17},{2,18},{3,19},{4,20},{5,21},{6,22},{7,23},{8,24},{9,... | collective-permute-start | bytes 3145736 | tf_op jit(solution)/shard_map/ppermute | solution.py:39
  (74 other events, 535.4 us)

commit v2 on v1

v2 whole, which is shorter than its diff:
```python
import functools

import jax
import jax.numpy as jnp
from jax import lax
from jax.experimental import pallas as pl
from jax.experimental.pallas import tpu as pltpu
from jax.sharding import PartitionSpec as P

STEP_SIZE = 0.4


def after(value, *earlier):
    return lax.optimization_barrier((value, *earlier))[0]


class Grid:
    def __init__(self, rows, cols):
        self.rows, self.cols = rows, cols
        self.groups = rows // 2
        row_id, col_id = lax.axis_index("row"), lax.axis_index("col")
        self.row_high, self.row_group = row_id // self.groups, row_id % self.groups
        self.col_high = col_id // (cols // 2)
        self.col_group = col_id % (cols // 2) // 2
        self.parity = col_id % 2

    def split(self, row, col):
        half = self.cols // 2
        return row // self.groups, row % self.groups, col // half, col % half // 2, col % 2

    def send(self, value, row_flip, col_flip, chosen=None):
        pairs = []
        for row in range(self.rows):
            for col in range(self.cols):
                if chosen is None or chosen(*self.split(row, col)):
                    target = (row ^ row_flip) * self.cols + (col ^ col_flip)
                    pairs.append((row * self.cols + col, target))
        return lax.ppermute(value, ("row", "col"), pairs)

    def swap_parity(self, value, chosen=None):
        return self.send(value, 0, 1, chosen)

    def swap_col_high(self, value, chosen=None):
        return self.send(value, 0, self.cols // 2, chosen)

    def swap_row_high(self, value, chosen=None):
        return self.send(value, self.rows // 2, 0, chosen)

    def spread_col_group(self, value):
        bit = 1
        while bit < self.groups:
            def holds(rh, rg, ch, cg, e, bit=bit):
                return (rg ^ cg) < bit

            arrived = self.send(value, 0, 2 * bit, holds)
            value = jnp.where((self.row_group ^ self.col_group) & bit != 0, arrived, value)
            bit *= 2
        return value

    def spread_row_group(self, value):
        bit = 1
        while bit < self.groups:
            def holds(rh, rg, ch, cg, e, bit=bit):
                return (rg ^ cg) < bit

            arrived = self.send(value, bit, 0, holds)
            value = jnp.where((self.row_group ^ self.col_group) & bit != 0, arrived, value)
            bit *= 2
        return value


def on_group(rh, rg, ch, cg, e):
    return rg == cg


def off_group(rh, rg, ch, cg, e):
    return rg != cg


def on_pair(rh, rg, ch, cg, e):
    return rg == cg and rh == ch


def triangle_masks(width):
    row = lax.broadcasted_iota(jnp.int32, (width, width), 0)
    col = lax.broadcasted_iota(jnp.int32, (width, width), 1)
    return row, col


def diagonal(blocks):
    row, col = triangle_masks(blocks.shape[-1])
    return jnp.sum(jnp.where((row == col)[None], blocks, 0.0), axis=1)


def halves(value):
    high = value.astype(jnp.bfloat16)
    return high, (value - high.astype(jnp.float32)).astype(jnp.bfloat16)


def beside(high, low):
    return jnp.concatenate((high, low, high), axis=1)


def stack_parts(ref, row, value):
    rows = value.shape[0]
    high, low = halves(value)
    stride = ref.shape[0] // 3
    for part, kept in enumerate((high, high, low)):
        ref[pl.ds(row + part * stride, rows), :] = kept


def dot(left, right):
    return jnp.dot(left, right, preferred_element_type=jnp.float32)


def rotation_kernel(
    flags_ref, first_ref, second_ref, columns_ref, high_ref, low_ref,
    gen, square_ref, gen_parts, in_parts,
):
    width = first_ref.shape[0]
    size = 2 * width
    step = min(width, 256)
    first, second = first_ref[...], second_ref[...]
    first_t, second_t = first.T, second.T
    row, col = triangle_masks(width)
    gen[:width, :width] = jnp.where(row < col, first, jnp.where(row > col, -first_t, 0.0))
    gen[width:, width:] = jnp.where(row < col, second, jnp.where(row > col, -second_t, 0.0))
    gen[width:, :width] = jnp.where(row >= col, first, -second_t)
    gen[:width, width:] = jnp.where(row <= col, -first_t, second)
    for start in range(0, size, step):
        stack_parts(gen_parts, start, gen[start : start + step, :])

    def on_eye(index):
        row = lax.broadcasted_iota(jnp.int32, (step, size), 0) + index * step
        return row == lax.broadcasted_iota(jnp.int32, (step, size), 1)

    def square(index, carry):
        rows = pl.ds(pl.multiple_of(index * step, step), step)
        start = index * step
        high = gen_parts[pl.ds(pl.multiple_of(start, step), step), :]
        low = gen_parts[pl.ds(pl.multiple_of(start + 2 * size, step), step), :]
        product = dot(beside(high, low), gen_parts[...])
        square_ref[rows, :] = product
        value = gen[rows, :] * (1 / 6) + product * (1 / 24)
        value = value + jnp.where(on_eye(index), 0.5, 0.0)
        stack_parts(in_parts, pl.multiple_of(start, step), value)
        return carry

    lax.fori_loop(0, size // step, square, 0)
    swap_rows, swap_cols, chosen = flags_ref[0], flags_ref[1], flags_ref[2]

    def outer(index, carry):
        rows = pl.ds(pl.multiple_of(index * step, step), step)
        product = dot(beside(*halves(square_ref[rows, :])), in_parts[...])
        value = product + gen[rows, :] + jnp.where(on_eye(index), 1.0, 0.0)
        columns_ref[rows, :] = jnp.where(chosen == 0, value[:, :width], value[:, width:])
        turned = value.T
        per_half = width // step
        place = (index // per_half + swap_cols) % 2 * per_half + index % per_half
        cols = pl.ds(pl.multiple_of(place * step, step), step)
        for part in range(2):
            start = pl.multiple_of((part + swap_rows) % 2 * width, width)
            high, low = halves(turned[part * width : (part + 1) * width])
            high_ref[pl.ds(start, width), cols] = high
            low_ref[pl.ds(start, width), cols] = low
        return carry

    lax.fori_loop(0, size // step, outer, 0)


NO_COST = pl.CostEstimate(flops=0, bytes_accessed=0, transcendentals=0)


def rotation_of(first, second, swap_rows, swap_cols, chosen):
    width = first.shape[0]
    size = 2 * width
    whole = pl.BlockSpec(memory_space=pltpu.VMEM)
    flags = jnp.stack([jnp.asarray(flag, jnp.int32) for flag in (swap_rows, swap_cols, chosen)])
    return pl.pallas_call(
        rotation_kernel,
        out_shape=(
            jax.ShapeDtypeStruct((size, width), jnp.float32),
            jax.ShapeDtypeStruct((size, size), jnp.bfloat16),
            jax.ShapeDtypeStruct((size, size), jnp.bfloat16),
        ),
        in_specs=[pl.BlockSpec(memory_space=pltpu.SMEM), whole, whole],
        out_specs=(whole, whole, whole),
        scratch_shapes=[pltpu.VMEM((size, size), jnp.float32)] * 2
        + [pltpu.VMEM((3 * size, size), jnp.bfloat16)] * 2,
        compiler_params=pltpu.CompilerParams(vmem_limit_bytes=48 * 2**20),
        cost_estimate=NO_COST,
    )(flags, first, second)


def rotate_kernel(spans, per_half, *refs):
    step = pl.program_id(0)
    at = sum(count for side in spans for _, _, count in side)
    weights, turn_high, turn_low = refs[at : at + 2], refs[at + 2], refs[at + 3]
    outs = refs[at + 4 : -3]
    weight_parts, mid_parts = refs[-3:-1], refs[-1]
    block = turn_high.shape[0]
    first_part = 2 * per_half

    @pl.when(step == 0)
    def _():
        for side in range(2):
            stack_parts(weight_parts[side], 0, weights[side][...])

    for now in range(first_part):

        @pl.when(step == now)
        def _(now=now):
            total, at = None, 0
            for side in range(2):
                for first, steps, count in spans[side]:
                    if first <= now < first + steps:
                        value = refs[at][...]
                        for ref in refs[at + 1 : at + count]:
                            value = value + ref[...]
                        part = dot(beside(*halves(value)), weight_parts[side][...])
                        total = part if total is None else total + part
                    at += count
            stack_parts(mid_parts, now * block, total)

    @pl.when(step >= first_part)
    def _():
        product = dot(beside(turn_high[...], turn_low[...]), mid_parts[...])
        for half, out in enumerate(outs):

            @pl.when((step - first_part) // per_half == half)
            def _(out=out):
                out[...] = product


def block_rows(width):
    return min(width, 256)


def rotate(near, far, near_weights, far_weights, turn):
    width = near_weights.shape[0]
    size = 2 * width
    block = block_rows(width)
    per_half = width // block
    first_part = 2 * per_half
    turn_high, turn_low = turn
    out_halves = turn_high.shape[0] // width
    arrays, specs, spans = [], [], []
    for side in (near, far):
        span, first = [], 0
        for piece in side:
            steps = piece[0].shape[0] // block
            span.append((first, steps, len(piece)))

            def place(step, first=first, steps=steps):
                return jnp.clip(step - first, 0, steps - 1), 0

            for array in piece:
                arrays.append(array)
                specs.append(pl.BlockSpec((block, width), place))
            first += steps
        spans.append(tuple(span))
    fixed = pl.BlockSpec((width, width), lambda step: (0, 0))
    turning = pl.BlockSpec(
        (block, size),
        lambda step: (jnp.clip(step - first_part, 0, out_halves * per_half - 1), 0),
    )
    outs = [
        pl.BlockSpec(
            (block, width),
            lambda step, half=half: (
                jnp.clip(step - first_part - half * per_half, 0, per_half - 1),
                0,
            ),
        )
        for half in range(out_halves)
    ]
    return pl.pallas_call(
        functools.partial(rotate_kernel, tuple(spans), per_half),
        grid=(first_part + out_halves * per_half,),
        out_shape=[jax.ShapeDtypeStruct((width, width), jnp.float32)] * out_halves,
        in_specs=[*specs, fixed, fixed, turning, turning],
        out_specs=outs,
        scratch_shapes=[pltpu.VMEM((3 * width, width), jnp.bfloat16)] * 2
        + [pltpu.VMEM((3 * size, width), jnp.bfloat16)],
        compiler_params=pltpu.CompilerParams(vmem_limit_bytes=40 * 2**20),
        cost_estimate=NO_COST,
    )(*arrays, near_weights, far_weights, turn_high, turn_low)


def rows_of(value, which, width):
    return lax.dynamic_slice_in_dim(value, which * width, width, value.ndim - 2)


def first_generator(grid, tiles, own_centres, other_centres):
    width = tiles.shape[2]
    is_first = grid.parity == 0
    centres = jnp.where(
        is_first,
        jnp.concatenate((own_centres, other_centres), axis=1),
        jnp.concatenate((other_centres, own_centres), axis=1),
    )
    generator = STEP_SIZE * jnp.sum(
        tiles * (own_centres[:, None, :] - centres[:, :, None]), axis=0
    )
    row, col = triangle_masks(width)
    top, bottom = generator[:width], generator[width:]
    return jnp.where(
        is_first, jnp.where(row < col, top, bottom), jnp.where(row < col, bottom, top)
    )


def second_generator(grid, blocks, own_centres, row_centres, col_centres):
    same = grid.row_high == grid.col_high
    row_centres = jnp.where(same, own_centres, row_centres)
    col_centres = jnp.where(same, own_centres, col_centres)
    return STEP_SIZE * jnp.sum(
        blocks * (col_centres[:, None, :] - row_centres[:, :, None]), axis=0
    )


def local(positions):
    grid = Grid(lax.axis_size("row"), lax.axis_size("col"))
    count, height, width = positions.shape
    half = count // 2
    block = block_rows(width)
    early, late = list(range(half)), list(range(half, count))
    is_first = grid.parity == 0
    is_low = grid.row_high == 0
    is_left = grid.col_high == 0
    same = grid.row_high == grid.col_high
    groups = grid.groups > 1

    def weights_of(columns, which):
        return rows_of(columns, which, width), rows_of(columns, 1 - which, width)

    raw_queue = [(k, row) for k in early for row in range(0, height, block)]
    raw = {k: [] for k in early}

    def send_raw(pieces, token):
        arrived = []
        for k, row in raw_queue[:pieces]:
            rows = after(positions[k, row : row + block], token)
            arrived.append(grid.swap_col_high(rows))
            raw[k].append(arrived[-1])
        del raw_queue[:pieces]
        return arrived

    urgent, rest = [None] * count, {}

    def send_urgent(k, *tokens):
        urgent[k] = grid.swap_parity(after(positions[k], *tokens), on_group)

    def send_rest(k, *tokens):
        rest[k] = grid.swap_parity(after(positions[k], *tokens), off_group) if groups else None

    def rests(k):
        return [rest[k]] if groups else []

    own_centres = diagonal(rows_of(positions, grid.parity, width))
    other_centres = grid.swap_parity(own_centres, on_pair)
    packed = first_generator(grid, positions, own_centres, other_centres)
    packed = jnp.where(same, packed, grid.swap_col_high(packed, on_pair))
    send_urgent(0, packed)
    pieces = []
    packed = grid.spread_col_group(packed)
    pieces_next = send_raw(1, packed)
    packed = after(packed, urgent[0], *pieces)
    other = after(grid.swap_parity(packed), *pieces_next)
    send_urgent(1, other)
    pieces = send_raw(1, other)
    columns, *turn = rotation_of(
        jnp.where(is_first, packed, other),
        jnp.where(is_first, other, packed),
        grid.row_high,
        0,
        grid.parity,
    )
    columns = after(columns, urgent[1], *pieces)
    send_urgent(2, columns)
    pieces = send_raw(2, columns)
    arrived = grid.swap_row_high(columns, on_group)
    columns = jnp.stack((jnp.where(same, columns, arrived), jnp.where(same, arrived, columns)))
    columns = after(columns, *pieces, urgent[2])
    send_urgent(3, columns)
    send_rest(late[0], columns)
    send_rest(late[1], columns)
    pieces = send_raw(2, columns)
    columns = grid.spread_row_group(columns)
    near_weights = weights_of(columns[0], grid.parity)
    far_weights = weights_of(columns[1], grid.parity)

    block_turn = [rows_of(part, grid.parity ^ grid.row_high, width) for part in turn]
    blocks = jnp.stack(
        [
            rotate([[positions[k]]], [[urgent[k]]], *near_weights, block_turn)[0]
            for k in range(count)
        ]
    )
    blocks = after(blocks, *pieces, *rests(late[0]))
    pieces = send_raw(len(raw_queue), blocks)
    send_rest(early[0], blocks)
    own_centres = diagonal(blocks)
    row_centres = grid.swap_col_high(own_centres, on_pair)
    col_centres = grid.swap_row_high(own_centres, on_pair)
    own = second_generator(grid, blocks, own_centres, row_centres, col_centres)
    other = grid.swap_row_high(own, lambda rh, rg, ch, cg, e: rg == cg and rh != e)

    near, sent, moved = {}, {}, {}

    def first_round(k, token):
        partner = [urgent[k], *rests(k)]
        tile = after(positions[k], token)
        near[k], sent[k] = rotate([[tile]], [partner], *near_weights, turn)

    def move(k, token):
        moved[k] = grid.swap_row_high(after(sent[k], token))

    away = grid.send(own, grid.rows // 2, 1, lambda rh, rg, ch, cg, e: rg == cg and rh != e)
    beside_own = grid.swap_parity(own, lambda rh, rg, ch, cg, e: rg == cg and rh == e)
    at_home = grid.parity == grid.row_high
    mine, theirs = jnp.where(at_home, own, beside_own), jnp.where(at_home, other, away)
    first_round(late[0], blocks)
    move(late[0], own)
    first_round(late[1], own)
    top, bottom = jnp.where(is_low, mine, theirs), jnp.where(is_low, theirs, mine)
    row, col = triangle_masks(width)
    packed = jnp.where(
        is_left, jnp.where(row < col, top, bottom), jnp.where(row < col, bottom, top)
    )
    packed = after(packed, near[late[1]], moved[late[0]], *pieces)
    packed = after(packed, *rests(early[0]))
    other = grid.swap_col_high(packed, on_group)
    move(late[1], packed)
    first_round(early[0], packed)
    move(early[0], packed)
    send_rest(early[1], packed)
    far_queue = [(k, part) for k in early for part in range(2)]
    far_partner = {k: [] for k in early}

    def send_far(token):
        k, part = far_queue.pop(0)
        pieces = raw[k][part * len(raw[k]) // 2 : (part + 1) * len(raw[k]) // 2]
        rows = jnp.concatenate(pieces, axis=0)
        far_partner[k].append(grid.swap_parity(after(rows, token)))
        return far_partner[k][-1]

    late_far = {k: [] for k in late}

    def send_late(k, part, token):
        late_far[k].append(grid.swap_col_high(after(part, token)))
        return late_far[k][-1]

    middle = width // 2
    pieces = [send_late(late[0], near[late[0]][:middle], packed)]
    partner = send_far(packed)
    both = jnp.stack((jnp.where(is_left, packed, other), jnp.where(is_left, other, packed)))
    both = after(both, moved[late[1]], moved[early[0]], *pieces, partner, *rests(early[1]))
    parts = (near[late[0]][middle:], moved[late[0]][:middle])
    late_half = send_late(late[0], jnp.concatenate(parts, axis=0), both)
    partner = [send_far(both), send_far(both)]
    first_round(early[1], both)
    move(early[1], both)
    both = grid.spread_col_group(both)
    both = after(both, moved[early[1]], *partner)
    far_near, far_sent, far_moved = {}, {}, {}

    def far_round(k, token):
        tiles = [[after(part, token)] for part in raw[k]]
        others = [[part] for part in far_partner[k]]
        far_near[k], far_sent[k] = rotate(tiles, others, *far_weights, turn)

    late_quarter = send_late(late[0], moved[late[0]][middle:], both)
    partner = send_far(both)
    columns, *second_turn = rotation_of(
        both[0], both[1], grid.row_high, grid.row_high, grid.col_high
    )
    columns = after(columns, late_half, partner)
    far_round(early[0], columns)
    far_round(early[1], columns)
    arrived = grid.swap_row_high(columns, lambda rh, rg, ch, cg, e: rg == cg and rh == e)
    columns = jnp.where(grid.row_high == grid.parity, columns, arrived)
    far_moved[early[0]] = grid.swap_row_high(far_sent[early[0]])
    columns = after(columns, far_near[early[0]], far_near[early[1]], late_quarter)
    far_moved[early[1]] = grid.swap_row_high(after(far_sent[early[1]], columns))
    for part in (near[late[1]], moved[late[1]]):
        send_late(late[1], part, columns)
    weights = weights_of(grid.spread_row_group(columns), grid.col_high)
    weights = [after(weight, far_moved[early[0]]) for weight in weights]

    outputs = [None] * count
    before = [late_far[late[1]][0]]
    for k in [*early, *late]:
        mine = [[near[k]], [moved[k]]]
        theirs = [[far_near[k]], [far_moved[k]]] if k in early else [[part] for part in late_far[k]]
        kept, leaving = rotate(mine, theirs, *weights, second_turn)
        arrived = grid.swap_row_high(leaving)
        if k == late[0]:
            before.append(arrived)
        weights = [after(weight, kept, *before) for weight in weights]
        before = [arrived]
        outputs[k] = [jnp.where(is_low, kept, arrived), jnp.where(is_low, arrived, kept)]
    return jnp.stack([part for pair in outputs for part in pair]).reshape(positions.shape)


def solution(mesh):
    spec = P(None, "row", "col")
    return jax.shard_map(local, mesh=mesh, in_specs=(spec,), out_specs=spec, check_vma=False)
```

time: 656 us -> 628 us (0.957)
  the two profiles are of different devices: /device:TPU:9 before, /device:TPU:31 now
where the time goes in v2:
time: 628 us; the launch traced here: 618 us
  waiting for transfers between devices  250 us (40%)
  Pallas kernels  176 us (28%)
  starting transfers between devices  114 us (18%)
  other arithmetic  41.5 us (7%)
  local copies, waits for them, and re-layouts  35 us (6%)
    ppermute x50, waiting for transfers between devices, send(): return lax.ppermute(value, ('row', 'col'), pairs)  250 us
    pallas_call x14, Pallas kernels, rotate(): pl.pallas_call(functools.partial(rotate_kernel, tuple(spans), per_half),...  135 us
    ppermute x50, starting transfers between devices, send(): return lax.ppermute(value, ('row', 'col'), pairs)  114 us
    pallas_call x2, Pallas kernels, rotation_of(): pl.pallas_call(rotation_kernel, out_shape=(jax.ShapeDtypeStruct((size, wi...  40.2 us
    unnamed x146, local copies, waits for them, and re-layouts  16.2 us
  transfers between devices with their start and end apart: 50, of which 28 were waited for; matrix products, arithmetic and copies ran while one was open for 8% of the time, Pallas kernels for 27%

profile of v2, /device:TPU:31, one launch (start us, length us, event | category | flops | bytes accessed | tf_op | source)
XLA Modules:
  0.0 618.3 jit_solution(16826369560766951532)
XLA Ops:
  0.1 2.8 select_reduce_fusion.1
  7.3 4.1 multiply_reduce_fusion
  13.2 2.3 collective-permute-start.1
  15.5 6.8 %slice_bitcast_fusion.1 = (f32[1024,512]{1,0:T(8,128)}, f32[1024,512]{1,0:T(8,128)}, f32[1024,512]{1,0:T(8,128)S(1)}, f32[1024,512]{1,0:T(8,128)}) fusion(f32[4,1024,512]{2,1,0:T(8,128)} %param.1), kind=kLoop, calls=%fused_computation.8 | loop fusion | bytes 16777216 | tf_op jit(solution)/shard_map/squeeze | solution.py:351
  22.2 4.0 collective-permute-done.1
  28.8 2.3 collective-permute-start.3
  31.1 10.7 %collective-permute-done.3 = f32[512,512]{1,0:T(8,128)} collective-permute-done((f32[512,512]{1,0:T(8,128)S(1)}, f32[512,512]{1,0:T(8,128)}, u32[]{:S(2)}, u32[]{:S(2)}) %collective-permute-start.3) | collective-permute-done | bytes 1048608 | tf_op jit(solution)/shard_map/ppermute | solution.py:38
  42.1 12.0 %collective-permute-done.2.refs_1_ = f32[1024,512]{1,0:T(8,128)} collective-permute-done((f32[1024,512]{1,0:T(8,128)}, f32[1024,512]{1,0:T(8,128)}, u32[]{:S(2)}, u32[]{:S(2)}) %collective-permute-start.2) | collective-permute-done | bytes 2097184 | tf_op jit(solution)/shard_map/ppermute | solution.py:38
  54.3 4.1 slice_bitcast_fusion.6
  58.4 4.2 collective-permute-start.5
  62.5 10.5 %collective-permute-done.5.refs_0_ = f32[256,512]{1,0:T(8,128)S(1)} collective-permute-done((f32[256,512]{1,0:T(8,128)S(1)}, f32[256,512]{1,0:T(8,128)S(1)}, u32[]{:S(2)}, u32[]{:S(2)}) %collective-permute-start.5) | collective-permute-done | bytes 524320 | tf_op jit(solution)/shard_map/ppermute | solution.py:38
  77.1 3.5 collective-permute-start.7
  81.0 19.8 %shard_map.17 = (f32[1024,512]{1,0:T(8,128)S(1)}, bf16[1024,1024]{1,0:T(8,128)(2,1)}, bf16[1024,1024]{1,0:T(8,128)(2,1)}) custom-call(s32[3]{0:T(128)S(1)} %pad_add_fusion.flags_ref, f32[512,512]{1,0:T(8,128)S(1)} %get-tuple-element.204.first_ref, f32[512,512]{1,0:T(8,128)S(1)} %get-tuple-element.203.second_ref), custom_call_target="tpu_custom_call" | custom-call | tf_op jit(solution)/shard_map/pallas_call | solution.py:179
  100.7 3.4 collective-permute-done.7.refs_1_
  104.2 29.8 %collective-permute-start.8 = (f32[1024,512]{1,0:T(8,128)S(1)}, f32[1024,512]{1,0:T(8,128)S(1)}, u32[]{:S(2)}, u32[]{:S(2)}) collective-permute-start(f32[1024,512]{1,0:T(8,128)S(1)} %get-tuple-element.98), channel_id=1, source_target_pairs={{0,16},{1,17},{4,20},{5,21},{10,26},{11,27},{14,30},{15,31},{16,0}... | collective-permute-start | bytes 6291464 | tf_op jit(solution)/shard_map/ppermute | solution.py:38
  133.9 3.8 collective-permute-start.11
  137.8 2.4 collective-permute-start.9
  140.2 17.5 %collective-permute-done.8 = f32[1024,512]{1,0:T(8,128)S(1)} collective-permute-done((f32[1024,512]{1,0:T(8,128)S(1)}, f32[1024,512]{1,0:T(8,128)S(1)}, u32[]{:S(2)}, u32[]{:S(2)}) %collective-permute-start.8) | collective-permute-done | bytes 2097184 | tf_op jit(solution)/shard_map/ppermute | solution.py:38
  158.4 2.5 pad_maximum_fusion
  160.9 8.2 %collective-permute-done.10.refs_3_ = f32[256,512]{1,0:T(8,128)S(1)} collective-permute-done((f32[256,512]{1,0:T(8,128)}, f32[256,512]{1,0:T(8,128)S(1)}, u32[]{:S(2)}, u32[]{:S(2)}) %collective-permute-start.10) | collective-permute-done | bytes 524320 | tf_op jit(solution)/shard_map/ppermute | solution.py:38
  169.1 5.4 collective-permute-done.9.refs_2_
  174.6 2.9 collective-permute-done.11.refs_1_
  178.8 3.3 collective-permute-start.12
  182.1 4.1 collective-permute-start.13
  190.9 2.3 collective-permute-start.15
  193.2 3.2 broadcast_select_fusion
  198.5 8.0 %shard_map.18 = f32[512,512]{1,0:T(8,128)S(1)} custom-call(f32[1024,512]{1,0:T(8,128)} %get-tuple-element.120.refs_0_, f32[1024,512]{1,0:T(8,128)} %collective-permute-done.2.refs_1_, f32[512,512]{1,0:T(8,128)S(1)} %get-tuple-element.202.refs_2_.refs_3_, f32[512,512]{1,0:T(8,128)S(1)} %get-tuple-element.201.refs_3_.refs_4_, ...), custom_call_target="tpu_custom_call" | custom-call | tf_op jit(solution)/shard_map/pallas_call | solution.py:277
  206.5 6.1 shard_map.19
  212.7 7.2 %shard_map.20 = f32[512,512]{1,0:T(8,128)S(1)} custom-call(f32[1024,512]{1,0:T(8,128)} %get-tuple-element.112.refs_0_, f32[1024,512]{1,0:T(8,128)S(1)} %copy-done.13, f32[512,512]{1,0:T(8,128)S(1)} %get-tuple-element.202.refs_2_.refs_3_, f32[512,512]{1,0:T(8,128)S(1)} %get-tuple-element.201.refs_3_.refs_4_, ...), custom_call_target="tpu_custom_call" | custom-call | tf_op jit(solution)/shard_map/pallas_call | solution.py:277
  219.9 9.0 %collective-permute-done.13.refs_1_ = f32[1024,512]{1,0:T(8,128)} collective-permute-done((f32[1024,512]{1,0:T(8,128)}, f32[1024,512]{1,0:T(8,128)}, u32[]{:S(2)}, u32[]{:S(2)}) %collective-permute-start.13) | collective-permute-done | bytes 2097184 | tf_op jit(solution)/shard_map/ppermute | solution.py:38
  228.9 17.7 %shard_map.21 = f32[512,512]{1,0:T(8,128)S(1)} custom-call(f32[1024,512]{1,0:T(8,128)} %get-tuple-element.110.refs_0_, f32[1024,512]{1,0:T(8,128)} %collective-permute-done.13.refs_1_, f32[512,512]{1,0:T(8,128)S(1)} %get-tuple-element.202.refs_2_.refs_3_, f32[512,512]{1,0:T(8,128)S(1)} %get-tuple-element.201.refs_3_.refs_4_, ...), custom_call_target="tpu_custom_call" | custom-call | tf_op jit(solution)/shard_map/pallas_call | solution.py:277
  255.1 4.3 collective-permute-start.19
  262.4 10.9 %shard_map.23 = (f32[512,512]{1,0:T(8,128)S(1)}, f32[512,512]{1,0:T(8,128)}) custom-call(f32[1024,512]{1,0:T(8,128)} %get-tuple-element.112.refs_0_, f32[1024,512]{1,0:T(8,128)S(1)} %copy-done.13, f32[1024,512]{1,0:T(8,128)} %collective-permute-done.16.refs_2_, f32[512,512]{1,0:T(8,128)S(1)} %get-tuple-element.202.refs_2_.refs_3_, ...), custom_call_target="tpu_custom_call" | custom-call | tf_op jit(solution)/shard_map/pallas_call | solution.py:277
  275.6 4.4 collective-permute-start.23
  281.0 4.3 collective-permute-done.20
  285.3 2.4 collective-permute-start.25
  290.6 10.1 %shard_map.22 = (f32[512,512]{1,0:T(8,128)S(1)}, f32[512,512]{1,0:T(8,128)S(1)}) custom-call(f32[1024,512]{1,0:T(8,128)} %get-tuple-element.110.refs_0_, f32[1024,512]{1,0:T(8,128)} %collective-permute-done.13.refs_1_, f32[1024,512]{1,0:T(8,128)S(1)} %copy-done.36, f32[512,512]{1,0:T(8,128)S(1)} %copy-done.3, ...), custom_call_target="tpu_custom_call" | custom-call | tf_op jit(solution)/shard_map/pallas_call | solution.py:277
  303.6 5.6 collective-permute-done.25.refs_3_
  314.0 10.7 %shard_map.24 = (f32[512,512]{1,0:T(8,128)S(1)}, f32[512,512]{1,0:T(8,128)S(1)}) custom-call(f32[1024,512]{1,0:T(8,128)} %get-tuple-element.120.refs_0_, f32[1024,512]{1,0:T(8,128)} %collective-permute-done.2.refs_1_, f32[1024,512]{1,0:T(8,128)} %collective-permute-done.26.refs_2_, f32[512,512]{1,0:T(8,128)S(1)} %copy-done.3, ...), custom_call_target="tpu_custom_call" | custom-call | tf_op jit(solution)/shard_map/pallas_call | solution.py:277
  325.4 23.5 %collective-permute-done.28 = f32[512,512]{1,0:T(8,128)S(1)} collective-permute-done((f32[512,512]{1,0:T(8,128)S(1)}, f32[512,512]{1,0:T(8,128)S(1)}, u32[]{:S(2)}, u32[]{:S(2)}) %collective-permute-start.28) | collective-permute-done | bytes 1048608 | tf_op jit(solution)/shard_map/ppermute | solution.py:38
  351.7 12.2 %collective-permute-done.30.refs_2_ = f32[256,512]{1,0:T(8,128)S(1)} collective-permute-done((f32[256,512]{1,0:T(8,128)S(1)}, f32[256,512]{1,0:T(8,128)S(1)}, u32[]{:S(2)}, u32[]{:S(2)}) %collective-permute-start.30) | collective-permute-done | bytes 524320 | tf_op jit(solution)/shard_map/ppermute | solution.py:38
  368.1 9.4 %shard_map.25 = (f32[512,512]{1,0:T(8,128)S(1)}, f32[512,512]{1,0:T(8,128)S(1)}) custom-call(f32[1024,512]{1,0:T(8,128)S(1)} %copy-done.8, f32[1024,512]{1,0:T(8,128)S(1)} %copy-done.11, f32[1024,512]{1,0:T(8,128)S(1)} %collective-permute-done.32.refs_2_, f32[512,512]{1,0:T(8,128)S(1)} %copy-done.3, f32[512,512]{1,0:T(8,128)S(1)} %get-tuple-element.201.refs_3_.refs_4_, ...), custom_call_target="tpu_custom_call" | custom-call | tf_op jit(solution)/shard_map/pallas_call | solution.py:277
  383.0 16.5 %collective-permute-done.33 = f32[2,512,512]{2,1,0:T(8,128)S(1)} collective-permute-done((f32[2,512,512]{2,1,0:T(8,128)S(1)}, f32[2,512,512]{2,1,0:T(8,128)S(1)}, u32[]{:S(2)}, u32[]{:S(2)}) %collective-permute-start.33) | collective-permute-done | bytes 2097184 | tf_op jit(solution)/shard_map/ppermute | solution.py:38
  400.0 3.0 collective-permute-done.35.refs_5_
  404.3 20.4 %shard_map.26 = (f32[1024,512]{1,0:T(8,128)}, bf16[1024,1024]{1,0:T(8,128)(2,1)}, bf16[1024,1024]{1,0:T(8,128)(2,1)}) custom-call(s32[3]{0:T(128)S(1)} %pad_add_fusion.1.flags_ref, f32[512,512]{1,0:T(8,128)S(1)} %get-tuple-element.198.first_ref, f32[512,512]{1,0:T(8,128)S(1)} %get-tuple-element.197.second_ref), custom_call_target="tpu_custom_call" | custom-call | tf_op jit(solution)/shard_map/pallas_call | solution.py:179
  427.8 5.1 collective-permute-start.40
  437.0 9.8 %shard_map.28 = (f32[512,512]{1,0:T(8,128)S(1)}, f32[512,512]{1,0:T(8,128)S(1)}) custom-call(f32[256,512]{1,0:T(8,128)S(1)} %copy-done.31, f32[256,512]{1,0:T(8,128)S(1)} %copy-done.34, f32[256,512]{1,0:T(8,128)} %collective-permute-done.24.refs_2_, f32[256,512]{1,0:T(8,128)} %collective-permute-done.25.refs_3_, f32[512,512]{1,0:T(8,128)S(1)} %copy-done.56, ...), custom_call_target="tpu_custom_call" | custom-call | tf_op jit(solution)/shard_map/pallas_call | solution.py:277
  447.9 9.3 %shard_map.27 = (f32[512,512]{1,0:T(8,128)S(1)}, f32[512,512]{1,0:T(8,128)}) custom-call(f32[256,512]{1,0:T(8,128)S(1)} %copy-done.19, f32[256,512]{1,0:T(8,128)S(1)} %copy-done.22, f32[256,512]{1,0:T(8,128)S(1)} %copy-done.28, f32[256,512]{1,0:T(8,128)S(1)} %copy-done.25, f32[512,512]{1,0:T(8,128)S(1)} %copy-done.50, f32[512,512]{1,0:T(8,128)S(1)} %copy-done.54, ...), custom_call_target="tpu_custom_call" | custom-call | tf_op jit(solution)/shard_map/pallas_call | solution.py:277
  457.2 3.8 broadcast_select_fusion.1
  461.8 2.6 collective-permute-start.42
  465.5 2.6 collective-permute-start.45
  470.7 19.1 %collective-permute-done.39.refs_3_ = f32[512,512]{1,0:T(8,128)} collective-permute-done((f32[512,512]{1,0:T(8,128)}, f32[512,512]{1,0:T(8,128)}, u32[]{:S(2)}, u32[]{:S(2)}) %collective-permute-start.39) | collective-permute-done | bytes 1048608 | tf_op jit(solution)/shard_map/ppermute | solution.py:38
  489.9 9.8 %shard_map.29 = (f32[512,512]{1,0:T(8,128)S(1)}, f32[512,512]{1,0:T(8,128)S(1)}) custom-call(f32[512,512]{1,0:T(8,128)S(1)} %copy-done.42, f32[512,512]{1,0:T(8,128)S(1)} %copy-done.44, f32[512,512]{1,0:T(8,128)S(1)} %copy-done.58, f32[512,512]{1,0:T(8,128)} %collective-permute-done.39.refs_3_, f32[512,512]{1,0:T(8,128)S(1)} %get-tuple-element.173.refs_4_.refs_5_, ...), custom_call_target="tpu_custom_call" | custom-call | tf_op jit(solution)/shard_map/pallas_call | solution.py:277
  500.9 8.3 %collective-permute-done.45.refs_2_ = f32[512,512]{1,0:T(8,128)S(1)} collective-permute-done((f32[512,512]{1,0:T(8,128)S(1)}, f32[512,512]{1,0:T(8,128)S(1)}, u32[]{:S(2)}, u32[]{:S(2)}) %collective-permute-start.45) | collective-permute-done | bytes 1048608 | tf_op jit(solution)/shard_map/ppermute | solution.py:38
  509.2 3.1 collective-permute-done.44.refs_3_
  512.4 8.3 %shard_map.30 = (f32[512,512]{1,0:T(8,128)S(1)}, f32[512,512]{1,0:T(8,128)S(1)}) custom-call(f32[512,512]{1,0:T(8,128)S(1)} %copy-done.46, f32[512,512]{1,0:T(8,128)S(1)} %copy-done.48, f32[512,512]{1,0:T(8,128)S(1)} %copy-done.52, f32[512,512]{1,0:T(8,128)S(1)} %collective-permute-done.44.refs_3_, f32[512,512]{1,0:T(8,128)S(1)} %get-tuple-element.173.refs_4_.refs_5_, ...), custom_call_target="tpu_custom_call" | custom-call | tf_op jit(solution)/shard_map/pallas_call | solution.py:277
  521.9 12.9 %collective-permute-done.43 = f32[512,512]{1,0:T(8,128)S(1)} collective-permute-done((f32[512,512]{1,0:T(8,128)S(1)}, f32[512,512]{1,0:T(8,128)S(1)}, u32[]{:S(2)}, u32[]{:S(2)}) %collective-permute-start.43) | collective-permute-done | bytes 1048608 | tf_op jit(solution)/shard_map/ppermute | solution.py:38
  534.8 9.5 %shard_map.31 = (f32[512,512]{1,0:T(8,128)S(1)}, f32[512,512]{1,0:T(8,128)S(1)}) custom-call(f32[512,512]{1,0:T(8,128)S(1)} %copy-done.16, f32[512,512]{1,0:T(8,128)} %collective-permute-done.23.refs_1_, f32[256,512]{1,0:T(8,128)S(1)} %copy-done.62, f32[512,512]{1,0:T(8,128)S(1)} %collective-permute-done.37.refs_3_, f32[256,512]{1,0:T(8,128)S(1)} %copy-done.64, ...), custom_call_target="tpu_custom_call" | custom-call | tf_op jit(solution)/shard_map/pallas_call | solution.py:277
  545.5 2.6 collective-permute-start.48
  550.5 6.8 %collective-permute-done.46 = f32[512,512]{1,0:T(8,128)S(1)} collective-permute-done((f32[512,512]{1,0:T(8,128)S(1)}, f32[512,512]{1,0:T(8,128)S(1)}, u32[]{:S(2)}, u32[]{:S(2)}) %collective-permute-start.46) | collective-permute-done | bytes 1048608 | tf_op jit(solution)/shard_map/ppermute | solution.py:38
  557.3 20.3 %collective-permute-done.47 = f32[512,512]{1,0:T(8,128)S(1)} collective-permute-done((f32[512,512]{1,0:T(8,128)S(1)}, f32[512,512]{1,0:T(8,128)S(1)}, u32[]{:S(2)}, u32[]{:S(2)}) %collective-permute-start.47) | collective-permute-done | bytes 1048608 | tf_op jit(solution)/shard_map/ppermute | solution.py:38
  577.6 4.4 collective-permute-done.48.refs_3_
  582.0 8.5 %shard_map.32 = (f32[512,512]{1,0:T(8,128)S(1)}, f32[512,512]{1,0:T(8,128)S(1)}) custom-call(f32[512,512]{1,0:T(8,128)S(1)} %copy-done.38, f32[512,512]{1,0:T(8,128)S(1)} %copy-done.40, f32[512,512]{1,0:T(8,128)S(1)} %collective-permute-done.45.refs_2_, f32[512,512]{1,0:T(8,128)S(1)} %collective-permute-done.48.refs_3_, ...), custom_call_target="tpu_custom_call" | custom-call | tf_op jit(solution)/shard_map/pallas_call | solution.py:277
  595.4 20.1 %collective-permute-done.49 = f32[512,512]{1,0:T(8,128)S(1)} collective-permute-done((f32[512,512]{1,0:T(8,128)S(1)}, f32[512,512]{1,0:T(8,128)S(1)}, u32[]{:S(2)}, u32[]{:S(2)}) %collective-permute-start.49) | collective-permute-done | bytes 1048608 | tf_op jit(solution)/shard_map/ppermute | solution.py:38
  (246 shorter events, 87.9 us)
Async XLA Ops:
  2.9 4.4 collective-permute-start
  13.2 13.1 %collective-permute-start.1 = (f32[512,512]{1,0:T(8,128)S(1)}, f32[512,512]{1,0:T(8,128)}, u32[]{:S(2)}, u32[]{:S(2)}) collective-permute-start(f32[512,512]{1,0:T(8,128)S(1)} %select_select_fusion.1), channel_id=1, source_target_pairs={{0,4},{1,5},{10,14},{11,15},{20,16},{21,17},{30,26},{31,27}} | collective-permute-start | bytes 3145736 | tf_op jit(solution)/shard_map/ppermute | solution.py:38
  22.2 52.6 %copy-start.6 = (f32[1024,512]{1,0:T(8,128)}, f32[1024,512]{1,0:T(8,128)S(1)}, u32[]{:S(2)}) copy-start(f32[1024,512]{1,0:T(8,128)S(1)} %get-tuple-element.131.refs_0_) | copy-start | bytes 6291460
  26.6 27.4 %collective-permute-start.2 = (f32[1024,512]{1,0:T(8,128)}, f32[1024,512]{1,0:T(8,128)}, u32[]{:S(2)}, u32[]{:S(2)}) collective-permute-start(f32[1024,512]{1,0:T(8,128)} %get-tuple-element.120.refs_0_), channel_id=1, source_target_pairs={{0,1},{1,0},{4,5},{5,4},{10,11},{11,10},{14,15},{15,14},{16,17},{1... | collective-permute-start | bytes 6291464 | tf_op jit(solution)/shard_map/ppermute | solution.py:38
  28.8 13.0 %collective-permute-start.3 = (f32[512,512]{1,0:T(8,128)S(1)}, f32[512,512]{1,0:T(8,128)}, u32[]{:S(2)}, u32[]{:S(2)}) collective-permute-start(f32[512,512]{1,0:T(8,128)S(1)} %broadcast_select_fusion.7), channel_id=1, source_target_pairs={{0,2},{1,3},{4,6},{5,7},{10,8},{11,9},{14,12},{15,13},{16,18},{17,... | collective-permute-start | bytes 3145736 | tf_op jit(solution)/shard_map/ppermute | solution.py:38
  54.0 20.8 %collective-permute-start.4 = (f32[512,512]{1,0:T(8,128)S(1)}, f32[512,512]{1,0:T(8,128)S(1)}, u32[]{:S(2)}, u32[]{:S(2)}) collective-permute-start(f32[512,512]{1,0:T(8,128)S(1)} %broadcast_select_fusion.4), channel_id=1, source_target_pairs={{0,1},{1,0},{2,3},{3,2},{4,5},{5,4},{6,7},{7,6},{8,9},{9,8},{10,11... | collective-permute-start | bytes 3145736 | tf_op jit(solution)/shard_map/ppermute | solution.py:38
  58.4 14.7 %collective-permute-start.5 = (f32[256,512]{1,0:T(8,128)S(1)}, f32[256,512]{1,0:T(8,128)S(1)}, u32[]{:S(2)}, u32[]{:S(2)}) collective-permute-start(f32[256,512]{1,0:T(8,128)S(1)} %get-tuple-element.93), channel_id=1, source_target_pairs={{0,4},{1,5},{2,6},{3,7},{4,0},{5,1},{6,2},{7,3},{8,12},{9,13},{10,... | collective-permute-start | bytes 1572872 | tf_op jit(solution)/shard_map/ppermute | solution.py:38
  74.9 29.3 %collective-permute-start.6 = (f32[1024,512]{1,0:T(8,128)S(1)}, f32[1024,512]{1,0:T(8,128)S(1)}, u32[]{:S(2)}, u32[]{:S(2)}) collective-permute-start(f32[1024,512]{1,0:T(8,128)S(1)} %get-tuple-element.131.refs_0_), channel_id=1, source_target_pairs={{0,1},{1,0},{4,5},{5,4},{10,11},{11,10},{14,15},{15,14},{16,17},{1... | collective-permute-start | bytes 6291464 | tf_op jit(solution)/shard_map/ppermute | solution.py:38
  77.1 27.0 %collective-permute-start.7 = (f32[256,512]{1,0:T(8,128)S(1)}, f32[256,512]{1,0:T(8,128)S(1)}, u32[]{:S(2)}, u32[]{:S(2)}) collective-permute-start(f32[256,512]{1,0:T(8,128)S(1)} %get-tuple-element.97), channel_id=1, source_target_pairs={{0,4},{1,5},{2,6},{3,7},{4,0},{5,1},{6,2},{7,3},{8,12},{9,13},{10,... | collective-permute-start | bytes 1572872 | tf_op jit(solution)/shard_map/ppermute | solution.py:38
  104.1 29.8 %copy-start.20 = (f32[256,512]{1,0:T(8,128)}, f32[256,512]{1,0:T(8,128)S(1)}, u32[]{:S(2)}) copy-start(f32[256,512]{1,0:T(8,128)S(1)} %collective-permute-done.7.refs_1_) | copy-start | bytes 1572868
  104.1 54.3 %copy-start.9 = (f32[1024,512]{1,0:T(8,128)}, f32[1024,512]{1,0:T(8,128)S(1)}, u32[]{:S(2)}) copy-start(f32[1024,512]{1,0:T(8,128)S(1)} %collective-permute-done.6.refs_1_) | copy-start | bytes 6291460
  104.2 53.6 %collective-permute-start.8 = (f32[1024,512]{1,0:T(8,128)S(1)}, f32[1024,512]{1,0:T(8,128)S(1)}, u32[]{:S(2)}, u32[]{:S(2)}) collective-permute-start(f32[1024,512]{1,0:T(8,128)S(1)} %get-tuple-element.98), channel_id=1, source_target_pairs={{0,16},{1,17},{4,20},{5,21},{10,26},{11,27},{14,30},{15,31},{16,0}... | collective-permute-start | bytes 6291464 | tf_op jit(solution)/shard_map/ppermute | solution.py:38
  133.9 43.5 %collective-permute-start.11 = (f32[1024,512]{1,0:T(8,128)}, f32[1024,512]{1,0:T(8,128)S(1)}, u32[]{:S(2)}, u32[]{:S(2)}) collective-permute-start(f32[1024,512]{1,0:T(8,128)} %get-tuple-element.112.refs_0_), channel_id=1, source_target_pairs={{0,1},{1,0},{4,5},{5,4},{10,11},{11,10},{14,15},{15,14},{16,17},{1... | collective-permute-start | bytes 6291464 | tf_op jit(solution)/shard_map/ppermute | solution.py:38
  137.8 31.4 %collective-permute-start.10 = (f32[256,512]{1,0:T(8,128)}, f32[256,512]{1,0:T(8,128)S(1)}, u32[]{:S(2)}, u32[]{:S(2)}) collective-permute-start(f32[256,512]{1,0:T(8,128)} %get-tuple-element.100), channel_id=1, source_target_pairs={{0,4},{1,5},{2,6},{3,7},{4,0},{5,1},{6,2},{7,3},{8,12},{9,13},{10,... | collective-permute-start | bytes 1572872 | tf_op jit(solution)/shard_map/ppermute | solution.py:38
  137.8 36.7 %collective-permute-start.9 = (f32[256,512]{1,0:T(8,128)}, f32[256,512]{1,0:T(8,128)S(1)}, u32[]{:S(2)}, u32[]{:S(2)}) collective-permute-start(f32[256,512]{1,0:T(8,128)} %get-tuple-element.99), channel_id=1, source_target_pairs={{0,4},{1,5},{2,6},{3,7},{4,0},{5,1},{6,2},{7,3},{8,12},{9,13},{10,... | collective-permute-start | bytes 1572872 | tf_op jit(solution)/shard_map/ppermute | solution.py:38
  158.4 29.8 %copy-start = (bf16[1024,1024]{1,0:T(8,128)(2,1)S(1)}, bf16[1024,1024]{1,0:T(8,128)(2,1)}, u32[]{:S(2)}) copy-start(bf16[1024,1024]{1,0:T(8,128)(2,1)} %get-tuple-element.103.refs_5_.refs_8_) | copy-start | bytes 6291460
  178.8 12.1 %collective-permute-start.12 = (f32[2,1024,512]{2,1,0:T(8,128)}, f32[2,1024,512]{2,1,0:T(8,128)}, u32[]{:S(2)}, u32[]{:S(2)}) collective-permute-start(f32[2,1024,512]{2,1,0:T(8,128)} %pad_maximum_fusion), channel_id=1, source_target_pairs={{0,8},{1,9},{4,12},{5,13},{10,2},{11,3},{14,6},{15,7},{16,24},{17,... | collective-permute-start | bytes 12582920 | tf_op jit(solution)/shard_map/ppermute | solution.py:38
  182.1 46.8 %collective-permute-start.13 = (f32[1024,512]{1,0:T(8,128)}, f32[1024,512]{1,0:T(8,128)}, u32[]{:S(2)}, u32[]{:S(2)}) collective-permute-start(f32[1024,512]{1,0:T(8,128)} %get-tuple-element.110.refs_0_), channel_id=1, source_target_pairs={{0,1},{1,0},{4,5},{5,4},{10,11},{11,10},{14,15},{15,14},{16,17},{1... | collective-permute-start | bytes 6291464 | tf_op jit(solution)/shard_map/ppermute | solution.py:38
  186.2 60.9 %collective-permute-start.16 = (f32[1024,512]{1,0:T(8,128)}, f32[1024,512]{1,0:T(8,128)}, u32[]{:S(2)}, u32[]{:S(2)}) collective-permute-start(f32[1024,512]{1,0:T(8,128)} %get-tuple-element.112.refs_0_), channel_id=1, source_target_pairs={{2,3},{3,2},{6,7},{7,6},{8,9},{9,8},{12,13},{13,12},{18,19},{19,18... | collective-permute-start | bytes 6291464 | tf_op jit(solution)/shard_map/ppermute | solution.py:38
  189.7 84.5 %collective-permute-start.22 = (f32[1024,512]{1,0:T(8,128)}, f32[1024,512]{1,0:T(8,128)S(1)}, u32[]{:S(2)}, u32[]{:S(2)}) collective-permute-start(f32[1024,512]{1,0:T(8,128)} %get-tuple-element.110.refs_0_), channel_id=1, source_target_pairs={{2,3},{3,2},{6,7},{7,6},{8,9},{9,8},{12,13},{13,12},{18,19},{19,18... | collective-permute-start | bytes 6291464 | tf_op jit(solution)/shard_map/ppermute | solution.py:38
  190.8 56.3 %collective-permute-start.14 = (f32[256,512]{1,0:T(8,128)S(1)}, f32[256,512]{1,0:T(8,128)S(1)}, u32[]{:S(2)}, u32[]{:S(2)}) collective-permute-start(f32[256,512]{1,0:T(8,128)S(1)} %copy-done.72), channel_id=1, source_target_pairs={{0,4},{1,5},{2,6},{3,7},{4,0},{5,1},{6,2},{7,3},{8,12},{9,13},{10,... | collective-permute-start | bytes 1572872 | tf_op jit(solution)/shard_map/ppermute | solution.py:38
  190.9 56.2 %collective-permute-start.15 = (f32[256,512]{1,0:T(8,128)S(1)}, f32[256,512]{1,0:T(8,128)S(1)}, u32[]{:S(2)}, u32[]{:S(2)}) collective-permute-start(f32[256,512]{1,0:T(8,128)S(1)} %copy-done.71), channel_id=1, source_target_pairs={{0,4},{1,5},{2,6},{3,7},{4,0},{5,1},{6,2},{7,3},{8,12},{9,13},{10,... | collective-permute-start | bytes 1572872 | tf_op jit(solution)/shard_map/ppermute | solution.py:38
  198.4 63.9 %copy-start.2 = (f32[512,512]{1,0:T(8,128)}, f32[512,512]{1,0:T(8,128)S(1)}, u32[]{:S(2)}) copy-start(f32[512,512]{1,0:T(8,128)S(1)} %get-tuple-element.202.refs_2_.refs_3_) | copy-start | bytes 3145732
  248.1 5.2 collective-permute-start.17
  250.0 3.3 collective-permute-start.18
  251.3 57.9 %collective-permute-start.26 = (f32[1024,512]{1,0:T(8,128)}, f32[1024,512]{1,0:T(8,128)}, u32[]{:S(2)}, u32[]{:S(2)}) collective-permute-start(f32[1024,512]{1,0:T(8,128)} %get-tuple-element.120.refs_0_), channel_id=1, source_target_pairs={{2,3},{3,2},{6,7},{7,6},{8,9},{9,8},{12,13},{13,12},{18,19},{19,18... | collective-permute-start | bytes 6291464 | tf_op jit(solution)/shard_map/ppermute | solution.py:38
  255.1 25.0 %collective-permute-start.19 = (f32[512,512]{1,0:T(8,128)}, f32[512,512]{1,0:T(8,128)}, u32[]{:S(2)}, u32[]{:S(2)}) collective-permute-start(f32[512,512]{1,0:T(8,128)} %broadcast_multiply_fusion.1), channel_id=1, source_target_pairs={{0,1},{4,5},{10,11},{14,15},{17,16},{21,20},{27,26},{31,30}} | collective-permute-start | bytes 3145736 | tf_op jit(solution)/shard_map/ppermute | solution.py:38
  259.4 25.9 %collective-permute-start.20 = (f32[512,512]{1,0:T(8,128)}, f32[512,512]{1,0:T(8,128)}, u32[]{:S(2)}, u32[]{:S(2)}) collective-permute-start(f32[512,512]{1,0:T(8,128)} %broadcast_multiply_fusion.1), channel_id=1, source_target_pairs={{1,17},{5,21},{11,27},{15,31},{16,0},{20,4},{26,10},{30,14}} | collective-permute-start | bytes 3145736 | tf_op jit(solution)/shard_map/ppermute | solution.py:38
  260.7 40.9 %collective-permute-start.21 = (f32[512,512]{1,0:T(8,128)}, f32[512,512]{1,0:T(8,128)}, u32[]{:S(2)}, u32[]{:S(2)}) collective-permute-start(f32[512,512]{1,0:T(8,128)} %broadcast_multiply_fusion.1), channel_id=1, source_target_pairs={{1,16},{5,20},{11,26},{15,30},{16,1},{20,5},{26,11},{30,15}} | collective-permute-start | bytes 3145736 | tf_op jit(solution)/shard_map/ppermute | solution.py:38
  275.6 33.6 %collective-permute-start.23 = (f32[512,512]{1,0:T(8,128)}, f32[512,512]{1,0:T(8,128)}, u32[]{:S(2)}, u32[]{:S(2)}) collective-permute-start(f32[512,512]{1,0:T(8,128)} %get-tuple-element.114), channel_id=1, source_target_pairs={{0,16},{1,17},{2,18},{3,19},{4,20},{5,21},{6,22},{7,23},{8,24},{9,... | collective-permute-start | bytes 3145736 | tf_op jit(solution)/shard_map/ppermute | solution.py:38
  280.0 23.6 %collective-permute-start.24 = (f32[256,512]{1,0:T(8,128)}, f32[256,512]{1,0:T(8,128)}, u32[]{:S(2)}, u32[]{:S(2)}) collective-permute-start(f32[256,512]{1,0:T(8,128)} %get-tuple-element.115), channel_id=1, source_target_pairs={{0,4},{1,5},{2,6},{3,7},{4,0},{5,1},{6,2},{7,3},{8,12},{9,13},{10,... | collective-permute-start | bytes 1572872 | tf_op jit(solution)/shard_map/ppermute | solution.py:38
  285.3 23.9 %collective-permute-start.25 = (f32[256,512]{1,0:T(8,128)}, f32[256,512]{1,0:T(8,128)}, u32[]{:S(2)}, u32[]{:S(2)}) collective-permute-start(f32[256,512]{1,0:T(8,128)} %get-tuple-element.116), channel_id=1, source_target_pairs={{0,4},{1,5},{2,6},{3,7},{4,0},{5,1},{6,2},{7,3},{8,12},{9,13},{10,... | collective-permute-start | bytes 1572872 | tf_op jit(solution)/shard_map/ppermute | solution.py:38
  309.2 54.8 %collective-permute-start.32 = (f32[1024,512]{1,0:T(8,128)S(1)}, f32[1024,512]{1,0:T(8,128)S(1)}, u32[]{:S(2)}, u32[]{:S(2)}) collective-permute-start(f32[1024,512]{1,0:T(8,128)S(1)} %copy-done.8), channel_id=1, source_target_pairs={{2,3},{3,2},{6,7},{7,6},{8,9},{9,8},{12,13},{13,12},{18,19},{19,18... | collective-permute-start | bytes 6291464 | tf_op jit(solution)/shard_map/ppermute | solution.py:38
  310.0 38.9 %collective-permute-start.28 = (f32[512,512]{1,0:T(8,128)S(1)}, f32[512,512]{1,0:T(8,128)S(1)}, u32[]{:S(2)}, u32[]{:S(2)}) collective-permute-start(f32[512,512]{1,0:T(8,128)S(1)} %select_select_fusion), channel_id=1, source_target_pairs={{0,4},{1,5},{4,0},{5,1},{10,14},{11,15},{14,10},{15,11},{16,20},{1... | collective-permute-start | bytes 3145736 | tf_op jit(solution)/shard_map/ppermute | solution.py:38
  313.0 50.9 %collective-permute-start.31 = (f32[512,512]{1,0:T(8,128)}, f32[512,512]{1,0:T(8,128)S(1)}, u32[]{:S(2)}, u32[]{:S(2)}) collective-permute-start(f32[512,512]{1,0:T(8,128)} %pad_maximum_fusion.3), channel_id=1, source_target_pairs={{0,1},{1,0},{2,3},{3,2},{4,5},{5,4},{6,7},{7,6},{8,9},{9,8},{10,11... | collective-permute-start | bytes 3145736 | tf_op jit(solution)/shard_map/ppermute | solution.py:38
  313.0 50.9 %collective-permute-start.29 = (f32[512,512]{1,0:T(8,128)S(1)}, f32[512,512]{1,0:T(8,128)S(1)}, u32[]{:S(2)}, u32[]{:S(2)}) collective-permute-start(f32[512,512]{1,0:T(8,128)S(1)} %get-tuple-element.125), channel_id=1, source_target_pairs={{0,16},{1,17},{2,18},{3,19},{4,20},{5,21},{6,22},{7,23},{8,24},{9,... | collective-permute-start | bytes 3145736 | tf_op jit(solution)/shard_map/ppermute | solution.py:38
  324.7 26.8 %copy-start.41 = (f32[512,512]{1,0:T(8,128)}, f32[512,512]{1,0:T(8,128)S(1)}, u32[]{:S(2)}) copy-start(f32[512,512]{1,0:T(8,128)S(1)} %get-tuple-element.121.refs_0_) | copy-start | bytes 3145732
  324.7 39.2 %collective-permute-start.27 = (f32[512,512]{1,0:T(8,128)S(1)}, f32[512,512]{1,0:T(8,128)S(1)}, u32[]{:S(2)}, u32[]{:S(2)}) collective-permute-start(f32[512,512]{1,0:T(8,128)S(1)} %get-tuple-element.123), channel_id=1, source_target_pairs={{0,16},{1,17},{2,18},{3,19},{4,20},{5,21},{6,22},{7,23},{8,24},{9,... | collective-permute-start | bytes 3145736 | tf_op jit(solution)/shard_map/ppermute | solution.py:38
  350.0 14.0 %collective-permute-start.30 = (f32[256,512]{1,0:T(8,128)S(1)}, f32[256,512]{1,0:T(8,128)S(1)}, u32[]{:S(2)}, u32[]{:S(2)}) collective-permute-start(f32[256,512]{1,0:T(8,128)S(1)} %get-tuple-element.127), channel_id=1, source_target_pairs={{0,4},{1,5},{2,6},{3,7},{4,0},{5,1},{6,2},{7,3},{8,12},{9,13},{10,... | collective-permute-start | bytes 1572872 | tf_op jit(solution)/shard_map/ppermute | solution.py:38
  364.0 35.5 %collective-permute-start.33 = (f32[2,512,512]{2,1,0:T(8,128)S(1)}, f32[2,512,512]{2,1,0:T(8,128)S(1)}, u32[]{:S(2)}, u32[]{:S(2)}) collective-permute-start(f32[2,512,512]{2,1,0:T(8,128)S(1)} %pad_maximum_fusion.2), channel_id=1, source_target_pairs={{0,2},{1,3},{4,6},{5,7},{10,8},{11,9},{14,12},{15,13},{16,18},{17,... | collective-permute-start | bytes 6291464 | tf_op jit(solution)/shard_map/ppermute | solution.py:38
  366.6 33.3 %collective-permute-start.36 = (f32[512,512]{1,0:T(8,128)}, f32[512,512]{1,0:T(8,128)S(1)}, u32[]{:S(2)}, u32[]{:S(2)}) collective-permute-start(f32[512,512]{1,0:T(8,128)} %pad_maximum_fusion.5), channel_id=1, source_target_pairs={{0,1},{1,0},{2,3},{3,2},{4,5},{5,4},{6,7},{7,6},{8,9},{9,8},{10,11... | collective-permute-start | bytes 3145736 | tf_op jit(solution)/shard_map/ppermute | solution.py:38
  366.6 36.3 %collective-permute-start.35 = (f32[512,512]{1,0:T(8,128)S(1)}, f32[512,512]{1,0:T(8,128)S(1)}, u32[]{:S(2)}, u32[]{:S(2)}) collective-permute-start(f32[512,512]{1,0:T(8,128)S(1)} %pad_maximum_fusion.4), channel_id=1, source_target_pairs={{0,1},{1,0},{2,3},{3,2},{4,5},{5,4},{6,7},{7,6},{8,9},{9,8},{10,11... | collective-permute-start | bytes 3145736 | tf_op jit(solution)/shard_map/ppermute | solution.py:38
  377.6 25.4 %collective-permute-start.34 = (f32[512,512]{1,0:T(8,128)S(1)}, f32[512,512]{1,0:T(8,128)S(1)}, u32[]{:S(2)}, u32[]{:S(2)}) collective-permute-start(f32[512,512]{1,0:T(8,128)S(1)} %get-tuple-element.133), channel_id=1, source_target_pairs={{0,16},{1,17},{2,18},{3,19},{4,20},{5,21},{6,22},{7,23},{8,24},{9,... | collective-permute-start | bytes 3145736 | tf_op jit(solution)/shard_map/ppermute | solution.py:38
  383.0 41.7 %collective-permute-start.37 = (f32[512,512]{1,0:T(8,128)}, f32[512,512]{1,0:T(8,128)S(1)}, u32[]{:S(2)}, u32[]{:S(2)}) collective-permute-start(f32[512,512]{1,0:T(8,128)} %pad_maximum_fusion.6), channel_id=1, source_target_pairs={{0,4},{1,5},{2,6},{3,7},{4,0},{5,1},{6,2},{7,3},{8,12},{9,13},{10,... | collective-permute-start | bytes 3145736 | tf_op jit(solution)/shard_map/ppermute | solution.py:38
  403.0 23.9 %collective-permute-start.38 = (f32[512,512]{1,0:T(8,128)S(1)}, f32[512,512]{1,0:T(8,128)S(1)}, u32[]{:S(2)}, u32[]{:S(2)}) collective-permute-start(f32[512,512]{1,0:T(8,128)S(1)} %pad_maximum_fusion.7), channel_id=1, source_target_pairs={{0,1},{1,0},{2,3},{3,2},{4,5},{5,4},{6,7},{7,6},{8,9},{9,8},{10,11... | collective-permute-start | bytes 3145736 | tf_op jit(solution)/shard_map/ppermute | solution.py:38
  427.8 29.3 %collective-permute-start.40 = (f32[1024,512]{1,0:T(8,128)}, f32[1024,512]{1,0:T(8,128)}, u32[]{:S(2)}, u32[]{:S(2)}) collective-permute-start(f32[1024,512]{1,0:T(8,128)} %get-tuple-element.140), channel_id=1, source_target_pairs={{0,16},{4,20},{10,26},{14,30},{17,1},{21,5},{27,11},{31,15}} | collective-permute-start | bytes 6291464 | tf_op jit(solution)/shard_map/ppermute | solution.py:38
  433.0 28.0 %collective-permute-start.41 = (f32[256,512]{1,0:T(8,128)}, f32[256,512]{1,0:T(8,128)S(1)}, u32[]{:S(2)}, u32[]{:S(2)}) collective-permute-start(f32[256,512]{1,0:T(8,128)} %get-tuple-element.152), channel_id=1, source_target_pairs={{0,4},{1,5},{2,6},{3,7},{4,0},{5,1},{6,2},{7,3},{8,12},{9,13},{10,... | collective-permute-start | bytes 1572872 | tf_op jit(solution)/shard_map/ppermute | solution.py:38
  461.8 6.5 %collective-permute-start.42 = (f32[1024,512]{1,0:T(8,128)}, f32[1024,512]{1,0:T(8,128)}, u32[]{:S(2)}, u32[]{:S(2)}) collective-permute-start(f32[1024,512]{1,0:T(8,128)} %broadcast_select_fusion.1), channel_id=1, source_target_pairs={{0,8},{1,9},{4,12},{5,13},{10,2},{11,3},{14,6},{15,7},{16,24},{17,... | collective-permute-start | bytes 6291464 | tf_op jit(solution)/shard_map/ppermute | solution.py:38
  464.4 25.5 %collective-permute-start.39 = (f32[512,512]{1,0:T(8,128)}, f32[512,512]{1,0:T(8,128)}, u32[]{:S(2)}, u32[]{:S(2)}) collective-permute-start(f32[512,512]{1,0:T(8,128)} %get-tuple-element.146), channel_id=1, source_target_pairs={{0,16},{1,17},{2,18},{3,19},{4,20},{5,21},{6,22},{7,23},{8,24},{9,... | collective-permute-start | bytes 3145736 | tf_op jit(solution)/shard_map/ppermute | solution.py:38
  465.5 43.7 %collective-permute-start.45 = (f32[512,512]{1,0:T(8,128)S(1)}, f32[512,512]{1,0:T(8,128)S(1)}, u32[]{:S(2)}, u32[]{:S(2)}) collective-permute-start(f32[512,512]{1,0:T(8,128)S(1)} %copy-done.38), channel_id=1, source_target_pairs={{0,4},{1,5},{2,6},{3,7},{4,0},{5,1},{6,2},{7,3},{8,12},{9,13},{10,... | collective-permute-start | bytes 3145736 | tf_op jit(solution)/shard_map/ppermute | solution.py:38
  468.2 44.2 %collective-permute-start.44 = (f32[512,512]{1,0:T(8,128)}, f32[512,512]{1,0:T(8,128)S(1)}, u32[]{:S(2)}, u32[]{:S(2)}) collective-permute-start(f32[512,512]{1,0:T(8,128)} %copy-done.65), channel_id=1, source_target_pairs={{0,16},{1,17},{2,18},{3,19},{4,20},{5,21},{6,22},{7,23},{8,24},{9,... | collective-permute-start | bytes 3145736 | tf_op jit(solution)/shard_map/ppermute | solution.py:38
  468.3 21.6 %copy-start.44 = (f32[512,512]{1,0:T(8,128)S(1)}, f32[512,512]{1,0:T(8,128)}, u32[]{:S(2)}) copy-start(f32[512,512]{1,0:T(8,128)} %copy-done.43) | copy-start | bytes 3145732
  468.3 21.6 %copy-start.58 = (f32[512,512]{1,0:T(8,128)S(1)}, f32[512,512]{1,0:T(8,128)}, u32[]{:S(2)}) copy-start(f32[512,512]{1,0:T(8,128)} %copy-done.57) | copy-start | bytes 3145732
  489.9 22.4 %copy-start.46 = (f32[512,512]{1,0:T(8,128)S(1)}, f32[512,512]{1,0:T(8,128)}, u32[]{:S(2)}) copy-start(f32[512,512]{1,0:T(8,128)} %copy-done.45) | copy-start | bytes 3145732
  489.9 22.4 %copy-start.48 = (f32[512,512]{1,0:T(8,128)S(1)}, f32[512,512]{1,0:T(8,128)}, u32[]{:S(2)}) copy-start(f32[512,512]{1,0:T(8,128)} %copy-done.47) | copy-start | bytes 3145732
  489.9 22.4 %copy-start.52 = (f32[512,512]{1,0:T(8,128)S(1)}, f32[512,512]{1,0:T(8,128)}, u32[]{:S(2)}) copy-start(f32[512,512]{1,0:T(8,128)} %copy-done.51) | copy-start | bytes 3145732
  499.7 35.1 %collective-permute-start.43 = (f32[512,512]{1,0:T(8,128)S(1)}, f32[512,512]{1,0:T(8,128)S(1)}, u32[]{:S(2)}, u32[]{:S(2)}) collective-permute-start(f32[512,512]{1,0:T(8,128)S(1)} %get-tuple-element.159), channel_id=1, source_target_pairs={{0,16},{1,17},{2,18},{3,19},{4,20},{5,21},{6,22},{7,23},{8,24},{9,... | collective-permute-start | bytes 3145736 | tf_op jit(solution)/shard_map/ppermute | solution.py:38
  512.4 22.5 %copy-start.16 = (f32[512,512]{1,0:T(8,128)S(1)}, f32[512,512]{1,0:T(8,128)}, u32[]{:S(2)}) copy-start(f32[512,512]{1,0:T(8,128)} %copy-done.14) | copy-start | bytes 3145732
  512.4 22.5 %copy-start.62 = (f32[256,512]{1,0:T(8,128)S(1)}, f32[256,512]{1,0:T(8,128)}, u32[]{:S(2)}) copy-start(f32[256,512]{1,0:T(8,128)} %copy-done.61) | copy-start | bytes 1572868
  512.4 22.4 %copy-start.64 = (f32[256,512]{1,0:T(8,128)S(1)}, f32[256,512]{1,0:T(8,128)}, u32[]{:S(2)}) copy-start(f32[256,512]{1,0:T(8,128)} %copy-done.63) | copy-start | bytes 1572868
  520.7 36.6 %collective-permute-start.46 = (f32[512,512]{1,0:T(8,128)S(1)}, f32[512,512]{1,0:T(8,128)S(1)}, u32[]{:S(2)}, u32[]{:S(2)}) collective-permute-start(f32[512,512]{1,0:T(8,128)S(1)} %get-tuple-element.167), channel_id=1, source_target_pairs={{0,16},{1,17},{2,18},{3,19},{4,20},{5,21},{6,22},{7,23},{8,24},{9,... | collective-permute-start | bytes 3145736 | tf_op jit(solution)/shard_map/ppermute | solution.py:38
  544.3 33.3 %collective-permute-start.47 = (f32[512,512]{1,0:T(8,128)S(1)}, f32[512,512]{1,0:T(8,128)S(1)}, u32[]{:S(2)}, u32[]{:S(2)}) collective-permute-start(f32[512,512]{1,0:T(8,128)S(1)} %get-tuple-element.171), channel_id=1, source_target_pairs={{0,16},{1,17},{2,18},{3,19},{4,20},{5,21},{6,22},{7,23},{8,24},{9,... | collective-permute-start | bytes 3145736 | tf_op jit(solution)/shard_map/ppermute | solution.py:38
  545.5 36.5 %collective-permute-start.48 = (f32[512,512]{1,0:T(8,128)S(1)}, f32[512,512]{1,0:T(8,128)S(1)}, u32[]{:S(2)}, u32[]{:S(2)}) collective-permute-start(f32[512,512]{1,0:T(8,128)S(1)} %copy-done.40), channel_id=1, source_target_pairs={{0,4},{1,5},{2,6},{3,7},{4,0},{5,1},{6,2},{7,3},{8,12},{9,13},{10,... | collective-permute-start | bytes 3145736 | tf_op jit(solution)/shard_map/ppermute | solution.py:38
  590.5 25.0 %collective-permute-start.49 = (f32[512,512]{1,0:T(8,128)S(1)}, f32[512,512]{1,0:T(8,128)S(1)}, u32[]{:S(2)}, u32[]{:S(2)}) collective-permute-start(f32[512,512]{1,0:T(8,128)S(1)} %get-tuple-element.176), channel_id=1, source_target_pairs={{0,16},{1,17},{2,18},{3,19},{4,20},{5,21},{6,22},{7,23},{8,24},{9,... | collective-permute-start | bytes 3145736 | tf_op jit(solution)/shard_map/ppermute | solution.py:38
  (59 other events, 427.2 us)

commit v3 on v2

--- a/solution.py
+++ b/solution.py
@@ -359,14 +359,15 @@
     own_centres = diagonal(rows_of(positions, grid.parity, width))
     other_centres = grid.swap_parity(own_centres, on_pair)
     packed = first_generator(grid, positions, own_centres, other_centres)
+    send_rest(late[0], other_centres)
     packed = jnp.where(same, packed, grid.swap_col_high(packed, on_pair))
-    send_urgent(0, packed)
-    pieces = []
+    packed = after(packed, *rests(late[0]))
+    send_rest(late[1], packed)
     packed = grid.spread_col_group(packed)
-    pieces_next = send_raw(1, packed)
-    packed = after(packed, urgent[0], *pieces)
-    other = after(grid.swap_parity(packed), *pieces_next)
-    send_urgent(1, other)
+    packed = after(packed, *rests(late[1]))
+    pieces = send_raw(1, packed)
+    other = after(grid.swap_parity(packed), *pieces)
+    send_urgent(0, other)
     pieces = send_raw(1, other)
     columns, *turn = rotation_of(
         jnp.where(is_first, packed, other),
@@ -375,15 +376,15 @@
         0,
         grid.parity,
     )
-    columns = after(columns, urgent[1], *pieces)
-    send_urgent(2, columns)
+    columns = after(columns, urgent[0], *pieces)
+    send_urgent(1, columns)
+    send_rest(early[0], columns)
     pieces = send_raw(2, columns)
     arrived = grid.swap_row_high(columns, on_group)
     columns = jnp.stack((jnp.where(same, columns, arrived), jnp.where(same, arrived, columns)))
-    columns = after(columns, *pieces, urgent[2])
+    columns = after(columns, *pieces, urgent[1], *rests(early[0]))
+    send_urgent(2, columns)
     send_urgent(3, columns)
-    send_rest(late[0], columns)
-    send_rest(late[1], columns)
     pieces = send_raw(2, columns)
     columns = grid.spread_row_group(columns)
     near_weights = weights_of(columns[0], grid.parity)
@@ -396,9 +397,9 @@
             for k in range(count)
         ]
     )
-    blocks = after(blocks, *pieces, *rests(late[0]))
+    blocks = after(blocks, *pieces)
     pieces = send_raw(len(raw_queue), blocks)
-    send_rest(early[0], blocks)
+    send_rest(early[1], blocks)
     own_centres = diagonal(blocks)
     row_centres = grid.swap_col_high(own_centres, on_pair)
     col_centres = grid.swap_row_high(own_centres, on_pair)
@@ -428,12 +429,12 @@
         is_left, jnp.where(row < col, top, bottom), jnp.where(row < col, bottom, top)
     )
     packed = after(packed, near[late[1]], moved[late[0]], *pieces)
-    packed = after(packed, *rests(early[0]))
+    packed = after(packed, *rests(early[1]))
     other = grid.swap_col_high(packed, on_group)
     move(late[1], packed)
     first_round(early[0], packed)
     move(early[0], packed)
-    send_rest(early[1], packed)
+    first_round(early[1], packed)
     far_queue = [(k, part) for k in early for part in range(2)]
     far_partner = {k: [] for k in early}
 
@@ -452,16 +453,13 @@
 
     middle = width // 2
     pieces = [send_late(late[0], near[late[0]][:middle], packed)]
-    partner = send_far(packed)
+    partner = [send_far(packed), send_far(packed)]
     both = jnp.stack((jnp.where(is_left, packed, other), jnp.where(is_left, other, packed)))
-    both = after(both, moved[late[1]], moved[early[0]], *pieces, partner, *rests(early[1]))
+    both = after(both, moved[late[1]], moved[early[0]], near[early[1]], *pieces, *partner)
     parts = (near[late[0]][middle:], moved[late[0]][:middle])
     late_half = send_late(late[0], jnp.concatenate(parts, axis=0), both)
-    partner = [send_far(both), send_far(both)]
-    first_round(early[1], both)
+    partner = send_far(both)
     move(early[1], both)
-    both = grid.spread_col_group(both)
-    both = after(both, moved[early[1]], *partner)
     far_near, far_sent, far_moved = {}, {}, {}
 
     def far_round(k, token):
@@ -469,26 +467,29 @@
         others = [[part] for part in far_partner[k]]
         far_near[k], far_sent[k] = rotate(tiles, others, *far_weights, turn)
 
+    def far_move(k, token):
+        far_moved[k] = grid.swap_row_high(after(far_sent[k], token))
+
+    far_round(early[0], both)
+    both = grid.spread_col_group(both)
+    both = after(both, far_near[early[0]], moved[early[1]], partner)
     late_quarter = send_late(late[0], moved[late[0]][middle:], both)
+    far_move(early[0], both)
     partner = send_far(both)
     columns, *second_turn = rotation_of(
         both[0], both[1], grid.row_high, grid.row_high, grid.col_high
     )
-    columns = after(columns, late_half, partner)
-    far_round(early[0], columns)
+    columns = after(columns, far_moved[early[0]], late_half, partner)
     far_round(early[1], columns)
     arrived = grid.swap_row_high(columns, lambda rh, rg, ch, cg, e: rg == cg and rh == e)
     columns = jnp.where(grid.row_high == grid.parity, columns, arrived)
-    far_moved[early[0]] = grid.swap_row_high(far_sent[early[0]])
-    columns = after(columns, far_near[early[0]], far_near[early[1]], late_quarter)
-    far_moved[early[1]] = grid.swap_row_high(after(far_sent[early[1]], columns))
-    for part in (near[late[1]], moved[late[1]]):
-        send_late(late[1], part, columns)
+    columns = after(columns, far_near[early[1]], late_quarter)
+    far_move(early[1], columns)
+    send_late(late[1], jnp.concatenate((near[late[1]], moved[late[1]]), axis=0), columns)
     weights = weights_of(grid.spread_row_group(columns), grid.col_high)
-    weights = [after(weight, far_moved[early[0]]) for weight in weights]
 
     outputs = [None] * count
-    before = [late_far[late[1]][0]]
+    before = [far_moved[early[1]]]
     for k in [*early, *late]:
         mine = [[near[k]], [moved[k]]]
         theirs = [[far_near[k]], [far_moved[k]]] if k in early else [[part] for part in late_far[k]]

time: 628 us -> 620 us (0.987)
  the two profiles are of different devices: /device:TPU:31 before, /device:TPU:0 now
where the time goes in v3:
time: 620 us; the launch traced here: 610 us
  waiting for transfers between devices  240 us (39%)
  Pallas kernels  174 us (28%)
  starting transfers between devices  114 us (18%)
  other arithmetic  40.6 us (7%)
  local copies, waits for them, and re-layouts  39.9 us (6%)
    ppermute x49, waiting for transfers between devices, send(): return lax.ppermute(value, ('row', 'col'), pairs)  240 us
    pallas_call x14, Pallas kernels, rotate(): pl.pallas_call(functools.partial(rotate_kernel, tuple(spans), per_half),...  134 us
    ppermute x49, starting transfers between devices, send(): return lax.ppermute(value, ('row', 'col'), pairs)  114 us
    pallas_call x2, Pallas kernels, rotation_of(): pl.pallas_call(rotation_kernel, out_shape=(jax.ShapeDtypeStruct((size, wi...  40.1 us
    unnamed x138, local copies, waits for them, and re-layouts  22.5 us
  transfers between devices with their start and end apart: 49, of which 23 were waited for; matrix products, arithmetic and copies ran while one was open for 9% of the time, Pallas kernels for 27%

profile of v3, /device:TPU:0, one launch (start us, length us, event | category | flops | bytes accessed | tf_op | source)
XLA Modules:
  0.0 610.3 jit_solution(9412524526589635098)
XLA Ops:
  0.1 2.8 select_reduce_fusion.1
  2.9 4.8 collective-permute-start
  7.7 7.0 %slice_bitcast_fusion = (f32[1024,512]{1,0:T(8,128)}, f32[1024,512]{1,0:T(8,128)}, f32[1024,512]{1,0:T(8,128)}, f32[1024,512]{1,0:T(8,128)}) fusion(f32[4,1024,512]{2,1,0:T(8,128)} %param.1), kind=kLoop, calls=%fused_computation.8 | loop fusion | bytes 16777216 | tf_op jit(solution)/shard_map/squeeze | solution.py:351
  15.5 4.1 multiply_reduce_fusion
  21.4 2.8 collective-permute-start.1
  24.2 11.4 %collective-permute-done.1 = f32[512,512]{1,0:T(8,128)} collective-permute-done((f32[512,512]{1,0:T(8,128)S(1)}, f32[512,512]{1,0:T(8,128)}, u32[]{:S(2)}, u32[]{:S(2)}) %collective-permute-start.1) | collective-permute-done | bytes 1048608 | tf_op jit(solution)/shard_map/ppermute | solution.py:38
  37.4 2.1 collective-permute-start.4
  39.5 8.4 %collective-permute-start.3 = (f32[512,512]{1,0:T(8,128)S(1)}, f32[512,512]{1,0:T(8,128)}, u32[]{:S(2)}, u32[]{:S(2)}) collective-permute-start(f32[512,512]{1,0:T(8,128)S(1)} %broadcast_select_fusion.6), channel_id=1, source_target_pairs={{0,2},{1,3},{4,6},{5,7},{10,8},{11,9},{14,12},{15,13},{16,18},{17,... | collective-permute-start | bytes 3145736 | tf_op jit(solution)/shard_map/ppermute | solution.py:38
  47.9 11.3 %collective-permute-done.3 = f32[512,512]{1,0:T(8,128)} collective-permute-done((f32[512,512]{1,0:T(8,128)S(1)}, f32[512,512]{1,0:T(8,128)}, u32[]{:S(2)}, u32[]{:S(2)}) %collective-permute-start.3) | collective-permute-done | bytes 1048608 | tf_op jit(solution)/shard_map/ppermute | solution.py:38
  60.1 4.1 slice_bitcast_fusion.6
  64.1 2.6 collective-permute-start.6
  66.7 13.5 %collective-permute-done.6.refs_0_ = f32[256,512]{1,0:T(8,128)S(1)} collective-permute-done((f32[256,512]{1,0:T(8,128)S(1)}, f32[256,512]{1,0:T(8,128)S(1)}, u32[]{:S(2)}, u32[]{:S(2)}) %collective-permute-start.6) | collective-permute-done | bytes 524320 | tf_op jit(solution)/shard_map/ppermute | solution.py:38
  81.7 9.3 %collective-permute-start.7 = (f32[1024,512]{1,0:T(8,128)}, f32[1024,512]{1,0:T(8,128)S(1)}, u32[]{:S(2)}, u32[]{:S(2)}) collective-permute-start(f32[1024,512]{1,0:T(8,128)} %get-tuple-element.123.refs_0_), channel_id=1, source_target_pairs={{0,1},{1,0},{4,5},{5,4},{10,11},{11,10},{14,15},{15,14},{16,17},{1... | collective-permute-start | bytes 6291464 | tf_op jit(solution)/shard_map/ppermute | solution.py:38
  91.5 19.7 %shard_map.17 = (f32[1024,512]{1,0:T(8,128)S(1)}, bf16[1024,1024]{1,0:T(8,128)(2,1)}, bf16[1024,1024]{1,0:T(8,128)(2,1)}) custom-call(s32[3]{0:T(128)S(1)} %pad_add_fusion.flags_ref, f32[512,512]{1,0:T(8,128)S(1)} %get-tuple-element.204.first_ref, f32[512,512]{1,0:T(8,128)S(1)} %get-tuple-element.203.second_ref), custom_call_target="tpu_custom_call" | custom-call | tf_op jit(solution)/shard_map/pallas_call | solution.py:179
  111.2 6.4 %collective-permute-done.8.refs_1_ = f32[256,512]{1,0:T(8,128)S(1)} collective-permute-done((f32[256,512]{1,0:T(8,128)S(1)}, f32[256,512]{1,0:T(8,128)S(1)}, u32[]{:S(2)}, u32[]{:S(2)}) %collective-permute-start.8) | collective-permute-done | bytes 524320 | tf_op jit(solution)/shard_map/ppermute | solution.py:38
  117.6 7.5 %collective-permute-start.9 = (f32[1024,512]{1,0:T(8,128)S(1)}, f32[1024,512]{1,0:T(8,128)S(1)}, u32[]{:S(2)}, u32[]{:S(2)}) collective-permute-start(f32[1024,512]{1,0:T(8,128)S(1)} %get-tuple-element.100), channel_id=1, source_target_pairs={{0,16},{1,17},{4,20},{5,21},{10,26},{11,27},{14,30},{15,31},{16,0}... | collective-permute-start | bytes 6291464 | tf_op jit(solution)/shard_map/ppermute | solution.py:38
  125.1 3.2 collective-permute-start.12
  132.1 17.0 %collective-permute-done.9 = f32[1024,512]{1,0:T(8,128)S(1)} collective-permute-done((f32[1024,512]{1,0:T(8,128)S(1)}, f32[1024,512]{1,0:T(8,128)S(1)}, u32[]{:S(2)}, u32[]{:S(2)}) %collective-permute-start.9) | collective-permute-done | bytes 2097184 | tf_op jit(solution)/shard_map/ppermute | solution.py:38
  149.7 2.5 pad_maximum_fusion
  152.2 7.8 %collective-permute-done.10.refs_2_ = f32[256,512]{1,0:T(8,128)S(1)} collective-permute-done((f32[256,512]{1,0:T(8,128)}, f32[256,512]{1,0:T(8,128)S(1)}, u32[]{:S(2)}, u32[]{:S(2)}) %collective-permute-start.10) | collective-permute-done | bytes 524320 | tf_op jit(solution)/shard_map/ppermute | solution.py:38
  160.0 10.1 %collective-permute-done.11.refs_3_ = f32[256,512]{1,0:T(8,128)S(1)} collective-permute-done((f32[256,512]{1,0:T(8,128)}, f32[256,512]{1,0:T(8,128)S(1)}, u32[]{:S(2)}, u32[]{:S(2)}) %collective-permute-start.11) | collective-permute-done | bytes 524320 | tf_op jit(solution)/shard_map/ppermute | solution.py:38
  173.0 3.3 collective-permute-start.14
  176.3 4.0 collective-permute-start.15
  180.3 2.2 collective-permute-start.16
  184.1 2.9 collective-permute-start.18
  187.0 3.2 broadcast_select_fusion
  194.0 7.4 %shard_map.18 = f32[512,512]{1,0:T(8,128)S(1)} custom-call(f32[1024,512]{1,0:T(8,128)} %get-tuple-element.123.refs_0_, f32[1024,512]{1,0:T(8,128)S(1)} %copy-done.10, f32[512,512]{1,0:T(8,128)S(1)} %get-tuple-element.202.refs_2_.refs_3_, f32[512,512]{1,0:T(8,128)S(1)} %get-tuple-element.201.refs_3_.refs_4_, ...), custom_call_target="tpu_custom_call" | custom-call | tf_op jit(solution)/shard_map/pallas_call | solution.py:277
  201.4 7.2 %shard_map.19 = f32[512,512]{1,0:T(8,128)S(1)} custom-call(f32[1024,512]{1,0:T(8,128)} %get-tuple-element.129.refs_0_, f32[1024,512]{1,0:T(8,128)S(1)} %copy-done.13, f32[512,512]{1,0:T(8,128)S(1)} %get-tuple-element.202.refs_2_.refs_3_, f32[512,512]{1,0:T(8,128)S(1)} %get-tuple-element.201.refs_3_.refs_4_, ...), custom_call_target="tpu_custom_call" | custom-call | tf_op jit(solution)/shard_map/pallas_call | solution.py:277
  208.6 7.6 %shard_map.20 = f32[512,512]{1,0:T(8,128)S(1)} custom-call(f32[1024,512]{1,0:T(8,128)} %get-tuple-element.115.refs_0_, f32[1024,512]{1,0:T(8,128)} %collective-permute-done.15.refs_1_, f32[512,512]{1,0:T(8,128)S(1)} %get-tuple-element.202.refs_2_.refs_3_, f32[512,512]{1,0:T(8,128)S(1)} %get-tuple-element.201.refs_3_.refs_4_, ...), custom_call_target="tpu_custom_call" | custom-call | tf_op jit(solution)/shard_map/pallas_call | solution.py:277
  216.3 10.8 %collective-permute-done.16.refs_1_ = f32[1024,512]{1,0:T(8,128)} collective-permute-done((f32[1024,512]{1,0:T(8,128)}, f32[1024,512]{1,0:T(8,128)}, u32[]{:S(2)}, u32[]{:S(2)}) %collective-permute-start.16) | collective-permute-done | bytes 2097184 | tf_op jit(solution)/shard_map/ppermute | solution.py:38
  227.1 17.6 %shard_map.21 = f32[512,512]{1,0:T(8,128)S(1)} custom-call(f32[1024,512]{1,0:T(8,128)} %get-tuple-element.113.refs_0_, f32[1024,512]{1,0:T(8,128)} %collective-permute-done.16.refs_1_, f32[512,512]{1,0:T(8,128)S(1)} %get-tuple-element.202.refs_2_.refs_3_, f32[512,512]{1,0:T(8,128)S(1)} %get-tuple-element.201.refs_3_.refs_4_, ...), custom_call_target="tpu_custom_call" | custom-call | tf_op jit(solution)/shard_map/pallas_call | solution.py:277
  252.6 5.0 collective-permute-start.21
  260.6 10.9 %shard_map.23 = (f32[512,512]{1,0:T(8,128)S(1)}, f32[512,512]{1,0:T(8,128)}) custom-call(f32[1024,512]{1,0:T(8,128)} %get-tuple-element.115.refs_0_, f32[1024,512]{1,0:T(8,128)} %collective-permute-done.15.refs_1_, f32[1024,512]{1,0:T(8,128)S(1)} %copy-done.37, f32[512,512]{1,0:T(8,128)S(1)} %get-tuple-element.202.refs_2_.refs_3_, ...), custom_call_target="tpu_custom_call" | custom-call | tf_op jit(solution)/shard_map/pallas_call | solution.py:277
  272.4 5.0 collective-permute-start.24
  281.6 10.4 %shard_map.22 = (f32[512,512]{1,0:T(8,128)S(1)}, f32[512,512]{1,0:T(8,128)S(1)}) custom-call(f32[1024,512]{1,0:T(8,128)} %get-tuple-element.113.refs_0_, f32[1024,512]{1,0:T(8,128)} %collective-permute-done.16.refs_1_, f32[1024,512]{1,0:T(8,128)} %collective-permute-done.4.refs_2_, f32[512,512]{1,0:T(8,128)S(1)} %copy-done.4, ...), custom_call_target="tpu_custom_call" | custom-call | tf_op jit(solution)/shard_map/pallas_call | solution.py:277
  292.1 2.1 select_select_fusion
  294.3 4.8 collective-permute-done.25.refs_2_
  299.1 15.1 %collective-permute-done.26.refs_3_ = f32[256,512]{1,0:T(8,128)} collective-permute-done((f32[256,512]{1,0:T(8,128)}, f32[256,512]{1,0:T(8,128)}, u32[]{:S(2)}, u32[]{:S(2)}) %collective-permute-start.26) | collective-permute-done | bytes 524320 | tf_op jit(solution)/shard_map/ppermute | solution.py:38
  320.8 10.1 %shard_map.24 = (f32[512,512]{1,0:T(8,128)S(1)}, f32[512,512]{1,0:T(8,128)S(1)}) custom-call(f32[1024,512]{1,0:T(8,128)} %get-tuple-element.123.refs_0_, f32[1024,512]{1,0:T(8,128)S(1)} %copy-done.11, f32[1024,512]{1,0:T(8,128)S(1)} %copy-done.39, f32[512,512]{1,0:T(8,128)S(1)} %copy-done.4, f32[512,512]{1,0:T(8,128)S(1)} %get-tuple-element.201.refs_3_.refs_4_, ...), custom_call_target="tpu_custom_call" | custom-call | tf_op jit(solution)/shard_map/pallas_call | solution.py:277
  332.6 7.6 %collective-permute-done.29 = f32[512,512]{1,0:T(8,128)S(1)} collective-permute-done((f32[512,512]{1,0:T(8,128)S(1)}, f32[512,512]{1,0:T(8,128)S(1)}, u32[]{:S(2)}, u32[]{:S(2)}) %collective-permute-start.29) | collective-permute-done | bytes 1048608 | tf_op jit(solution)/shard_map/ppermute | solution.py:38
  340.2 10.0 %shard_map.25 = (f32[512,512]{1,0:T(8,128)S(1)}, f32[512,512]{1,0:T(8,128)S(1)}) custom-call(f32[1024,512]{1,0:T(8,128)} %get-tuple-element.129.refs_0_, f32[1024,512]{1,0:T(8,128)S(1)} %copy-done.14, f32[1024,512]{1,0:T(8,128)} %collective-permute-done.27.refs_2_, f32[512,512]{1,0:T(8,128)S(1)} %copy-done.4, ...), custom_call_target="tpu_custom_call" | custom-call | tf_op jit(solution)/shard_map/pallas_call | solution.py:277
  351.4 18.8 %collective-permute-done.31.refs_2_ = f32[256,512]{1,0:T(8,128)S(1)} collective-permute-done((f32[256,512]{1,0:T(8,128)S(1)}, f32[256,512]{1,0:T(8,128)S(1)}, u32[]{:S(2)}, u32[]{:S(2)}) %collective-permute-start.31) | collective-permute-done | bytes 524320 | tf_op jit(solution)/shard_map/ppermute | solution.py:38
  376.7 2.2 fusion.1
  380.0 8.5 %shard_map.26 = (f32[512,512]{1,0:T(8,128)S(1)}, f32[512,512]{1,0:T(8,128)S(1)}) custom-call(f32[256,512]{1,0:T(8,128)S(1)} %copy-done.23, f32[256,512]{1,0:T(8,128)S(1)} %copy-done.25, f32[256,512]{1,0:T(8,128)S(1)} %copy-done.27, f32[256,512]{1,0:T(8,128)S(1)} %copy-done.32, f32[512,512]{1,0:T(8,128)S(1)} %collective-permute-done.32.refs_4_, ...), custom_call_target="tpu_custom_call" | custom-call | tf_op jit(solution)/shard_map/pallas_call | solution.py:277
  388.5 6.6 %collective-permute-done.34 = f32[2,512,512]{2,1,0:T(8,128)S(1)} collective-permute-done((f32[2,512,512]{2,1,0:T(8,128)S(1)}, f32[2,512,512]{2,1,0:T(8,128)S(1)}, u32[]{:S(2)}, u32[]{:S(2)}) %collective-permute-start.34) | collective-permute-done | bytes 2097184 | tf_op jit(solution)/shard_map/ppermute | solution.py:38
  398.0 20.3 %shard_map.27 = (f32[1024,512]{1,0:T(8,128)}, bf16[1024,1024]{1,0:T(8,128)(2,1)}, bf16[1024,1024]{1,0:T(8,128)(2,1)}) custom-call(s32[3]{0:T(128)S(1)} %pad_add_fusion.1.flags_ref, f32[512,512]{1,0:T(8,128)S(1)} %get-tuple-element.196.first_ref, f32[512,512]{1,0:T(8,128)S(1)} %get-tuple-element.195.second_ref), custom_call_target="tpu_custom_call" | custom-call | tf_op jit(solution)/shard_map/pallas_call | solution.py:179
  421.3 3.3 collective-permute-start.40
  424.6 12.8 %collective-permute-start.41 = (f32[256,512]{1,0:T(8,128)}, f32[256,512]{1,0:T(8,128)}, u32[]{:S(2)}, u32[]{:S(2)}) collective-permute-start(f32[256,512]{1,0:T(8,128)} %get-tuple-element.156), channel_id=1, source_target_pairs={{0,4},{1,5},{2,6},{3,7},{4,0},{5,1},{6,2},{7,3},{8,12},{9,13},{10,... | collective-permute-start | bytes 1572872 | tf_op jit(solution)/shard_map/ppermute | solution.py:38
  444.8 9.5 %shard_map.28 = (f32[512,512]{1,0:T(8,128)S(1)}, f32[512,512]{1,0:T(8,128)S(1)}) custom-call(f32[256,512]{1,0:T(8,128)S(1)} %copy-done.30, f32[256,512]{1,0:T(8,128)S(1)} %copy-done.35, f32[256,512]{1,0:T(8,128)} %collective-permute-done.25.refs_2_, f32[256,512]{1,0:T(8,128)} %collective-permute-done.26.refs_3_, f32[512,512]{1,0:T(8,128)S(1)} %copy-done.55, ...), custom_call_target="tpu_custom_call" | custom-call | tf_op jit(solution)/shard_map/pallas_call | solution.py:277
  454.4 2.8 broadcast_select_fusion.1
  457.2 4.0 collective-permute-done.41.refs_4_
  461.2 3.4 collective-permute-start.42
  464.6 2.6 collective-permute-done.42
  470.7 8.5 %shard_map.29 = (f32[512,512]{1,0:T(8,128)S(1)}, f32[512,512]{1,0:T(8,128)S(1)}) custom-call(f32[512,512]{1,0:T(8,128)S(1)} %copy-done.41, f32[512,512]{1,0:T(8,128)S(1)} %copy-done.45, f32[512,512]{1,0:T(8,128)S(1)} %copy-done.51, f32[512,512]{1,0:T(8,128)S(1)} %copy-done.53, f32[512,512]{1,0:T(8,128)S(1)} %get-tuple-element.173.refs_4_.refs_5_.refs_3_, ...), custom_call_target="tpu_custom_call" | custom-call | tf_op jit(solution)/shard_map/pallas_call | solution.py:277
  479.5 2.6 collective-permute-start.47
  482.2 8.7 %collective-permute-done.44.refs_3_ = f32[512,512]{1,0:T(8,128)S(1)} collective-permute-done((f32[512,512]{1,0:T(8,128)}, f32[512,512]{1,0:T(8,128)S(1)}, u32[]{:S(2)}, u32[]{:S(2)}) %collective-permute-start.44) | collective-permute-done | bytes 1048608 | tf_op jit(solution)/shard_map/ppermute | solution.py:38
  490.9 8.3 %shard_map.30 = (f32[512,512]{1,0:T(8,128)S(1)}, f32[512,512]{1,0:T(8,128)S(1)}) custom-call(f32[512,512]{1,0:T(8,128)S(1)} %copy-done.43, f32[512,512]{1,0:T(8,128)S(1)} %copy-done.47, f32[512,512]{1,0:T(8,128)S(1)} %copy-done.57, f32[512,512]{1,0:T(8,128)S(1)} %collective-permute-done.44.refs_3_, ...), custom_call_target="tpu_custom_call" | custom-call | tf_op jit(solution)/shard_map/pallas_call | solution.py:277
  499.3 14.0 %collective-permute-done.43 = f32[512,512]{1,0:T(8,128)S(1)} collective-permute-done((f32[512,512]{1,0:T(8,128)S(1)}, f32[512,512]{1,0:T(8,128)S(1)}, u32[]{:S(2)}, u32[]{:S(2)}) %collective-permute-start.43) | collective-permute-done | bytes 1048608 | tf_op jit(solution)/shard_map/ppermute | solution.py:38
  513.4 9.6 %shard_map.31 = (f32[512,512]{1,0:T(8,128)S(1)}, f32[512,512]{1,0:T(8,128)S(1)}) custom-call(f32[512,512]{1,0:T(8,128)S(1)} %copy-done.17, f32[512,512]{1,0:T(8,128)} %collective-permute-done.24.refs_1_, f32[256,512]{1,0:T(8,128)S(1)} %copy-done.61, f32[512,512]{1,0:T(8,128)S(1)} %copy-done.49, f32[256,512]{1,0:T(8,128)} %collective-permute-done.41.refs_4_, ...), custom_call_target="tpu_custom_call" | custom-call | tf_op jit(solution)/shard_map/pallas_call | solution.py:277
  525.4 10.4 %collective-permute-done.45 = f32[512,512]{1,0:T(8,128)S(1)} collective-permute-done((f32[512,512]{1,0:T(8,128)S(1)}, f32[512,512]{1,0:T(8,128)S(1)}, u32[]{:S(2)}, u32[]{:S(2)}) %collective-permute-start.45) | collective-permute-done | bytes 1048608 | tf_op jit(solution)/shard_map/ppermute | solution.py:38
  535.8 19.6 %collective-permute-done.46 = f32[512,512]{1,0:T(8,128)S(1)} collective-permute-done((f32[512,512]{1,0:T(8,128)S(1)}, f32[512,512]{1,0:T(8,128)S(1)}, u32[]{:S(2)}, u32[]{:S(2)}) %collective-permute-start.46) | collective-permute-done | bytes 1048608 | tf_op jit(solution)/shard_map/ppermute | solution.py:38
  555.4 18.3 %collective-permute-done.47.refs_2_ = f32[1024,512]{1,0:T(8,128)S(1)} collective-permute-done((f32[1024,512]{1,0:T(8,128)S(1)}, f32[1024,512]{1,0:T(8,128)S(1)}, u32[]{:S(2)}, u32[]{:S(2)}) %collective-permute-start.47) | collective-permute-done | bytes 2097184 | tf_op jit(solution)/shard_map/ppermute | solution.py:38
  573.6 8.5 %shard_map.32 = (f32[512,512]{1,0:T(8,128)S(1)}, f32[512,512]{1,0:T(8,128)S(1)}) custom-call(f32[512,512]{1,0:T(8,128)S(1)} %copy-done.19, f32[512,512]{1,0:T(8,128)S(1)} %copy-done.21, f32[1024,512]{1,0:T(8,128)S(1)} %collective-permute-done.47.refs_2_, f32[512,512]{1,0:T(8,128)S(1)} %get-tuple-element.173.refs_4_.refs_5_.refs_3_, ...), custom_call_target="tpu_custom_call" | custom-call | tf_op jit(solution)/shard_map/pallas_call | solution.py:277
  588.5 19.0 %collective-permute-done.48 = f32[512,512]{1,0:T(8,128)S(1)} collective-permute-done((f32[512,512]{1,0:T(8,128)S(1)}, f32[512,512]{1,0:T(8,128)S(1)}, u32[]{:S(2)}, u32[]{:S(2)}) %collective-permute-start.48) | collective-permute-done | bytes 1048608 | tf_op jit(solution)/shard_map/ppermute | solution.py:38
  (237 shorter events, 80.7 us)
Async XLA Ops:
  2.9 11.8 %collective-permute-start = (f32[4,512]{1,0:T(4,128)S(1)}, f32[4,512]{1,0:T(4,128)S(1)}, u32[]{:S(2)}, u32[]{:S(2)}) collective-permute-start(f32[4,512]{1,0:T(4,128)S(1)} %select_reduce_fusion.1), channel_id=1, source_target_pairs={{0,1},{1,0},{10,11},{11,10},{20,21},{21,20},{30,31},{31,30}} | collective-permute-start | bytes 24584 | tf_op jit(solution)/shard_map/ppermute | solution.py:38
  14.7 22.8 %collective-permute-start.2 = (f32[1024,512]{1,0:T(8,128)}, f32[1024,512]{1,0:T(8,128)S(1)}, u32[]{:S(2)}, u32[]{:S(2)}) collective-permute-start(f32[1024,512]{1,0:T(8,128)} %get-tuple-element.115.refs_0_), channel_id=1, source_target_pairs={{2,3},{3,2},{6,7},{7,6},{8,9},{9,8},{12,13},{13,12},{18,19},{19,18... | collective-permute-start | bytes 6291464 | tf_op jit(solution)/shard_map/ppermute | solution.py:38
  21.4 14.1 %collective-permute-start.1 = (f32[512,512]{1,0:T(8,128)S(1)}, f32[512,512]{1,0:T(8,128)}, u32[]{:S(2)}, u32[]{:S(2)}) collective-permute-start(f32[512,512]{1,0:T(8,128)S(1)} %select_select_fusion.1), channel_id=1, source_target_pairs={{0,4},{1,5},{10,14},{11,15},{20,16},{21,17},{30,26},{31,27}} | collective-permute-start | bytes 3145736 | tf_op jit(solution)/shard_map/ppermute | solution.py:38
  37.4 26.7 %copy-start.36 = (f32[1024,512]{1,0:T(8,128)}, f32[1024,512]{1,0:T(8,128)S(1)}, u32[]{:S(2)}) copy-start(f32[1024,512]{1,0:T(8,128)S(1)} %collective-permute-done.2.refs_2_) | copy-start | bytes 6291460
  37.4 22.0 %collective-permute-start.4 = (f32[1024,512]{1,0:T(8,128)}, f32[1024,512]{1,0:T(8,128)}, u32[]{:S(2)}, u32[]{:S(2)}) collective-permute-start(f32[1024,512]{1,0:T(8,128)} %get-tuple-element.113.refs_0_), channel_id=1, source_target_pairs={{2,3},{3,2},{6,7},{7,6},{8,9},{9,8},{12,13},{13,12},{18,19},{19,18... | collective-permute-start | bytes 6291464 | tf_op jit(solution)/shard_map/ppermute | solution.py:38
  39.5 19.7 %collective-permute-start.3 = (f32[512,512]{1,0:T(8,128)S(1)}, f32[512,512]{1,0:T(8,128)}, u32[]{:S(2)}, u32[]{:S(2)}) collective-permute-start(f32[512,512]{1,0:T(8,128)S(1)} %broadcast_select_fusion.6), channel_id=1, source_target_pairs={{0,2},{1,3},{4,6},{5,7},{10,8},{11,9},{14,12},{15,13},{16,18},{17,... | collective-permute-start | bytes 3145736 | tf_op jit(solution)/shard_map/ppermute | solution.py:38
  59.5 22.2 %collective-permute-start.5 = (f32[512,512]{1,0:T(8,128)S(1)}, f32[512,512]{1,0:T(8,128)S(1)}, u32[]{:S(2)}, u32[]{:S(2)}) collective-permute-start(f32[512,512]{1,0:T(8,128)S(1)} %broadcast_select_fusion.7), channel_id=1, source_target_pairs={{0,1},{1,0},{2,3},{3,2},{4,5},{5,4},{6,7},{7,6},{8,9},{9,8},{10,11... | collective-permute-start | bytes 3145736 | tf_op jit(solution)/shard_map/ppermute | solution.py:38
  64.1 16.1 %collective-permute-start.6 = (f32[256,512]{1,0:T(8,128)S(1)}, f32[256,512]{1,0:T(8,128)S(1)}, u32[]{:S(2)}, u32[]{:S(2)}) collective-permute-start(f32[256,512]{1,0:T(8,128)S(1)} %get-tuple-element.95), channel_id=1, source_target_pairs={{0,4},{1,5},{2,6},{3,7},{4,0},{5,1},{6,2},{7,3},{8,12},{9,13},{10,... | collective-permute-start | bytes 1572872 | tf_op jit(solution)/shard_map/ppermute | solution.py:38
  81.7 36.0 %collective-permute-start.7 = (f32[1024,512]{1,0:T(8,128)}, f32[1024,512]{1,0:T(8,128)S(1)}, u32[]{:S(2)}, u32[]{:S(2)}) collective-permute-start(f32[1024,512]{1,0:T(8,128)} %get-tuple-element.123.refs_0_), channel_id=1, source_target_pairs={{0,1},{1,0},{4,5},{5,4},{10,11},{11,10},{14,15},{15,14},{16,17},{1... | collective-permute-start | bytes 6291464 | tf_op jit(solution)/shard_map/ppermute | solution.py:38
  91.0 26.6 %collective-permute-start.8 = (f32[256,512]{1,0:T(8,128)S(1)}, f32[256,512]{1,0:T(8,128)S(1)}, u32[]{:S(2)}, u32[]{:S(2)}) collective-permute-start(f32[256,512]{1,0:T(8,128)S(1)} %get-tuple-element.99), channel_id=1, source_target_pairs={{0,4},{1,5},{2,6},{3,7},{4,0},{5,1},{6,2},{7,3},{8,12},{9,13},{10,... | collective-permute-start | bytes 1572872 | tf_op jit(solution)/shard_map/ppermute | solution.py:38
  117.6 32.0 %copy-start.9 = (f32[1024,512]{1,0:T(8,128)}, f32[1024,512]{1,0:T(8,128)S(1)}, u32[]{:S(2)}) copy-start(f32[1024,512]{1,0:T(8,128)S(1)} %collective-permute-done.7.refs_1_) | copy-start | bytes 6291460
  117.6 31.5 %collective-permute-start.9 = (f32[1024,512]{1,0:T(8,128)S(1)}, f32[1024,512]{1,0:T(8,128)S(1)}, u32[]{:S(2)}, u32[]{:S(2)}) collective-permute-start(f32[1024,512]{1,0:T(8,128)S(1)} %get-tuple-element.100), channel_id=1, source_target_pairs={{0,16},{1,17},{4,20},{5,21},{10,26},{11,27},{14,30},{15,31},{16,0}... | collective-permute-start | bytes 6291464 | tf_op jit(solution)/shard_map/ppermute | solution.py:38
  125.1 45.0 %collective-permute-start.12 = (f32[1024,512]{1,0:T(8,128)}, f32[1024,512]{1,0:T(8,128)S(1)}, u32[]{:S(2)}, u32[]{:S(2)}) collective-permute-start(f32[1024,512]{1,0:T(8,128)} %get-tuple-element.129.refs_0_), channel_id=1, source_target_pairs={{0,1},{1,0},{4,5},{5,4},{10,11},{11,10},{14,15},{15,14},{16,17},{1... | collective-permute-start | bytes 6291464 | tf_op jit(solution)/shard_map/ppermute | solution.py:38
  128.3 43.2 %collective-permute-start.13 = (f32[1024,512]{1,0:T(8,128)}, f32[1024,512]{1,0:T(8,128)S(1)}, u32[]{:S(2)}, u32[]{:S(2)}) collective-permute-start(f32[1024,512]{1,0:T(8,128)} %get-tuple-element.123.refs_0_), channel_id=1, source_target_pairs={{2,3},{3,2},{6,7},{7,6},{8,9},{9,8},{12,13},{13,12},{18,19},{19,18... | collective-permute-start | bytes 6291464 | tf_op jit(solution)/shard_map/ppermute | solution.py:38
  129.1 30.9 %collective-permute-start.10 = (f32[256,512]{1,0:T(8,128)}, f32[256,512]{1,0:T(8,128)S(1)}, u32[]{:S(2)}, u32[]{:S(2)}) collective-permute-start(f32[256,512]{1,0:T(8,128)} %get-tuple-element.101), channel_id=1, source_target_pairs={{0,4},{1,5},{2,6},{3,7},{4,0},{5,1},{6,2},{7,3},{8,12},{9,13},{10,... | collective-permute-start | bytes 1572872 | tf_op jit(solution)/shard_map/ppermute | solution.py:38
  130.9 39.2 %collective-permute-start.11 = (f32[256,512]{1,0:T(8,128)}, f32[256,512]{1,0:T(8,128)S(1)}, u32[]{:S(2)}, u32[]{:S(2)}) collective-permute-start(f32[256,512]{1,0:T(8,128)} %get-tuple-element.102), channel_id=1, source_target_pairs={{0,4},{1,5},{2,6},{3,7},{4,0},{5,1},{6,2},{7,3},{8,12},{9,13},{10,... | collective-permute-start | bytes 1572872 | tf_op jit(solution)/shard_map/ppermute | solution.py:38
  149.7 32.8 %copy-start = (bf16[1024,1024]{1,0:T(8,128)(2,1)S(1)}, bf16[1024,1024]{1,0:T(8,128)(2,1)}, u32[]{:S(2)}) copy-start(bf16[1024,1024]{1,0:T(8,128)(2,1)} %get-tuple-element.106.refs_5_.refs_8_) | copy-start | bytes 6291460
  173.0 14.1 %collective-permute-start.14 = (f32[2,1024,512]{2,1,0:T(8,128)}, f32[2,1024,512]{2,1,0:T(8,128)}, u32[]{:S(2)}, u32[]{:S(2)}) collective-permute-start(f32[2,1024,512]{2,1,0:T(8,128)} %pad_maximum_fusion), channel_id=1, source_target_pairs={{0,8},{1,9},{4,12},{5,13},{10,2},{11,3},{14,6},{15,7},{16,24},{17,... | collective-permute-start | bytes 12582920 | tf_op jit(solution)/shard_map/ppermute | solution.py:38
  176.3 32.4 %collective-permute-start.15 = (f32[1024,512]{1,0:T(8,128)}, f32[1024,512]{1,0:T(8,128)}, u32[]{:S(2)}, u32[]{:S(2)}) collective-permute-start(f32[1024,512]{1,0:T(8,128)} %get-tuple-element.115.refs_0_), channel_id=1, source_target_pairs={{0,1},{1,0},{4,5},{5,4},{10,11},{11,10},{14,15},{15,14},{16,17},{1... | collective-permute-start | bytes 6291464 | tf_op jit(solution)/shard_map/ppermute | solution.py:38
  180.3 46.8 %collective-permute-start.16 = (f32[1024,512]{1,0:T(8,128)}, f32[1024,512]{1,0:T(8,128)}, u32[]{:S(2)}, u32[]{:S(2)}) collective-permute-start(f32[1024,512]{1,0:T(8,128)} %get-tuple-element.113.refs_0_), channel_id=1, source_target_pairs={{0,1},{1,0},{4,5},{5,4},{10,11},{11,10},{14,15},{15,14},{16,17},{1... | collective-permute-start | bytes 6291464 | tf_op jit(solution)/shard_map/ppermute | solution.py:38
  184.0 61.1 %collective-permute-start.17 = (f32[256,512]{1,0:T(8,128)S(1)}, f32[256,512]{1,0:T(8,128)S(1)}, u32[]{:S(2)}, u32[]{:S(2)}) collective-permute-start(f32[256,512]{1,0:T(8,128)S(1)} %copy-done.68), channel_id=1, source_target_pairs={{0,4},{1,5},{2,6},{3,7},{4,0},{5,1},{6,2},{7,3},{8,12},{9,13},{10,... | collective-permute-start | bytes 1572872 | tf_op jit(solution)/shard_map/ppermute | solution.py:38
  184.1 61.0 %collective-permute-start.18 = (f32[256,512]{1,0:T(8,128)S(1)}, f32[256,512]{1,0:T(8,128)S(1)}, u32[]{:S(2)}, u32[]{:S(2)}) collective-permute-start(f32[256,512]{1,0:T(8,128)S(1)} %copy-done.67), channel_id=1, source_target_pairs={{0,4},{1,5},{2,6},{3,7},{4,0},{5,1},{6,2},{7,3},{8,12},{9,13},{10,... | collective-permute-start | bytes 1572872 | tf_op jit(solution)/shard_map/ppermute | solution.py:38
  192.2 68.3 %copy-start.3 = (f32[512,512]{1,0:T(8,128)}, f32[512,512]{1,0:T(8,128)S(1)}, u32[]{:S(2)}) copy-start(f32[512,512]{1,0:T(8,128)S(1)} %get-tuple-element.202.refs_2_.refs_3_) | copy-start | bytes 3145732
  246.2 4.8 collective-permute-start.19
  247.5 3.5 collective-permute-start.20
  249.0 65.1 %collective-permute-start.27 = (f32[1024,512]{1,0:T(8,128)}, f32[1024,512]{1,0:T(8,128)}, u32[]{:S(2)}, u32[]{:S(2)}) collective-permute-start(f32[1024,512]{1,0:T(8,128)} %get-tuple-element.129.refs_0_), channel_id=1, source_target_pairs={{2,3},{3,2},{6,7},{7,6},{8,9},{9,8},{12,13},{13,12},{18,19},{19,18... | collective-permute-start | bytes 6291464 | tf_op jit(solution)/shard_map/ppermute | solution.py:38
  252.6 24.8 %collective-permute-start.21 = (f32[512,512]{1,0:T(8,128)}, f32[512,512]{1,0:T(8,128)}, u32[]{:S(2)}, u32[]{:S(2)}) collective-permute-start(f32[512,512]{1,0:T(8,128)} %broadcast_multiply_fusion.1), channel_id=1, source_target_pairs={{0,1},{4,5},{10,11},{14,15},{17,16},{21,20},{27,26},{31,30}} | collective-permute-start | bytes 3145736 | tf_op jit(solution)/shard_map/ppermute | solution.py:38
  257.6 21.9 %collective-permute-start.22 = (f32[512,512]{1,0:T(8,128)}, f32[512,512]{1,0:T(8,128)}, u32[]{:S(2)}, u32[]{:S(2)}) collective-permute-start(f32[512,512]{1,0:T(8,128)} %broadcast_multiply_fusion.1), channel_id=1, source_target_pairs={{1,17},{5,21},{11,27},{15,31},{16,0},{20,4},{26,10},{30,14}} | collective-permute-start | bytes 3145736 | tf_op jit(solution)/shard_map/ppermute | solution.py:38
  258.9 33.2 %collective-permute-start.23 = (f32[512,512]{1,0:T(8,128)}, f32[512,512]{1,0:T(8,128)}, u32[]{:S(2)}, u32[]{:S(2)}) collective-permute-start(f32[512,512]{1,0:T(8,128)} %broadcast_multiply_fusion.1), channel_id=1, source_target_pairs={{1,16},{5,20},{11,26},{15,30},{16,1},{20,5},{26,11},{30,15}} | collective-permute-start | bytes 3145736 | tf_op jit(solution)/shard_map/ppermute | solution.py:38
  272.4 41.7 %collective-permute-start.24 = (f32[512,512]{1,0:T(8,128)}, f32[512,512]{1,0:T(8,128)}, u32[]{:S(2)}, u32[]{:S(2)}) collective-permute-start(f32[512,512]{1,0:T(8,128)} %get-tuple-element.117), channel_id=1, source_target_pairs={{0,16},{1,17},{2,18},{3,19},{4,20},{5,21},{6,22},{7,23},{8,24},{9,... | collective-permute-start | bytes 3145736 | tf_op jit(solution)/shard_map/ppermute | solution.py:38
  277.4 21.6 %collective-permute-start.25 = (f32[256,512]{1,0:T(8,128)}, f32[256,512]{1,0:T(8,128)}, u32[]{:S(2)}, u32[]{:S(2)}) collective-permute-start(f32[256,512]{1,0:T(8,128)} %get-tuple-element.118), channel_id=1, source_target_pairs={{0,4},{1,5},{2,6},{3,7},{4,0},{5,1},{6,2},{7,3},{8,12},{9,13},{10,... | collective-permute-start | bytes 1572872 | tf_op jit(solution)/shard_map/ppermute | solution.py:38
  279.5 34.7 %collective-permute-start.26 = (f32[256,512]{1,0:T(8,128)}, f32[256,512]{1,0:T(8,128)}, u32[]{:S(2)}, u32[]{:S(2)}) collective-permute-start(f32[256,512]{1,0:T(8,128)} %get-tuple-element.119), channel_id=1, source_target_pairs={{0,4},{1,5},{2,6},{3,7},{4,0},{5,1},{6,2},{7,3},{8,12},{9,13},{10,... | collective-permute-start | bytes 1572872 | tf_op jit(solution)/shard_map/ppermute | solution.py:38
  292.0 24.2 %copy-start.23 = (f32[256,512]{1,0:T(8,128)S(1)}, f32[256,512]{1,0:T(8,128)}, u32[]{:S(2)}) copy-start(f32[256,512]{1,0:T(8,128)} %copy-done.22) | copy-start | bytes 1572868
  292.1 24.2 %copy-start.25 = (f32[256,512]{1,0:T(8,128)S(1)}, f32[256,512]{1,0:T(8,128)}, u32[]{:S(2)}) copy-start(f32[256,512]{1,0:T(8,128)} %copy-done.24) | copy-start | bytes 1572868
  292.1 28.7 %copy-start.39 = (f32[1024,512]{1,0:T(8,128)S(1)}, f32[1024,512]{1,0:T(8,128)}, u32[]{:S(2)}) copy-start(f32[1024,512]{1,0:T(8,128)} %copy-done.38) | copy-start | bytes 6291460
  294.3 23.0 %copy-start.27 = (f32[256,512]{1,0:T(8,128)S(1)}, f32[256,512]{1,0:T(8,128)}, u32[]{:S(2)}) copy-start(f32[256,512]{1,0:T(8,128)} %copy-done.26) | copy-start | bytes 1572868
  294.3 23.0 %copy-start.32 = (f32[256,512]{1,0:T(8,128)S(1)}, f32[256,512]{1,0:T(8,128)}, u32[]{:S(2)}) copy-start(f32[256,512]{1,0:T(8,128)} %copy-done.31) | copy-start | bytes 1572868
  314.1 26.0 %collective-permute-start.29 = (f32[512,512]{1,0:T(8,128)S(1)}, f32[512,512]{1,0:T(8,128)S(1)}, u32[]{:S(2)}, u32[]{:S(2)}) collective-permute-start(f32[512,512]{1,0:T(8,128)S(1)} %select_select_fusion), channel_id=1, source_target_pairs={{0,4},{1,5},{4,0},{5,1},{10,14},{11,15},{14,10},{15,11},{16,20},{1... | collective-permute-start | bytes 3145736 | tf_op jit(solution)/shard_map/ppermute | solution.py:38
  318.3 51.9 %collective-permute-start.33 = (f32[512,512]{1,0:T(8,128)}, f32[512,512]{1,0:T(8,128)S(1)}, u32[]{:S(2)}, u32[]{:S(2)}) collective-permute-start(f32[512,512]{1,0:T(8,128)} %pad_maximum_fusion.5), channel_id=1, source_target_pairs={{0,1},{1,0},{2,3},{3,2},{4,5},{5,4},{6,7},{7,6},{8,9},{9,8},{10,11... | collective-permute-start | bytes 3145736 | tf_op jit(solution)/shard_map/ppermute | solution.py:38
  318.3 51.9 %collective-permute-start.32 = (f32[512,512]{1,0:T(8,128)}, f32[512,512]{1,0:T(8,128)S(1)}, u32[]{:S(2)}, u32[]{:S(2)}) collective-permute-start(f32[512,512]{1,0:T(8,128)} %pad_maximum_fusion.4), channel_id=1, source_target_pairs={{0,1},{1,0},{2,3},{3,2},{4,5},{5,4},{6,7},{7,6},{8,9},{9,8},{10,11... | collective-permute-start | bytes 3145736 | tf_op jit(solution)/shard_map/ppermute | solution.py:38
  320.3 49.9 %collective-permute-start.30 = (f32[512,512]{1,0:T(8,128)S(1)}, f32[512,512]{1,0:T(8,128)S(1)}, u32[]{:S(2)}, u32[]{:S(2)}) collective-permute-start(f32[512,512]{1,0:T(8,128)S(1)} %get-tuple-element.128), channel_id=1, source_target_pairs={{0,16},{1,17},{2,18},{3,19},{4,20},{5,21},{6,22},{7,23},{8,24},{9,... | collective-permute-start | bytes 3145736 | tf_op jit(solution)/shard_map/ppermute | solution.py:38
  330.9 39.4 %collective-permute-start.28 = (f32[512,512]{1,0:T(8,128)S(1)}, f32[512,512]{1,0:T(8,128)S(1)}, u32[]{:S(2)}, u32[]{:S(2)}) collective-permute-start(f32[512,512]{1,0:T(8,128)S(1)} %get-tuple-element.126), channel_id=1, source_target_pairs={{0,16},{1,17},{2,18},{3,19},{4,20},{5,21},{6,22},{7,23},{8,24},{9,... | collective-permute-start | bytes 3145736 | tf_op jit(solution)/shard_map/ppermute | solution.py:38
  340.2 30.0 %collective-permute-start.31 = (f32[256,512]{1,0:T(8,128)S(1)}, f32[256,512]{1,0:T(8,128)S(1)}, u32[]{:S(2)}, u32[]{:S(2)}) collective-permute-start(f32[256,512]{1,0:T(8,128)S(1)} %get-tuple-element.132), channel_id=1, source_target_pairs={{0,4},{1,5},{2,6},{3,7},{4,0},{5,1},{6,2},{7,3},{8,12},{9,13},{10,... | collective-permute-start | bytes 1572872 | tf_op jit(solution)/shard_map/ppermute | solution.py:38
  351.2 20.5 %copy-start.29 = (f32[256,512]{1,0:T(8,128)S(1)}, f32[256,512]{1,0:T(8,128)}, u32[]{:S(2)}) copy-start(f32[256,512]{1,0:T(8,128)} %copy-done.28) | copy-start | bytes 1572868
  351.2 20.5 %copy-start.34 = (f32[256,512]{1,0:T(8,128)S(1)}, f32[256,512]{1,0:T(8,128)}, u32[]{:S(2)}) copy-start(f32[256,512]{1,0:T(8,128)} %copy-done.33) | copy-start | bytes 1572868
  351.4 23.4 %copy-start.66 = (f32[1,1024,512]{2,1,0:T(8,128)S(1)}, f32[1,1024,512]{2,1,0:T(8,128)}, u32[]{:S(2)}) copy-start(f32[1,1024,512]{2,1,0:T(8,128)} %get-tuple-element.189) | copy-start | bytes 6291460
  370.3 24.8 %collective-permute-start.34 = (f32[2,512,512]{2,1,0:T(8,128)S(1)}, f32[2,512,512]{2,1,0:T(8,128)S(1)}, u32[]{:S(2)}, u32[]{:S(2)}) collective-permute-start(f32[2,512,512]{2,1,0:T(8,128)S(1)} %pad_maximum_fusion.2), channel_id=1, source_target_pairs={{0,2},{1,3},{4,6},{5,7},{10,8},{11,9},{14,12},{15,13},{16,18},{17,... | collective-permute-start | bytes 6291464 | tf_op jit(solution)/shard_map/ppermute | solution.py:38
  372.8 22.8 %collective-permute-start.36 = (f32[512,512]{1,0:T(8,128)}, f32[512,512]{1,0:T(8,128)S(1)}, u32[]{:S(2)}, u32[]{:S(2)}) collective-permute-start(f32[512,512]{1,0:T(8,128)} %pad_maximum_fusion.6), channel_id=1, source_target_pairs={{0,1},{1,0},{2,3},{3,2},{4,5},{5,4},{6,7},{7,6},{8,9},{9,8},{10,11... | collective-permute-start | bytes 3145736 | tf_op jit(solution)/shard_map/ppermute | solution.py:38
  372.8 22.8 %collective-permute-start.35 = (f32[512,512]{1,0:T(8,128)S(1)}, f32[512,512]{1,0:T(8,128)S(1)}, u32[]{:S(2)}, u32[]{:S(2)}) collective-permute-start(f32[512,512]{1,0:T(8,128)S(1)} %get-tuple-element.143), channel_id=1, source_target_pairs={{0,16},{1,17},{2,18},{3,19},{4,20},{5,21},{6,22},{7,23},{8,24},{9,... | collective-permute-start | bytes 3145736 | tf_op jit(solution)/shard_map/ppermute | solution.py:38
  380.0 38.4 %collective-permute-start.38 = (f32[512,512]{1,0:T(8,128)}, f32[512,512]{1,0:T(8,128)S(1)}, u32[]{:S(2)}, u32[]{:S(2)}) collective-permute-start(f32[512,512]{1,0:T(8,128)} %pad_maximum_fusion.7), channel_id=1, source_target_pairs={{0,4},{1,5},{2,6},{3,7},{4,0},{5,1},{6,2},{7,3},{8,12},{9,13},{10,... | collective-permute-start | bytes 3145736 | tf_op jit(solution)/shard_map/ppermute | solution.py:38
  395.6 23.7 %collective-permute-start.39 = (f32[512,512]{1,0:T(8,128)S(1)}, f32[512,512]{1,0:T(8,128)S(1)}, u32[]{:S(2)}, u32[]{:S(2)}) collective-permute-start(f32[512,512]{1,0:T(8,128)S(1)} %pad_maximum_fusion.8), channel_id=1, source_target_pairs={{0,1},{1,0},{2,3},{3,2},{4,5},{5,4},{6,7},{7,6},{8,9},{9,8},{10,11... | collective-permute-start | bytes 3145736 | tf_op jit(solution)/shard_map/ppermute | solution.py:38
  395.7 24.6 %collective-permute-start.37 = (f32[512,512]{1,0:T(8,128)S(1)}, f32[512,512]{1,0:T(8,128)S(1)}, u32[]{:S(2)}, u32[]{:S(2)}) collective-permute-start(f32[512,512]{1,0:T(8,128)S(1)} %get-tuple-element.146), channel_id=1, source_target_pairs={{0,16},{1,17},{2,18},{3,19},{4,20},{5,21},{6,22},{7,23},{8,24},{9,... | collective-permute-start | bytes 3145736 | tf_op jit(solution)/shard_map/ppermute | solution.py:38
  421.3 33.1 %collective-permute-start.40 = (f32[1024,512]{1,0:T(8,128)}, f32[1024,512]{1,0:T(8,128)}, u32[]{:S(2)}, u32[]{:S(2)}) collective-permute-start(f32[1024,512]{1,0:T(8,128)} %get-tuple-element.150), channel_id=1, source_target_pairs={{0,16},{4,20},{10,26},{14,30},{17,1},{21,5},{27,11},{31,15}} | collective-permute-start | bytes 6291464 | tf_op jit(solution)/shard_map/ppermute | solution.py:38
  424.6 36.6 %collective-permute-start.41 = (f32[256,512]{1,0:T(8,128)}, f32[256,512]{1,0:T(8,128)}, u32[]{:S(2)}, u32[]{:S(2)}) collective-permute-start(f32[256,512]{1,0:T(8,128)} %get-tuple-element.156), channel_id=1, source_target_pairs={{0,4},{1,5},{2,6},{3,7},{4,0},{5,1},{6,2},{7,3},{8,12},{9,13},{10,... | collective-permute-start | bytes 1572872 | tf_op jit(solution)/shard_map/ppermute | solution.py:38
  461.2 5.9 collective-permute-start.42
  464.6 26.3 %collective-permute-start.44 = (f32[512,512]{1,0:T(8,128)}, f32[512,512]{1,0:T(8,128)S(1)}, u32[]{:S(2)}, u32[]{:S(2)}) collective-permute-start(f32[512,512]{1,0:T(8,128)} %copy-done.62), channel_id=1, source_target_pairs={{0,16},{1,17},{2,18},{3,19},{4,20},{5,21},{6,22},{7,23},{8,24},{9,... | collective-permute-start | bytes 3145736 | tf_op jit(solution)/shard_map/ppermute | solution.py:38
  479.3 34.1 %collective-permute-start.43 = (f32[512,512]{1,0:T(8,128)S(1)}, f32[512,512]{1,0:T(8,128)S(1)}, u32[]{:S(2)}, u32[]{:S(2)}) collective-permute-start(f32[512,512]{1,0:T(8,128)S(1)} %get-tuple-element.161), channel_id=1, source_target_pairs={{0,16},{1,17},{2,18},{3,19},{4,20},{5,21},{6,22},{7,23},{8,24},{9,... | collective-permute-start | bytes 3145736 | tf_op jit(solution)/shard_map/ppermute | solution.py:38
  479.5 94.1 %collective-permute-start.47 = (f32[1024,512]{1,0:T(8,128)S(1)}, f32[1024,512]{1,0:T(8,128)S(1)}, u32[]{:S(2)}, u32[]{:S(2)}) collective-permute-start(f32[1024,512]{1,0:T(8,128)S(1)} %pad_maximum_fusion.3), channel_id=1, source_target_pairs={{0,4},{1,5},{2,6},{3,7},{4,0},{5,1},{6,2},{7,3},{8,12},{9,13},{10,... | collective-permute-start | bytes 6291464 | tf_op jit(solution)/shard_map/ppermute | solution.py:38
  490.9 22.5 %copy-start.17 = (f32[512,512]{1,0:T(8,128)S(1)}, f32[512,512]{1,0:T(8,128)}, u32[]{:S(2)}) copy-start(f32[512,512]{1,0:T(8,128)} %copy-done.15) | copy-start | bytes 3145732
  490.9 22.5 %copy-start.49 = (f32[512,512]{1,0:T(8,128)S(1)}, f32[512,512]{1,0:T(8,128)}, u32[]{:S(2)}) copy-start(f32[512,512]{1,0:T(8,128)} %copy-done.48) | copy-start | bytes 3145732
  490.9 22.4 %copy-start.61 = (f32[256,512]{1,0:T(8,128)S(1)}, f32[256,512]{1,0:T(8,128)}, u32[]{:S(2)}) copy-start(f32[256,512]{1,0:T(8,128)} %copy-done.60) | copy-start | bytes 1572868
  499.2 36.6 %collective-permute-start.45 = (f32[512,512]{1,0:T(8,128)S(1)}, f32[512,512]{1,0:T(8,128)S(1)}, u32[]{:S(2)}, u32[]{:S(2)}) collective-permute-start(f32[512,512]{1,0:T(8,128)S(1)} %get-tuple-element.167), channel_id=1, source_target_pairs={{0,16},{1,17},{2,18},{3,19},{4,20},{5,21},{6,22},{7,23},{8,24},{9,... | collective-permute-start | bytes 3145736 | tf_op jit(solution)/shard_map/ppermute | solution.py:38
  522.9 32.4 %collective-permute-start.46 = (f32[512,512]{1,0:T(8,128)S(1)}, f32[512,512]{1,0:T(8,128)S(1)}, u32[]{:S(2)}, u32[]{:S(2)}) collective-permute-start(f32[512,512]{1,0:T(8,128)S(1)} %get-tuple-element.171), channel_id=1, source_target_pairs={{0,16},{1,17},{2,18},{3,19},{4,20},{5,21},{6,22},{7,23},{8,24},{9,... | collective-permute-start | bytes 3145736 | tf_op jit(solution)/shard_map/ppermute | solution.py:38
  582.2 25.3 %collective-permute-start.48 = (f32[512,512]{1,0:T(8,128)S(1)}, f32[512,512]{1,0:T(8,128)S(1)}, u32[]{:S(2)}, u32[]{:S(2)}) collective-permute-start(f32[512,512]{1,0:T(8,128)S(1)} %get-tuple-element.176), channel_id=1, source_target_pairs={{0,16},{1,17},{2,18},{3,19},{4,20},{5,21},{6,22},{7,23},{8,24},{9,... | collective-permute-start | bytes 3145736 | tf_op jit(solution)/shard_map/ppermute | solution.py:38
  (54 other events, 216.2 us)

commit v4 on v3

--- a/solution.py
+++ b/solution.py
@@ -485,8 +485,11 @@
     columns = jnp.where(grid.row_high == grid.parity, columns, arrived)
     columns = after(columns, far_near[early[1]], late_quarter)
     far_move(early[1], columns)
-    send_late(late[1], jnp.concatenate((near[late[1]], moved[late[1]]), axis=0), columns)
+    first_quarter = send_late(late[1], near[late[1]][:middle], columns)
     weights = weights_of(grid.spread_row_group(columns), grid.col_high)
+    weights = [after(weight, first_quarter) for weight in weights]
+    parts = (near[late[1]][middle:], moved[late[1]])
+    send_late(late[1], jnp.concatenate(parts, axis=0), first_quarter)
 
     outputs = [None] * count
     before = [far_moved[early[1]]]

time: 620 us -> 617 us (level)
  waiting for transfers between devices: 240 us -> 230 us
    ppermute x49 -> x50, waiting for transfers between devices: 240 us -> 230 us  [send(): return lax.ppermute(value, ('row', 'col'), pairs)]
    ppermute x49 -> x50, starting transfers between devices: 114 us -> 119 us  [send(): return lax.ppermute(value, ('row', 'col'), pairs)]
    unnamed x138 -> x140, local copies, waits for them, and re-layouts: 22.5 us -> 19.7 us
  transfers between devices with their start and end apart: 49 -> 50, of which waited for: 23 -> 22; matrix products, arithmetic and copies ran while one was open for 9% -> 9% of each run, Pallas kernels for 27% -> 27%
where the time goes in v4:
time: 617 us; the launch traced here: 607 us
  waiting for transfers between devices  230 us (37%)
  Pallas kernels  174 us (28%)
  starting transfers between devices  119 us (19%)
  other arithmetic  44.8 us (7%)
  local copies, waits for them, and re-layouts  37.2 us (6%)
    ppermute x50, waiting for transfers between devices, send(): return lax.ppermute(value, ('row', 'col'), pairs)  230 us
    pallas_call x14, Pallas kernels, rotate(): pl.pallas_call(functools.partial(rotate_kernel, tuple(spans), per_half),...  134 us
    ppermute x50, starting transfers between devices, send(): return lax.ppermute(value, ('row', 'col'), pairs)  119 us
    pallas_call x2, Pallas kernels, rotation_of(): pl.pallas_call(rotation_kernel, out_shape=(jax.ShapeDtypeStruct((size, wi...  40.1 us
    unnamed x140, local copies, waits for them, and re-layouts  19.7 us
  transfers between devices with their start and end apart: 50, of which 22 were waited for; matrix products, arithmetic and copies ran while one was open for 9% of the time, Pallas kernels for 27%

profile of v4, /device:TPU:0, one launch (start us, length us, event | category | flops | bytes accessed | tf_op | source)
XLA Modules:
  0.0 606.5 jit_solution(3826193239813051623)
XLA Ops:
  0.1 2.8 select_reduce_fusion.1
  2.9 4.8 collective-permute-start
  7.7 7.0 %slice_bitcast_fusion = (f32[1024,512]{1,0:T(8,128)}, f32[1024,512]{1,0:T(8,128)}, f32[1024,512]{1,0:T(8,128)}, f32[1024,512]{1,0:T(8,128)}) fusion(f32[4,1024,512]{2,1,0:T(8,128)} %param.1), kind=kLoop, calls=%fused_computation.7 | loop fusion | bytes 16777216 | tf_op jit(solution)/shard_map/squeeze | solution.py:351
  15.5 4.1 multiply_reduce_fusion
  21.4 2.8 collective-permute-start.1
  24.2 11.4 %collective-permute-done.1 = f32[512,512]{1,0:T(8,128)} collective-permute-done((f32[512,512]{1,0:T(8,128)S(1)}, f32[512,512]{1,0:T(8,128)}, u32[]{:S(2)}, u32[]{:S(2)}) %collective-permute-start.1) | collective-permute-done | bytes 1048608 | tf_op jit(solution)/shard_map/ppermute | solution.py:38
  39.5 8.4 %collective-permute-start.3 = (f32[512,512]{1,0:T(8,128)S(1)}, f32[512,512]{1,0:T(8,128)}, u32[]{:S(2)}, u32[]{:S(2)}) collective-permute-start(f32[512,512]{1,0:T(8,128)S(1)} %broadcast_select_fusion.6), channel_id=1, source_target_pairs={{0,2},{1,3},{4,6},{5,7},{10,8},{11,9},{14,12},{15,13},{16,18},{17,... | collective-permute-start | bytes 3145736 | tf_op jit(solution)/shard_map/ppermute | solution.py:38
  47.9 11.3 %collective-permute-done.3 = f32[512,512]{1,0:T(8,128)} collective-permute-done((f32[512,512]{1,0:T(8,128)S(1)}, f32[512,512]{1,0:T(8,128)}, u32[]{:S(2)}, u32[]{:S(2)}) %collective-permute-start.3) | collective-permute-done | bytes 1048608 | tf_op jit(solution)/shard_map/ppermute | solution.py:38
  60.1 4.1 slice_bitcast_fusion.6
  64.2 2.6 collective-permute-start.6
  66.8 13.5 %collective-permute-done.6.refs_0_ = f32[256,512]{1,0:T(8,128)S(1)} collective-permute-done((f32[256,512]{1,0:T(8,128)S(1)}, f32[256,512]{1,0:T(8,128)S(1)}, u32[]{:S(2)}, u32[]{:S(2)}) %collective-permute-start.6) | collective-permute-done | bytes 524320 | tf_op jit(solution)/shard_map/ppermute | solution.py:38
  81.7 9.4 %collective-permute-start.7 = (f32[1024,512]{1,0:T(8,128)}, f32[1024,512]{1,0:T(8,128)S(1)}, u32[]{:S(2)}, u32[]{:S(2)}) collective-permute-start(f32[1024,512]{1,0:T(8,128)} %get-tuple-element.126.refs_0_), channel_id=1, source_target_pairs={{0,1},{1,0},{4,5},{5,4},{10,11},{11,10},{14,15},{15,14},{16,17},{1... | collective-permute-start | bytes 6291464 | tf_op jit(solution)/shard_map/ppermute | solution.py:38
  91.5 19.8 %shard_map.17 = (f32[1024,512]{1,0:T(8,128)S(1)}, bf16[1024,1024]{1,0:T(8,128)(2,1)}, bf16[1024,1024]{1,0:T(8,128)(2,1)}) custom-call(s32[3]{0:T(128)S(1)} %pad_add_fusion.flags_ref, f32[512,512]{1,0:T(8,128)S(1)} %get-tuple-element.210.first_ref, f32[512,512]{1,0:T(8,128)S(1)} %get-tuple-element.209.second_ref), custom_call_target="tpu_custom_call" | custom-call | tf_op jit(solution)/shard_map/pallas_call | solution.py:179
  111.3 6.4 %collective-permute-done.8.refs_1_ = f32[256,512]{1,0:T(8,128)S(1)} collective-permute-done((f32[256,512]{1,0:T(8,128)S(1)}, f32[256,512]{1,0:T(8,128)S(1)}, u32[]{:S(2)}, u32[]{:S(2)}) %collective-permute-start.8) | collective-permute-done | bytes 524320 | tf_op jit(solution)/shard_map/ppermute | solution.py:38
  117.7 7.4 %collective-permute-start.9 = (f32[1024,512]{1,0:T(8,128)S(1)}, f32[1024,512]{1,0:T(8,128)S(1)}, u32[]{:S(2)}, u32[]{:S(2)}) collective-permute-start(f32[1024,512]{1,0:T(8,128)S(1)} %get-tuple-element.103), channel_id=1, source_target_pairs={{0,16},{1,17},{4,20},{5,21},{10,26},{11,27},{14,30},{15,31},{16,0}... | collective-permute-start | bytes 6291464 | tf_op jit(solution)/shard_map/ppermute | solution.py:38
  125.1 3.2 collective-permute-start.12
  132.0 17.0 %collective-permute-done.9 = f32[1024,512]{1,0:T(8,128)S(1)} collective-permute-done((f32[1024,512]{1,0:T(8,128)S(1)}, f32[1024,512]{1,0:T(8,128)S(1)}, u32[]{:S(2)}, u32[]{:S(2)}) %collective-permute-start.9) | collective-permute-done | bytes 2097184 | tf_op jit(solution)/shard_map/ppermute | solution.py:38
  149.7 2.5 pad_maximum_fusion
  152.1 7.9 %collective-permute-done.10.refs_2_ = f32[256,512]{1,0:T(8,128)S(1)} collective-permute-done((f32[256,512]{1,0:T(8,128)}, f32[256,512]{1,0:T(8,128)S(1)}, u32[]{:S(2)}, u32[]{:S(2)}) %collective-permute-start.10) | collective-permute-done | bytes 524320 | tf_op jit(solution)/shard_map/ppermute | solution.py:38
  160.0 10.1 %collective-permute-done.11.refs_3_ = f32[256,512]{1,0:T(8,128)S(1)} collective-permute-done((f32[256,512]{1,0:T(8,128)}, f32[256,512]{1,0:T(8,128)S(1)}, u32[]{:S(2)}, u32[]{:S(2)}) %collective-permute-start.11) | collective-permute-done | bytes 524320 | tf_op jit(solution)/shard_map/ppermute | solution.py:38
  173.0 3.3 collective-permute-start.14
  176.4 4.0 collective-permute-start.15
  180.4 2.2 collective-permute-start.16
  184.2 2.9 collective-permute-start.18
  187.1 3.2 broadcast_select_fusion
  194.1 7.4 %shard_map.18 = f32[512,512]{1,0:T(8,128)S(1)} custom-call(f32[1024,512]{1,0:T(8,128)} %get-tuple-element.126.refs_0_, f32[1024,512]{1,0:T(8,128)S(1)} %copy-done.10, f32[512,512]{1,0:T(8,128)S(1)} %get-tuple-element.208.refs_2_.refs_3_, f32[512,512]{1,0:T(8,128)S(1)} %get-tuple-element.207.refs_3_.refs_4_, ...), custom_call_target="tpu_custom_call" | custom-call | tf_op jit(solution)/shard_map/pallas_call | solution.py:277
  201.5 7.2 %shard_map.19 = f32[512,512]{1,0:T(8,128)S(1)} custom-call(f32[1024,512]{1,0:T(8,128)} %get-tuple-element.132.refs_0_, f32[1024,512]{1,0:T(8,128)S(1)} %copy-done.13, f32[512,512]{1,0:T(8,128)S(1)} %get-tuple-element.208.refs_2_.refs_3_, f32[512,512]{1,0:T(8,128)S(1)} %get-tuple-element.207.refs_3_.refs_4_, ...), custom_call_target="tpu_custom_call" | custom-call | tf_op jit(solution)/shard_map/pallas_call | solution.py:277
  208.7 7.6 %shard_map.20 = f32[512,512]{1,0:T(8,128)S(1)} custom-call(f32[1024,512]{1,0:T(8,128)} %get-tuple-element.118.refs_0_, f32[1024,512]{1,0:T(8,128)} %collective-permute-done.15.refs_1_, f32[512,512]{1,0:T(8,128)S(1)} %get-tuple-element.208.refs_2_.refs_3_, f32[512,512]{1,0:T(8,128)S(1)} %get-tuple-element.207.refs_3_.refs_4_, ...), custom_call_target="tpu_custom_call" | custom-call | tf_op jit(solution)/shard_map/pallas_call | solution.py:277
  216.4 10.8 %collective-permute-done.16.refs_1_ = f32[1024,512]{1,0:T(8,128)} collective-permute-done((f32[1024,512]{1,0:T(8,128)}, f32[1024,512]{1,0:T(8,128)}, u32[]{:S(2)}, u32[]{:S(2)}) %collective-permute-start.16) | collective-permute-done | bytes 2097184 | tf_op jit(solution)/shard_map/ppermute | solution.py:38
  227.2 17.6 %shard_map.21 = f32[512,512]{1,0:T(8,128)S(1)} custom-call(f32[1024,512]{1,0:T(8,128)} %get-tuple-element.116.refs_0_, f32[1024,512]{1,0:T(8,128)} %collective-permute-done.16.refs_1_, f32[512,512]{1,0:T(8,128)S(1)} %get-tuple-element.208.refs_2_.refs_3_, f32[512,512]{1,0:T(8,128)S(1)} %get-tuple-element.207.refs_3_.refs_4_, ...), custom_call_target="tpu_custom_call" | custom-call | tf_op jit(solution)/shard_map/pallas_call | solution.py:277
  252.7 5.0 collective-permute-start.21
  260.7 10.9 %shard_map.23 = (f32[512,512]{1,0:T(8,128)S(1)}, f32[512,512]{1,0:T(8,128)}) custom-call(f32[1024,512]{1,0:T(8,128)} %get-tuple-element.118.refs_0_, f32[1024,512]{1,0:T(8,128)} %collective-permute-done.15.refs_1_, f32[1024,512]{1,0:T(8,128)S(1)} %copy-done.37, f32[512,512]{1,0:T(8,128)S(1)} %get-tuple-element.208.refs_2_.refs_3_, ...), custom_call_target="tpu_custom_call" | custom-call | tf_op jit(solution)/shard_map/pallas_call | solution.py:277
  272.5 5.0 collective-permute-start.24
  281.7 10.4 %shard_map.22 = (f32[512,512]{1,0:T(8,128)S(1)}, f32[512,512]{1,0:T(8,128)S(1)}) custom-call(f32[1024,512]{1,0:T(8,128)} %get-tuple-element.116.refs_0_, f32[1024,512]{1,0:T(8,128)} %collective-permute-done.16.refs_1_, f32[1024,512]{1,0:T(8,128)} %collective-permute-done.4.refs_2_, f32[512,512]{1,0:T(8,128)S(1)} %copy-done.4, ...), custom_call_target="tpu_custom_call" | custom-call | tf_op jit(solution)/shard_map/pallas_call | solution.py:277
  292.2 2.1 select_select_fusion
  294.4 4.8 collective-permute-done.25.refs_2_
  299.2 15.1 %collective-permute-done.26.refs_3_ = f32[256,512]{1,0:T(8,128)} collective-permute-done((f32[256,512]{1,0:T(8,128)}, f32[256,512]{1,0:T(8,128)}, u32[]{:S(2)}, u32[]{:S(2)}) %collective-permute-start.26) | collective-permute-done | bytes 524320 | tf_op jit(solution)/shard_map/ppermute | solution.py:38
  314.2 2.1 collective-permute-start.29
  320.7 10.1 %shard_map.24 = (f32[512,512]{1,0:T(8,128)S(1)}, f32[512,512]{1,0:T(8,128)S(1)}) custom-call(f32[1024,512]{1,0:T(8,128)} %get-tuple-element.126.refs_0_, f32[1024,512]{1,0:T(8,128)S(1)} %copy-done.11, f32[1024,512]{1,0:T(8,128)S(1)} %copy-done.39, f32[512,512]{1,0:T(8,128)S(1)} %copy-done.4, f32[512,512]{1,0:T(8,128)S(1)} %get-tuple-element.207.refs_3_.refs_4_, ...), custom_call_target="tpu_custom_call" | custom-call | tf_op jit(solution)/shard_map/pallas_call | solution.py:277
  332.7 7.3 %collective-permute-done.29 = f32[512,512]{1,0:T(8,128)S(1)} collective-permute-done((f32[512,512]{1,0:T(8,128)S(1)}, f32[512,512]{1,0:T(8,128)S(1)}, u32[]{:S(2)}, u32[]{:S(2)}) %collective-permute-start.29) | collective-permute-done | bytes 1048608 | tf_op jit(solution)/shard_map/ppermute | solution.py:38
  340.0 10.0 %shard_map.25 = (f32[512,512]{1,0:T(8,128)S(1)}, f32[512,512]{1,0:T(8,128)S(1)}) custom-call(f32[1024,512]{1,0:T(8,128)} %get-tuple-element.132.refs_0_, f32[1024,512]{1,0:T(8,128)S(1)} %copy-done.14, f32[1024,512]{1,0:T(8,128)} %collective-permute-done.27.refs_2_, f32[512,512]{1,0:T(8,128)S(1)} %copy-done.4, ...), custom_call_target="tpu_custom_call" | custom-call | tf_op jit(solution)/shard_map/pallas_call | solution.py:277
  351.2 19.0 %collective-permute-done.31.refs_2_ = f32[256,512]{1,0:T(8,128)S(1)} collective-permute-done((f32[256,512]{1,0:T(8,128)S(1)}, f32[256,512]{1,0:T(8,128)S(1)}, u32[]{:S(2)}, u32[]{:S(2)}) %collective-permute-start.31) | collective-permute-done | bytes 524320 | tf_op jit(solution)/shard_map/ppermute | solution.py:38
  376.7 2.2 fusion.2
  380.0 8.5 %shard_map.26 = (f32[512,512]{1,0:T(8,128)S(1)}, f32[512,512]{1,0:T(8,128)S(1)}) custom-call(f32[256,512]{1,0:T(8,128)S(1)} %copy-done.23, f32[256,512]{1,0:T(8,128)S(1)} %copy-done.25, f32[256,512]{1,0:T(8,128)S(1)} %copy-done.27, f32[256,512]{1,0:T(8,128)S(1)} %copy-done.32, f32[512,512]{1,0:T(8,128)S(1)} %collective-permute-done.32.refs_4_, ...), custom_call_target="tpu_custom_call" | custom-call | tf_op jit(solution)/shard_map/pallas_call | solution.py:277
  388.5 6.6 %collective-permute-done.34 = f32[2,512,512]{2,1,0:T(8,128)S(1)} collective-permute-done((f32[2,512,512]{2,1,0:T(8,128)S(1)}, f32[2,512,512]{2,1,0:T(8,128)S(1)}, u32[]{:S(2)}, u32[]{:S(2)}) %collective-permute-start.34) | collective-permute-done | bytes 2097184 | tf_op jit(solution)/shard_map/ppermute | solution.py:38
  398.0 20.3 %shard_map.27 = (f32[1024,512]{1,0:T(8,128)}, bf16[1024,1024]{1,0:T(8,128)(2,1)}, bf16[1024,1024]{1,0:T(8,128)(2,1)}) custom-call(s32[3]{0:T(128)S(1)} %pad_add_fusion.1.flags_ref, f32[512,512]{1,0:T(8,128)S(1)} %get-tuple-element.202.first_ref, f32[512,512]{1,0:T(8,128)S(1)} %get-tuple-element.201.second_ref), custom_call_target="tpu_custom_call" | custom-call | tf_op jit(solution)/shard_map/pallas_call | solution.py:179
  421.3 3.3 collective-permute-start.40
  424.6 12.9 %collective-permute-start.41 = (f32[256,512]{1,0:T(8,128)}, f32[256,512]{1,0:T(8,128)}, u32[]{:S(2)}, u32[]{:S(2)}) collective-permute-start(f32[256,512]{1,0:T(8,128)} %get-tuple-element.159), channel_id=1, source_target_pairs={{0,4},{1,5},{2,6},{3,7},{4,0},{5,1},{6,2},{7,3},{8,12},{9,13},{10,... | collective-permute-start | bytes 1572872 | tf_op jit(solution)/shard_map/ppermute | solution.py:38
  444.8 9.5 %shard_map.28 = (f32[512,512]{1,0:T(8,128)S(1)}, f32[512,512]{1,0:T(8,128)S(1)}) custom-call(f32[256,512]{1,0:T(8,128)S(1)} %copy-done.30, f32[256,512]{1,0:T(8,128)S(1)} %copy-done.35, f32[256,512]{1,0:T(8,128)} %collective-permute-done.25.refs_2_, f32[256,512]{1,0:T(8,128)} %collective-permute-done.26.refs_3_, f32[512,512]{1,0:T(8,128)S(1)} %copy-done.57, ...), custom_call_target="tpu_custom_call" | custom-call | tf_op jit(solution)/shard_map/pallas_call | solution.py:277
  454.4 4.2 broadcast_select_fusion.1
  458.6 2.7 collective-permute-done.41.refs_4_
  461.2 3.5 collective-permute-start.42
  464.9 3.9 collective-permute-start.43
  468.8 2.3 broadcast_select_fusion.2
  471.3 17.7 %collective-permute-done.43.refs_2_ = f32[256,512]{1,0:T(8,128)S(1)} collective-permute-done((f32[256,512]{1,0:T(8,128)S(1)}, f32[256,512]{1,0:T(8,128)S(1)}, u32[]{:S(2)}, u32[]{:S(2)}) %collective-permute-start.43) | collective-permute-done | bytes 524320 | tf_op jit(solution)/shard_map/ppermute | solution.py:38
  489.1 8.5 %shard_map.29 = (f32[512,512]{1,0:T(8,128)S(1)}, f32[512,512]{1,0:T(8,128)S(1)}) custom-call(f32[512,512]{1,0:T(8,128)S(1)} %copy-done.43, f32[512,512]{1,0:T(8,128)S(1)} %copy-done.45, f32[512,512]{1,0:T(8,128)S(1)} %copy-done.51, f32[512,512]{1,0:T(8,128)S(1)} %copy-done.53, f32[512,512]{1,0:T(8,128)S(1)} %get-tuple-element.179.refs_4_.refs_5_, ...), custom_call_target="tpu_custom_call" | custom-call | tf_op jit(solution)/shard_map/pallas_call | solution.py:277
  500.7 8.3 %shard_map.30 = (f32[512,512]{1,0:T(8,128)S(1)}, f32[512,512]{1,0:T(8,128)S(1)}) custom-call(f32[512,512]{1,0:T(8,128)S(1)} %copy-done.41, f32[512,512]{1,0:T(8,128)S(1)} %copy-done.47, f32[512,512]{1,0:T(8,128)S(1)} %copy-done.55, f32[512,512]{1,0:T(8,128)S(1)} %collective-permute-done.45.refs_3_, f32[512,512]{1,0:T(8,128)S(1)} %get-tuple-element.179.refs_4_.refs_5_, ...), custom_call_target="tpu_custom_call" | custom-call | tf_op jit(solution)/shard_map/pallas_call | solution.py:277
  510.0 13.7 %collective-permute-done.44 = f32[512,512]{1,0:T(8,128)S(1)} collective-permute-done((f32[512,512]{1,0:T(8,128)S(1)}, f32[512,512]{1,0:T(8,128)S(1)}, u32[]{:S(2)}, u32[]{:S(2)}) %collective-permute-start.44) | collective-permute-done | bytes 1048608 | tf_op jit(solution)/shard_map/ppermute | solution.py:38
  523.8 9.6 %shard_map.31 = (f32[512,512]{1,0:T(8,128)S(1)}, f32[512,512]{1,0:T(8,128)S(1)}) custom-call(f32[512,512]{1,0:T(8,128)S(1)} %copy-done.21, f32[512,512]{1,0:T(8,128)} %collective-permute-done.24.refs_1_, f32[256,512]{1,0:T(8,128)S(1)} %copy-done.61, f32[512,512]{1,0:T(8,128)S(1)} %copy-done.49, f32[256,512]{1,0:T(8,128)} %collective-permute-done.41.refs_4_, ...), custom_call_target="tpu_custom_call" | custom-call | tf_op jit(solution)/shard_map/pallas_call | solution.py:277
  537.5 8.8 %collective-permute-done.46 = f32[512,512]{1,0:T(8,128)S(1)} collective-permute-done((f32[512,512]{1,0:T(8,128)S(1)}, f32[512,512]{1,0:T(8,128)S(1)}, u32[]{:S(2)}, u32[]{:S(2)}) %collective-permute-start.46) | collective-permute-done | bytes 1048608 | tf_op jit(solution)/shard_map/ppermute | solution.py:38
  546.2 21.1 %collective-permute-done.47 = f32[512,512]{1,0:T(8,128)S(1)} collective-permute-done((f32[512,512]{1,0:T(8,128)S(1)}, f32[512,512]{1,0:T(8,128)S(1)}, u32[]{:S(2)}, u32[]{:S(2)}) %collective-permute-start.47) | collective-permute-done | bytes 1048608 | tf_op jit(solution)/shard_map/ppermute | solution.py:38
  567.3 2.7 collective-permute-done.48.refs_3_
  570.0 8.6 %shard_map.32 = (f32[512,512]{1,0:T(8,128)S(1)}, f32[512,512]{1,0:T(8,128)S(1)}) custom-call(f32[512,512]{1,0:T(8,128)S(1)} %copy-done.18, f32[512,512]{1,0:T(8,128)S(1)} %copy-done.16, f32[256,512]{1,0:T(8,128)S(1)} %collective-permute-done.43.refs_2_, f32[768,512]{1,0:T(8,128)S(1)} %collective-permute-done.48.refs_3_, ...), custom_call_target="tpu_custom_call" | custom-call | tf_op jit(solution)/shard_map/pallas_call | solution.py:277
  583.7 20.0 %collective-permute-done.49 = f32[512,512]{1,0:T(8,128)S(1)} collective-permute-done((f32[512,512]{1,0:T(8,128)S(1)}, f32[512,512]{1,0:T(8,128)S(1)}, u32[]{:S(2)}, u32[]{:S(2)}) %collective-permute-start.49) | collective-permute-done | bytes 1048608 | tf_op jit(solution)/shard_map/ppermute | solution.py:38
  (242 shorter events, 81.8 us)
Async XLA Ops:
  2.9 11.8 %collective-permute-start = (f32[4,512]{1,0:T(4,128)S(1)}, f32[4,512]{1,0:T(4,128)S(1)}, u32[]{:S(2)}, u32[]{:S(2)}) collective-permute-start(f32[4,512]{1,0:T(4,128)S(1)} %select_reduce_fusion.1), channel_id=1, source_target_pairs={{0,1},{1,0},{10,11},{11,10},{20,21},{21,20},{30,31},{31,30}} | collective-permute-start | bytes 24584 | tf_op jit(solution)/shard_map/ppermute | solution.py:38
  14.7 22.8 %collective-permute-start.2 = (f32[1024,512]{1,0:T(8,128)}, f32[1024,512]{1,0:T(8,128)S(1)}, u32[]{:S(2)}, u32[]{:S(2)}) collective-permute-start(f32[1024,512]{1,0:T(8,128)} %get-tuple-element.118.refs_0_), channel_id=1, source_target_pairs={{2,3},{3,2},{6,7},{7,6},{8,9},{9,8},{12,13},{13,12},{18,19},{19,18... | collective-permute-start | bytes 6291464 | tf_op jit(solution)/shard_map/ppermute | solution.py:38
  21.4 14.1 %collective-permute-start.1 = (f32[512,512]{1,0:T(8,128)S(1)}, f32[512,512]{1,0:T(8,128)}, u32[]{:S(2)}, u32[]{:S(2)}) collective-permute-start(f32[512,512]{1,0:T(8,128)S(1)} %select_select_fusion.1), channel_id=1, source_target_pairs={{0,4},{1,5},{10,14},{11,15},{20,16},{21,17},{30,26},{31,27}} | collective-permute-start | bytes 3145736 | tf_op jit(solution)/shard_map/ppermute | solution.py:38
  37.4 26.7 %copy-start.36 = (f32[1024,512]{1,0:T(8,128)}, f32[1024,512]{1,0:T(8,128)S(1)}, u32[]{:S(2)}) copy-start(f32[1024,512]{1,0:T(8,128)S(1)} %collective-permute-done.2.refs_2_) | copy-start | bytes 6291460
  37.4 22.0 %collective-permute-start.4 = (f32[1024,512]{1,0:T(8,128)}, f32[1024,512]{1,0:T(8,128)}, u32[]{:S(2)}, u32[]{:S(2)}) collective-permute-start(f32[1024,512]{1,0:T(8,128)} %get-tuple-element.116.refs_0_), channel_id=1, source_target_pairs={{2,3},{3,2},{6,7},{7,6},{8,9},{9,8},{12,13},{13,12},{18,19},{19,18... | collective-permute-start | bytes 6291464 | tf_op jit(solution)/shard_map/ppermute | solution.py:38
  39.5 19.8 %collective-permute-start.3 = (f32[512,512]{1,0:T(8,128)S(1)}, f32[512,512]{1,0:T(8,128)}, u32[]{:S(2)}, u32[]{:S(2)}) collective-permute-start(f32[512,512]{1,0:T(8,128)S(1)} %broadcast_select_fusion.6), channel_id=1, source_target_pairs={{0,2},{1,3},{4,6},{5,7},{10,8},{11,9},{14,12},{15,13},{16,18},{17,... | collective-permute-start | bytes 3145736 | tf_op jit(solution)/shard_map/ppermute | solution.py:38
  59.5 22.2 %collective-permute-start.5 = (f32[512,512]{1,0:T(8,128)S(1)}, f32[512,512]{1,0:T(8,128)S(1)}, u32[]{:S(2)}, u32[]{:S(2)}) collective-permute-start(f32[512,512]{1,0:T(8,128)S(1)} %broadcast_select_fusion.7), channel_id=1, source_target_pairs={{0,1},{1,0},{2,3},{3,2},{4,5},{5,4},{6,7},{7,6},{8,9},{9,8},{10,11... | collective-permute-start | bytes 3145736 | tf_op jit(solution)/shard_map/ppermute | solution.py:38
  64.2 16.1 %collective-permute-start.6 = (f32[256,512]{1,0:T(8,128)S(1)}, f32[256,512]{1,0:T(8,128)S(1)}, u32[]{:S(2)}, u32[]{:S(2)}) collective-permute-start(f32[256,512]{1,0:T(8,128)S(1)} %get-tuple-element.98), channel_id=1, source_target_pairs={{0,4},{1,5},{2,6},{3,7},{4,0},{5,1},{6,2},{7,3},{8,12},{9,13},{10,... | collective-permute-start | bytes 1572872 | tf_op jit(solution)/shard_map/ppermute | solution.py:38
  81.7 36.0 %collective-permute-start.7 = (f32[1024,512]{1,0:T(8,128)}, f32[1024,512]{1,0:T(8,128)S(1)}, u32[]{:S(2)}, u32[]{:S(2)}) collective-permute-start(f32[1024,512]{1,0:T(8,128)} %get-tuple-element.126.refs_0_), channel_id=1, source_target_pairs={{0,1},{1,0},{4,5},{5,4},{10,11},{11,10},{14,15},{15,14},{16,17},{1... | collective-permute-start | bytes 6291464 | tf_op jit(solution)/shard_map/ppermute | solution.py:38
  91.1 26.6 %collective-permute-start.8 = (f32[256,512]{1,0:T(8,128)S(1)}, f32[256,512]{1,0:T(8,128)S(1)}, u32[]{:S(2)}, u32[]{:S(2)}) collective-permute-start(f32[256,512]{1,0:T(8,128)S(1)} %get-tuple-element.102), channel_id=1, source_target_pairs={{0,4},{1,5},{2,6},{3,7},{4,0},{5,1},{6,2},{7,3},{8,12},{9,13},{10,... | collective-permute-start | bytes 1572872 | tf_op jit(solution)/shard_map/ppermute | solution.py:38
  117.7 31.9 %copy-start.9 = (f32[1024,512]{1,0:T(8,128)}, f32[1024,512]{1,0:T(8,128)S(1)}, u32[]{:S(2)}) copy-start(f32[1024,512]{1,0:T(8,128)S(1)} %collective-permute-done.7.refs_1_) | copy-start | bytes 6291460
  117.7 31.4 %collective-permute-start.9 = (f32[1024,512]{1,0:T(8,128)S(1)}, f32[1024,512]{1,0:T(8,128)S(1)}, u32[]{:S(2)}, u32[]{:S(2)}) collective-permute-start(f32[1024,512]{1,0:T(8,128)S(1)} %get-tuple-element.103), channel_id=1, source_target_pairs={{0,16},{1,17},{4,20},{5,21},{10,26},{11,27},{14,30},{15,31},{16,0}... | collective-permute-start | bytes 6291464 | tf_op jit(solution)/shard_map/ppermute | solution.py:38
  125.1 45.1 %collective-permute-start.12 = (f32[1024,512]{1,0:T(8,128)}, f32[1024,512]{1,0:T(8,128)S(1)}, u32[]{:S(2)}, u32[]{:S(2)}) collective-permute-start(f32[1024,512]{1,0:T(8,128)} %get-tuple-element.132.refs_0_), channel_id=1, source_target_pairs={{0,1},{1,0},{4,5},{5,4},{10,11},{11,10},{14,15},{15,14},{16,17},{1... | collective-permute-start | bytes 6291464 | tf_op jit(solution)/shard_map/ppermute | solution.py:38
  128.3 43.3 %collective-permute-start.13 = (f32[1024,512]{1,0:T(8,128)}, f32[1024,512]{1,0:T(8,128)S(1)}, u32[]{:S(2)}, u32[]{:S(2)}) collective-permute-start(f32[1024,512]{1,0:T(8,128)} %get-tuple-element.126.refs_0_), channel_id=1, source_target_pairs={{2,3},{3,2},{6,7},{7,6},{8,9},{9,8},{12,13},{13,12},{18,19},{19,18... | collective-permute-start | bytes 6291464 | tf_op jit(solution)/shard_map/ppermute | solution.py:38
  129.1 31.0 %collective-permute-start.10 = (f32[256,512]{1,0:T(8,128)}, f32[256,512]{1,0:T(8,128)S(1)}, u32[]{:S(2)}, u32[]{:S(2)}) collective-permute-start(f32[256,512]{1,0:T(8,128)} %get-tuple-element.104), channel_id=1, source_target_pairs={{0,4},{1,5},{2,6},{3,7},{4,0},{5,1},{6,2},{7,3},{8,12},{9,13},{10,... | collective-permute-start | bytes 1572872 | tf_op jit(solution)/shard_map/ppermute | solution.py:38
  130.9 39.3 %collective-permute-start.11 = (f32[256,512]{1,0:T(8,128)}, f32[256,512]{1,0:T(8,128)S(1)}, u32[]{:S(2)}, u32[]{:S(2)}) collective-permute-start(f32[256,512]{1,0:T(8,128)} %get-tuple-element.105), channel_id=1, source_target_pairs={{0,4},{1,5},{2,6},{3,7},{4,0},{5,1},{6,2},{7,3},{8,12},{9,13},{10,... | collective-permute-start | bytes 1572872 | tf_op jit(solution)/shard_map/ppermute | solution.py:38
  149.6 32.9 %copy-start = (bf16[1024,1024]{1,0:T(8,128)(2,1)S(1)}, bf16[1024,1024]{1,0:T(8,128)(2,1)}, u32[]{:S(2)}) copy-start(bf16[1024,1024]{1,0:T(8,128)(2,1)} %get-tuple-element.109.refs_5_.refs_8_) | copy-start | bytes 6291460
  173.0 14.1 %collective-permute-start.14 = (f32[2,1024,512]{2,1,0:T(8,128)}, f32[2,1024,512]{2,1,0:T(8,128)}, u32[]{:S(2)}, u32[]{:S(2)}) collective-permute-start(f32[2,1024,512]{2,1,0:T(8,128)} %pad_maximum_fusion), channel_id=1, source_target_pairs={{0,8},{1,9},{4,12},{5,13},{10,2},{11,3},{14,6},{15,7},{16,24},{17,... | collective-permute-start | bytes 12582920 | tf_op jit(solution)/shard_map/ppermute | solution.py:38
  176.4 32.4 %collective-permute-start.15 = (f32[1024,512]{1,0:T(8,128)}, f32[1024,512]{1,0:T(8,128)}, u32[]{:S(2)}, u32[]{:S(2)}) collective-permute-start(f32[1024,512]{1,0:T(8,128)} %get-tuple-element.118.refs_0_), channel_id=1, source_target_pairs={{0,1},{1,0},{4,5},{5,4},{10,11},{11,10},{14,15},{15,14},{16,17},{1... | collective-permute-start | bytes 6291464 | tf_op jit(solution)/shard_map/ppermute | solution.py:38
  180.4 46.8 %collective-permute-start.16 = (f32[1024,512]{1,0:T(8,128)}, f32[1024,512]{1,0:T(8,128)}, u32[]{:S(2)}, u32[]{:S(2)}) collective-permute-start(f32[1024,512]{1,0:T(8,128)} %get-tuple-element.116.refs_0_), channel_id=1, source_target_pairs={{0,1},{1,0},{4,5},{5,4},{10,11},{11,10},{14,15},{15,14},{16,17},{1... | collective-permute-start | bytes 6291464 | tf_op jit(solution)/shard_map/ppermute | solution.py:38
  184.1 61.1 %collective-permute-start.17 = (f32[256,512]{1,0:T(8,128)S(1)}, f32[256,512]{1,0:T(8,128)S(1)}, u32[]{:S(2)}, u32[]{:S(2)}) collective-permute-start(f32[256,512]{1,0:T(8,128)S(1)} %copy-done.69), channel_id=1, source_target_pairs={{0,4},{1,5},{2,6},{3,7},{4,0},{5,1},{6,2},{7,3},{8,12},{9,13},{10,... | collective-permute-start | bytes 1572872 | tf_op jit(solution)/shard_map/ppermute | solution.py:38
  184.2 61.0 %collective-permute-start.18 = (f32[256,512]{1,0:T(8,128)S(1)}, f32[256,512]{1,0:T(8,128)S(1)}, u32[]{:S(2)}, u32[]{:S(2)}) collective-permute-start(f32[256,512]{1,0:T(8,128)S(1)} %copy-done.68), channel_id=1, source_target_pairs={{0,4},{1,5},{2,6},{3,7},{4,0},{5,1},{6,2},{7,3},{8,12},{9,13},{10,... | collective-permute-start | bytes 1572872 | tf_op jit(solution)/shard_map/ppermute | solution.py:38
  192.3 68.3 %copy-start.3 = (f32[512,512]{1,0:T(8,128)}, f32[512,512]{1,0:T(8,128)S(1)}, u32[]{:S(2)}) copy-start(f32[512,512]{1,0:T(8,128)S(1)} %get-tuple-element.208.refs_2_.refs_3_) | copy-start | bytes 3145732
  246.3 4.8 collective-permute-start.19
  247.5 3.5 collective-permute-start.20
  249.1 65.1 %collective-permute-start.27 = (f32[1024,512]{1,0:T(8,128)}, f32[1024,512]{1,0:T(8,128)}, u32[]{:S(2)}, u32[]{:S(2)}) collective-permute-start(f32[1024,512]{1,0:T(8,128)} %get-tuple-element.132.refs_0_), channel_id=1, source_target_pairs={{2,3},{3,2},{6,7},{7,6},{8,9},{9,8},{12,13},{13,12},{18,19},{19,18... | collective-permute-start | bytes 6291464 | tf_op jit(solution)/shard_map/ppermute | solution.py:38
  252.7 24.8 %collective-permute-start.21 = (f32[512,512]{1,0:T(8,128)}, f32[512,512]{1,0:T(8,128)}, u32[]{:S(2)}, u32[]{:S(2)}) collective-permute-start(f32[512,512]{1,0:T(8,128)} %broadcast_multiply_fusion.1), channel_id=1, source_target_pairs={{0,1},{4,5},{10,11},{14,15},{17,16},{21,20},{27,26},{31,30}} | collective-permute-start | bytes 3145736 | tf_op jit(solution)/shard_map/ppermute | solution.py:38
  257.7 21.8 %collective-permute-start.22 = (f32[512,512]{1,0:T(8,128)}, f32[512,512]{1,0:T(8,128)}, u32[]{:S(2)}, u32[]{:S(2)}) collective-permute-start(f32[512,512]{1,0:T(8,128)} %broadcast_multiply_fusion.1), channel_id=1, source_target_pairs={{1,17},{5,21},{11,27},{15,31},{16,0},{20,4},{26,10},{30,14}} | collective-permute-start | bytes 3145736 | tf_op jit(solution)/shard_map/ppermute | solution.py:38
  259.0 33.2 %collective-permute-start.23 = (f32[512,512]{1,0:T(8,128)}, f32[512,512]{1,0:T(8,128)}, u32[]{:S(2)}, u32[]{:S(2)}) collective-permute-start(f32[512,512]{1,0:T(8,128)} %broadcast_multiply_fusion.1), channel_id=1, source_target_pairs={{1,16},{5,20},{11,26},{15,30},{16,1},{20,5},{26,11},{30,15}} | collective-permute-start | bytes 3145736 | tf_op jit(solution)/shard_map/ppermute | solution.py:38
  272.5 41.7 %collective-permute-start.24 = (f32[512,512]{1,0:T(8,128)}, f32[512,512]{1,0:T(8,128)}, u32[]{:S(2)}, u32[]{:S(2)}) collective-permute-start(f32[512,512]{1,0:T(8,128)} %get-tuple-element.120), channel_id=1, source_target_pairs={{0,16},{1,17},{2,18},{3,19},{4,20},{5,21},{6,22},{7,23},{8,24},{9,... | collective-permute-start | bytes 3145736 | tf_op jit(solution)/shard_map/ppermute | solution.py:38
  277.5 21.6 %collective-permute-start.25 = (f32[256,512]{1,0:T(8,128)}, f32[256,512]{1,0:T(8,128)}, u32[]{:S(2)}, u32[]{:S(2)}) collective-permute-start(f32[256,512]{1,0:T(8,128)} %get-tuple-element.121), channel_id=1, source_target_pairs={{0,4},{1,5},{2,6},{3,7},{4,0},{5,1},{6,2},{7,3},{8,12},{9,13},{10,... | collective-permute-start | bytes 1572872 | tf_op jit(solution)/shard_map/ppermute | solution.py:38
  279.5 34.7 %collective-permute-start.26 = (f32[256,512]{1,0:T(8,128)}, f32[256,512]{1,0:T(8,128)}, u32[]{:S(2)}, u32[]{:S(2)}) collective-permute-start(f32[256,512]{1,0:T(8,128)} %get-tuple-element.122), channel_id=1, source_target_pairs={{0,4},{1,5},{2,6},{3,7},{4,0},{5,1},{6,2},{7,3},{8,12},{9,13},{10,... | collective-permute-start | bytes 1572872 | tf_op jit(solution)/shard_map/ppermute | solution.py:38
  292.1 24.2 %copy-start.23 = (f32[256,512]{1,0:T(8,128)S(1)}, f32[256,512]{1,0:T(8,128)}, u32[]{:S(2)}) copy-start(f32[256,512]{1,0:T(8,128)} %copy-done.22) | copy-start | bytes 1572868
  292.1 24.2 %copy-start.25 = (f32[256,512]{1,0:T(8,128)S(1)}, f32[256,512]{1,0:T(8,128)}, u32[]{:S(2)}) copy-start(f32[256,512]{1,0:T(8,128)} %copy-done.24) | copy-start | bytes 1572868
  292.2 28.5 %copy-start.39 = (f32[1024,512]{1,0:T(8,128)S(1)}, f32[1024,512]{1,0:T(8,128)}, u32[]{:S(2)}) copy-start(f32[1024,512]{1,0:T(8,128)} %copy-done.38) | copy-start | bytes 6291460
  294.3 23.0 %copy-start.27 = (f32[256,512]{1,0:T(8,128)S(1)}, f32[256,512]{1,0:T(8,128)}, u32[]{:S(2)}) copy-start(f32[256,512]{1,0:T(8,128)} %copy-done.26) | copy-start | bytes 1572868
  294.4 23.0 %copy-start.32 = (f32[256,512]{1,0:T(8,128)S(1)}, f32[256,512]{1,0:T(8,128)}, u32[]{:S(2)}) copy-start(f32[256,512]{1,0:T(8,128)} %copy-done.31) | copy-start | bytes 1572868
  314.2 25.7 %collective-permute-start.29 = (f32[512,512]{1,0:T(8,128)S(1)}, f32[512,512]{1,0:T(8,128)S(1)}, u32[]{:S(2)}, u32[]{:S(2)}) collective-permute-start(f32[512,512]{1,0:T(8,128)S(1)} %select_select_fusion), channel_id=1, source_target_pairs={{0,4},{1,5},{4,0},{5,1},{10,14},{11,15},{14,10},{15,11},{16,20},{1... | collective-permute-start | bytes 3145736 | tf_op jit(solution)/shard_map/ppermute | solution.py:38
  318.4 51.8 %collective-permute-start.33 = (f32[512,512]{1,0:T(8,128)}, f32[512,512]{1,0:T(8,128)S(1)}, u32[]{:S(2)}, u32[]{:S(2)}) collective-permute-start(f32[512,512]{1,0:T(8,128)} %pad_maximum_fusion.5), channel_id=1, source_target_pairs={{0,1},{1,0},{2,3},{3,2},{4,5},{5,4},{6,7},{7,6},{8,9},{9,8},{10,11... | collective-permute-start | bytes 3145736 | tf_op jit(solution)/shard_map/ppermute | solution.py:38
  318.4 51.8 %collective-permute-start.32 = (f32[512,512]{1,0:T(8,128)}, f32[512,512]{1,0:T(8,128)S(1)}, u32[]{:S(2)}, u32[]{:S(2)}) collective-permute-start(f32[512,512]{1,0:T(8,128)} %pad_maximum_fusion.4), channel_id=1, source_target_pairs={{0,1},{1,0},{2,3},{3,2},{4,5},{5,4},{6,7},{7,6},{8,9},{9,8},{10,11... | collective-permute-start | bytes 3145736 | tf_op jit(solution)/shard_map/ppermute | solution.py:38
  320.4 49.8 %collective-permute-start.30 = (f32[512,512]{1,0:T(8,128)S(1)}, f32[512,512]{1,0:T(8,128)S(1)}, u32[]{:S(2)}, u32[]{:S(2)}) collective-permute-start(f32[512,512]{1,0:T(8,128)S(1)} %get-tuple-element.131), channel_id=1, source_target_pairs={{0,16},{1,17},{2,18},{3,19},{4,20},{5,21},{6,22},{7,23},{8,24},{9,... | collective-permute-start | bytes 3145736 | tf_op jit(solution)/shard_map/ppermute | solution.py:38
  330.8 39.5 %collective-permute-start.28 = (f32[512,512]{1,0:T(8,128)S(1)}, f32[512,512]{1,0:T(8,128)S(1)}, u32[]{:S(2)}, u32[]{:S(2)}) collective-permute-start(f32[512,512]{1,0:T(8,128)S(1)} %get-tuple-element.129), channel_id=1, source_target_pairs={{0,16},{1,17},{2,18},{3,19},{4,20},{5,21},{6,22},{7,23},{8,24},{9,... | collective-permute-start | bytes 3145736 | tf_op jit(solution)/shard_map/ppermute | solution.py:38
  340.0 30.2 %collective-permute-start.31 = (f32[256,512]{1,0:T(8,128)S(1)}, f32[256,512]{1,0:T(8,128)S(1)}, u32[]{:S(2)}, u32[]{:S(2)}) collective-permute-start(f32[256,512]{1,0:T(8,128)S(1)} %get-tuple-element.135), channel_id=1, source_target_pairs={{0,4},{1,5},{2,6},{3,7},{4,0},{5,1},{6,2},{7,3},{8,12},{9,13},{10,... | collective-permute-start | bytes 1572872 | tf_op jit(solution)/shard_map/ppermute | solution.py:38
  351.0 20.7 %copy-start.34 = (f32[256,512]{1,0:T(8,128)S(1)}, f32[256,512]{1,0:T(8,128)}, u32[]{:S(2)}) copy-start(f32[256,512]{1,0:T(8,128)} %copy-done.33) | copy-start | bytes 1572868
  351.2 23.6 %copy-start.67 = (f32[1,1024,512]{2,1,0:T(8,128)S(1)}, f32[1,1024,512]{2,1,0:T(8,128)}, u32[]{:S(2)}) copy-start(f32[1,1024,512]{2,1,0:T(8,128)} %get-tuple-element.195) | copy-start | bytes 6291460
  370.2 24.8 %collective-permute-start.34 = (f32[2,512,512]{2,1,0:T(8,128)S(1)}, f32[2,512,512]{2,1,0:T(8,128)S(1)}, u32[]{:S(2)}, u32[]{:S(2)}) collective-permute-start(f32[2,512,512]{2,1,0:T(8,128)S(1)} %pad_maximum_fusion.2), channel_id=1, source_target_pairs={{0,2},{1,3},{4,6},{5,7},{10,8},{11,9},{14,12},{15,13},{16,18},{17,... | collective-permute-start | bytes 6291464 | tf_op jit(solution)/shard_map/ppermute | solution.py:38
  372.7 22.8 %collective-permute-start.36 = (f32[512,512]{1,0:T(8,128)}, f32[512,512]{1,0:T(8,128)S(1)}, u32[]{:S(2)}, u32[]{:S(2)}) collective-permute-start(f32[512,512]{1,0:T(8,128)} %pad_maximum_fusion.6), channel_id=1, source_target_pairs={{0,1},{1,0},{2,3},{3,2},{4,5},{5,4},{6,7},{7,6},{8,9},{9,8},{10,11... | collective-permute-start | bytes 3145736 | tf_op jit(solution)/shard_map/ppermute | solution.py:38
  372.7 22.8 %collective-permute-start.35 = (f32[512,512]{1,0:T(8,128)S(1)}, f32[512,512]{1,0:T(8,128)S(1)}, u32[]{:S(2)}, u32[]{:S(2)}) collective-permute-start(f32[512,512]{1,0:T(8,128)S(1)} %get-tuple-element.146), channel_id=1, source_target_pairs={{0,16},{1,17},{2,18},{3,19},{4,20},{5,21},{6,22},{7,23},{8,24},{9,... | collective-permute-start | bytes 3145736 | tf_op jit(solution)/shard_map/ppermute | solution.py:38
  380.0 38.3 %collective-permute-start.38 = (f32[512,512]{1,0:T(8,128)}, f32[512,512]{1,0:T(8,128)S(1)}, u32[]{:S(2)}, u32[]{:S(2)}) collective-permute-start(f32[512,512]{1,0:T(8,128)} %pad_maximum_fusion.7), channel_id=1, source_target_pairs={{0,4},{1,5},{2,6},{3,7},{4,0},{5,1},{6,2},{7,3},{8,12},{9,13},{10,... | collective-permute-start | bytes 3145736 | tf_op jit(solution)/shard_map/ppermute | solution.py:38
  395.6 23.7 %collective-permute-start.39 = (f32[512,512]{1,0:T(8,128)S(1)}, f32[512,512]{1,0:T(8,128)S(1)}, u32[]{:S(2)}, u32[]{:S(2)}) collective-permute-start(f32[512,512]{1,0:T(8,128)S(1)} %pad_maximum_fusion.8), channel_id=1, source_target_pairs={{0,1},{1,0},{2,3},{3,2},{4,5},{5,4},{6,7},{7,6},{8,9},{9,8},{10,11... | collective-permute-start | bytes 3145736 | tf_op jit(solution)/shard_map/ppermute | solution.py:38
  395.7 24.6 %collective-permute-start.37 = (f32[512,512]{1,0:T(8,128)S(1)}, f32[512,512]{1,0:T(8,128)S(1)}, u32[]{:S(2)}, u32[]{:S(2)}) collective-permute-start(f32[512,512]{1,0:T(8,128)S(1)} %get-tuple-element.149), channel_id=1, source_target_pairs={{0,16},{1,17},{2,18},{3,19},{4,20},{5,21},{6,22},{7,23},{8,24},{9,... | collective-permute-start | bytes 3145736 | tf_op jit(solution)/shard_map/ppermute | solution.py:38
  421.3 33.1 %collective-permute-start.40 = (f32[1024,512]{1,0:T(8,128)}, f32[1024,512]{1,0:T(8,128)}, u32[]{:S(2)}, u32[]{:S(2)}) collective-permute-start(f32[1024,512]{1,0:T(8,128)} %get-tuple-element.153), channel_id=1, source_target_pairs={{0,16},{4,20},{10,26},{14,30},{17,1},{21,5},{27,11},{31,15}} | collective-permute-start | bytes 6291464 | tf_op jit(solution)/shard_map/ppermute | solution.py:38
  424.6 36.7 %collective-permute-start.41 = (f32[256,512]{1,0:T(8,128)}, f32[256,512]{1,0:T(8,128)}, u32[]{:S(2)}, u32[]{:S(2)}) collective-permute-start(f32[256,512]{1,0:T(8,128)} %get-tuple-element.159), channel_id=1, source_target_pairs={{0,4},{1,5},{2,6},{3,7},{4,0},{5,1},{6,2},{7,3},{8,12},{9,13},{10,... | collective-permute-start | bytes 1572872 | tf_op jit(solution)/shard_map/ppermute | solution.py:38
  461.2 7.5 %collective-permute-start.42 = (f32[1024,512]{1,0:T(8,128)}, f32[1024,512]{1,0:T(8,128)}, u32[]{:S(2)}, u32[]{:S(2)}) collective-permute-start(f32[1024,512]{1,0:T(8,128)} %broadcast_select_fusion.1), channel_id=1, source_target_pairs={{0,8},{1,9},{4,12},{5,13},{10,2},{11,3},{14,6},{15,7},{16,24},{17,... | collective-permute-start | bytes 6291464 | tf_op jit(solution)/shard_map/ppermute | solution.py:38
  464.8 35.8 %collective-permute-start.45 = (f32[512,512]{1,0:T(8,128)S(1)}, f32[512,512]{1,0:T(8,128)S(1)}, u32[]{:S(2)}, u32[]{:S(2)}) collective-permute-start(f32[512,512]{1,0:T(8,128)S(1)} %copy-done.63), channel_id=1, source_target_pairs={{0,16},{1,17},{2,18},{3,19},{4,20},{5,21},{6,22},{7,23},{8,24},{9,... | collective-permute-start | bytes 3145736 | tf_op jit(solution)/shard_map/ppermute | solution.py:38
  464.9 24.1 %collective-permute-start.43 = (f32[256,512]{1,0:T(8,128)S(1)}, f32[256,512]{1,0:T(8,128)S(1)}, u32[]{:S(2)}, u32[]{:S(2)}) collective-permute-start(f32[256,512]{1,0:T(8,128)S(1)} %get-tuple-element.161), channel_id=1, source_target_pairs={{0,4},{1,5},{2,6},{3,7},{4,0},{5,1},{6,2},{7,3},{8,12},{9,13},{10,... | collective-permute-start | bytes 1572872 | tf_op jit(solution)/shard_map/ppermute | solution.py:38
  497.6 26.1 %collective-permute-start.44 = (f32[512,512]{1,0:T(8,128)S(1)}, f32[512,512]{1,0:T(8,128)S(1)}, u32[]{:S(2)}, u32[]{:S(2)}) collective-permute-start(f32[512,512]{1,0:T(8,128)S(1)} %get-tuple-element.167), channel_id=1, source_target_pairs={{0,16},{1,17},{2,18},{3,19},{4,20},{5,21},{6,22},{7,23},{8,24},{9,... | collective-permute-start | bytes 3145736 | tf_op jit(solution)/shard_map/ppermute | solution.py:38
  500.6 69.4 %collective-permute-start.48 = (f32[768,512]{1,0:T(8,128)}, f32[768,512]{1,0:T(8,128)S(1)}, u32[]{:S(2)}, u32[]{:S(2)}) collective-permute-start(f32[768,512]{1,0:T(8,128)} %pad_maximum_fusion.3), channel_id=1, source_target_pairs={{0,4},{1,5},{2,6},{3,7},{4,0},{5,1},{6,2},{7,3},{8,12},{9,13},{10,... | collective-permute-start | bytes 4718600 | tf_op jit(solution)/shard_map/ppermute | solution.py:38
  500.6 23.1 %copy-start.21 = (f32[512,512]{1,0:T(8,128)S(1)}, f32[512,512]{1,0:T(8,128)}, u32[]{:S(2)}) copy-start(f32[512,512]{1,0:T(8,128)} %copy-done.19) | copy-start | bytes 3145732
  500.7 23.1 %copy-start.49 = (f32[512,512]{1,0:T(8,128)S(1)}, f32[512,512]{1,0:T(8,128)}, u32[]{:S(2)}) copy-start(f32[512,512]{1,0:T(8,128)} %copy-done.48) | copy-start | bytes 3145732
  500.7 23.1 %copy-start.61 = (f32[256,512]{1,0:T(8,128)S(1)}, f32[256,512]{1,0:T(8,128)}, u32[]{:S(2)}) copy-start(f32[256,512]{1,0:T(8,128)} %copy-done.60) | copy-start | bytes 1572868
  509.0 37.2 %collective-permute-start.46 = (f32[512,512]{1,0:T(8,128)S(1)}, f32[512,512]{1,0:T(8,128)S(1)}, u32[]{:S(2)}, u32[]{:S(2)}) collective-permute-start(f32[512,512]{1,0:T(8,128)S(1)} %get-tuple-element.173), channel_id=1, source_target_pairs={{0,16},{1,17},{2,18},{3,19},{4,20},{5,21},{6,22},{7,23},{8,24},{9,... | collective-permute-start | bytes 3145736 | tf_op jit(solution)/shard_map/ppermute | solution.py:38
  533.4 33.9 %collective-permute-start.47 = (f32[512,512]{1,0:T(8,128)S(1)}, f32[512,512]{1,0:T(8,128)S(1)}, u32[]{:S(2)}, u32[]{:S(2)}) collective-permute-start(f32[512,512]{1,0:T(8,128)S(1)} %get-tuple-element.177), channel_id=1, source_target_pairs={{0,16},{1,17},{2,18},{3,19},{4,20},{5,21},{6,22},{7,23},{8,24},{9,... | collective-permute-start | bytes 3145736 | tf_op jit(solution)/shard_map/ppermute | solution.py:38
  578.6 25.1 %collective-permute-start.49 = (f32[512,512]{1,0:T(8,128)S(1)}, f32[512,512]{1,0:T(8,128)S(1)}, u32[]{:S(2)}, u32[]{:S(2)}) collective-permute-start(f32[512,512]{1,0:T(8,128)S(1)} %get-tuple-element.182), channel_id=1, source_target_pairs={{0,16},{1,17},{2,18},{3,19},{4,20},{5,21},{6,22},{7,23},{8,24},{9,... | collective-permute-start | bytes 3145736 | tf_op jit(solution)/shard_map/ppermute | solution.py:38
  (56 other events, 332.3 us)
